TPU v7x, 32 devices: a whole 2x2x4 slice. The times are simulated.
32 devices in a mesh: replica: 4 (over y, x), fsdp: 8 (over z, core).
Axes of the slice: x: 2, y: 2, z: 4, core: 2. Of those that a mesh axis runs over, the one named last changes fastest.
Arguments:
- tokens: bfloat16 [4, 3072, 4096], P('replica', 'fsdp'), may hold values from -16 to 16
- positions: int32 [4, 3072], P('replica', 'fsdp'), may hold values from 0 to 383, as said below
- partner: int32 [4], replicated, may hold values from 0 to 3, as said below
- weights: bfloat16 [4, 4096, 3072], P('replica', 'fsdp'), may hold values from -6 to 6
- anchor: float32 [4, 4096, 3072], P('replica', 'fsdp'), may hold values from -6 to 6
- momentum: float32 [4, 4096, 3072], P('replica', 'fsdp'), may hold values from -6 to 6
Outputs:
- context: bfloat16 [4, 3072, 2048], P('replica', 'fsdp')
- new_params: float32 [4, 4096, 3072], P('replica', 'fsdp')
- new_momentum: float32 [4, 4096, 3072], P('replica', 'fsdp')
Inputs may be any that keep to these rules, and one draw needn't show every extreme that they name: partner pairs the replicas: partner[partner[r]] = r and partner[r] != r. positions count up by one from 0 within each document; every document lies within one aligned block of 384 tokens, and in each replica the first block is one document.
All inputs are finite; a program needn't handle non-finite values.
Results may differ from a plain program's by a relative error of at most 0.011.
Values may be sent and summed in bfloat16 or wider, within the bound.
No kernel may reach another device: no remote copies, remote signals or barrier semaphores. Data moves between devices by JAX's collectives and lax.ppermute only.
A program may use at most 128 MiB of HBM per device.

v0:
```python
import jax
import jax.numpy as jnp
from jax import lax
from jax.sharding import PartitionSpec as P

D = 4096
HEADS = 16
KV_HEADS = 4
HEAD_DIM = 128


ROPE_BASE = 500000.0
MOMENTUM_RATE = 0.9
OUTER_RATE = 0.7


def rotate(heads, places):
    half = heads.shape[-1] // 2
    frequency = ROPE_BASE ** (-(jnp.arange(half, dtype=jnp.float32) * 2.0) / heads.shape[-1])
    angles = places.astype(jnp.float32)[:, None] * frequency[None, :]
    cosine = jnp.cos(angles)[:, None, :]
    sine = jnp.sin(angles)[:, None, :]
    first = heads[..., :half]
    second = heads[..., half:]
    return jnp.concatenate([first * cosine - second * sine, second * cosine + first * sine], -1)


def attend(projected, places):
    count = projected.shape[0]
    width_q = HEADS * HEAD_DIM
    width_kv = KV_HEADS * HEAD_DIM
    group = HEADS // KV_HEADS
    scaled = projected * D ** (-0.5)
    query = rotate(scaled[:, :width_q].reshape(count, HEADS, HEAD_DIM), places).astype(jnp.bfloat16)
    keys = rotate(
        scaled[:, width_q : width_q + width_kv].reshape(count, KV_HEADS, HEAD_DIM), places
    ).astype(jnp.bfloat16)
    values = scaled[:, width_q + width_kv :].reshape(count, KV_HEADS, HEAD_DIM).astype(jnp.bfloat16)
    query = query.reshape(count, KV_HEADS, group, HEAD_DIM)
    ordinal = jnp.arange(count, dtype=jnp.int32)
    distance = ordinal[:, None] - ordinal[None, :]
    visible = (distance >= 0) & (distance <= places[:, None])
    scores = jnp.einsum(
        "tkge,ske->kgts", query, keys, preferred_element_type=jnp.float32
    ) * HEAD_DIM ** (-0.5)
    scores = jnp.where(visible[None, None], scores, -1e30)
    highest = jnp.max(scores, -1, keepdims=True)
    exponent = jnp.exp(scores - highest)
    probabilities = (exponent / jnp.sum(exponent, -1, keepdims=True)).astype(jnp.bfloat16)
    context = jnp.einsum(
        "kgts,ske->tkge", probabilities, values, preferred_element_type=jnp.float32
    )
    return context.reshape(count, width_q).astype(jnp.bfloat16)


def outer_step(partner, weights, anchor, momentum):
    pseudo = anchor[0] - weights[0].astype(jnp.float32)
    count = lax.axis_size("replica")
    shard_rows, columns = pseudo.shape
    own_grad = lax.all_to_all(
        pseudo.reshape(shard_rows, count, columns // count),
        "replica",
        split_axis=1,
        concat_axis=1,
        tiled=True,
    )
    own_mom = lax.all_to_all(
        momentum[0].reshape(shard_rows, count, columns // count),
        "replica",
        split_axis=1,
        concat_axis=1,
        tiled=True,
    )
    grad_pair = 0.5 * (own_grad + jnp.take(own_grad, partner, axis=1))
    mom_pair = 0.5 * (own_mom + jnp.take(own_mom, partner, axis=1))
    grad_mean = lax.all_to_all(grad_pair, "replica", split_axis=1, concat_axis=1, tiled=True)
    mom_mean = lax.all_to_all(mom_pair, "replica", split_axis=1, concat_axis=1, tiled=True)
    grad_mean = grad_mean.reshape(shard_rows, columns)
    mom_mean = mom_mean.reshape(shard_rows, columns)
    new_momentum = MOMENTUM_RATE * mom_mean + grad_mean
    new_params = anchor[0] - OUTER_RATE * (grad_mean + MOMENTUM_RATE * new_momentum)
    return (new_params[None], new_momentum[None])


def attention_step(tokens, positions, weights):
    rows = tokens[0]
    places = positions[0]
    projected = jnp.dot(
        rows,
        lax.all_gather(weights, "fsdp", axis=1, tiled=True)[0],
        preferred_element_type=jnp.float32,
    )
    return attend(projected, places)[None]


def body(tokens, positions, partner, weights, anchor, momentum):
    context = attention_step(tokens, positions, weights)
    new_params, new_momentum = outer_step(partner, weights, anchor, momentum)
    return (context, new_params, new_momentum)


def solution(mesh):
    placed = (
        P("replica", "fsdp", None),
        P("replica", "fsdp"),
        P(),
        P("replica", "fsdp", None),
        P("replica", "fsdp", None),
        P("replica", "fsdp", None),
    )
    return jax.shard_map(
        body,
        mesh=mesh,
        in_specs=placed,
        out_specs=(
            P("replica", "fsdp", None),
            P("replica", "fsdp", None),
            P("replica", "fsdp", None),
        ),
        check_vma=False,
    )
```

profile of v0, /device:TPU:0, one launch (start us, length us, event | category | flops | bytes accessed | tf_op | source)
XLA Modules:
  0.0 433.8 jit_solution(6660484141151303497)
XLA Ops:
  7.9 4.9 %copy.29 = bf16[1,512,3072]{1,2,0:T(8,128)(2,1)} copy(bf16[1,512,3072]{2,1,0:T(8,128)(2,1)} %param.11) | data formatting | bytes 6291456 | tf_op args[3]
  12.9 6.6 %copy.36 = f32[1,512,3072]{1,2,0:T(8,128)} copy(f32[1,512,3072]{2,1,0:T(8,128)} %param.12) | data formatting | bytes 12582912 | tf_op args[4]
  19.4 9.2 %convert_subtract_fusion = f32[1,512,3072]{1,2,0:T(8,128)} fusion(f32[1,512,3072]{1,2,0:T(8,128)} %copy.36, bf16[1,512,3072]{1,2,0:T(8,128)(2,1)} %copy.29), kind=kLoop, calls=%fused_computation.17 | loop fusion | flops 3145728 | bytes 15728640 | tf_op jit(solution)/shard_map/sub | solution.py:57
  28.6 6.7 %copy.31 = f32[512,4,768]{2,0,1:T(8,128)} copy(f32[512,4,768]{0,2,1:T(8,128)} %bitcast.61) | data formatting | bytes 12582912 | tf_op jit(solution)/shard_map/sub | solution.py:57
  35.3 5.3 %all-to-all-start = ((f32[512,4,768]{2,0,1:T(8,128)}), f32[512,4,768]{2,0,1:T(8,128)}, u32[]{:S(2)}, u32[]{:S(2)}) async-start(f32[512,4,768]{2,0,1:T(8,128)} %copy.31), calls=%async_computation | async-start | bytes 12582912 | tf_op jit(solution)/shard_map/all_to_all | solution.py:60
  40.6 6.6 %copy.33 = f32[1,512,3072]{1,2,0:T(8,128)} copy(f32[1,512,3072]{2,1,0:T(8,128)} %param.13) | data formatting | bytes 12582912 | tf_op args[5]
  47.2 6.6 %copy.34 = f32[512,4,768]{2,0,1:T(8,128)} copy(f32[512,4,768]{0,2,1:T(8,128)} %bitcast.60) | data formatting | bytes 12582912 | tf_op jit(solution)/shard_map/reshape;squeeze | solution.py:68
  53.8 57.8 %all-to-all-done = f32[512,4,768]{2,0,1:T(8,128)} async-done(((f32[512,4,768]{2,0,1:T(8,128)}), f32[512,4,768]{2,0,1:T(8,128)}, u32[]{:S(2)}, u32[]{:S(2)}) %all-to-all-start) | async-done | bytes 6291488 | tf_op jit(solution)/shard_map/all_to_all | solution.py:60
  111.7 5.3 %all-to-all-start.2 = ((f32[512,4,768]{2,0,1:T(8,128)}), f32[512,4,768]{2,0,1:T(8,128)}, u32[]{:S(2)}, u32[]{:S(2)}) async-start(f32[512,4,768]{2,0,1:T(8,128)} %copy.34), calls=%async_computation.2 | async-start | bytes 12582912 | tf_op jit(solution)/shard_map/all_to_all | solution.py:67
  117.0 6.3 %gather_fusion = f32[4,512,768]{2,1,0:T(8,128)} fusion(f32[512,4,768]{2,0,1:T(8,128)} %all-to-all-done, s32[1024]{0:T(1024)S(1)} %pad_clamp_fusion), kind=kCustom, calls=%fused_computation.clone | custom fusion | bytes 12582928 | tf_op jit(solution)/shard_map/jit(_take)/gather | solution.py:74
  123.3 63.4 %all-to-all-done.2 = f32[512,4,768]{2,0,1:T(8,128)} async-done(((f32[512,4,768]{2,0,1:T(8,128)}), f32[512,4,768]{2,0,1:T(8,128)}, u32[]{:S(2)}, u32[]{:S(2)}) %all-to-all-start.2) | async-done | bytes 6291488 | tf_op jit(solution)/shard_map/all_to_all | solution.py:67
  186.7 6.5 %gather_fusion.1 = f32[4,512,768]{2,1,0:T(8,128)} fusion(f32[512,4,768]{2,0,1:T(8,128)} %all-to-all-done.2, s32[1024]{0:T(1024)S(1)} %pad_clamp_fusion), kind=kCustom, calls=%fused_computation.1.clone | custom fusion | bytes 12582928 | tf_op jit(solution)/shard_map/jit(_take)/gather | solution.py:75
  193.2 12.0 %fusion.4 = (f32[512,4,768]{2,0,1:T(8,128)S(1)}, f32[512,4,768]{2,0,1:T(8,128)}) fusion(f32[512,4,768]{2,0,1:T(8,128)} %all-to-all-done.2, f32[4,512,768]{2,1,0:T(8,128)} %gather_fusion.1, pred[4]{0:T(512)(128)(4,1)S(1)} %compare_and_fusion, f32[512,4,768]{2,0,1:T(8,128)} %all-to-all-done, f32[4,512,768]{2,1,0:T(8,128)} %gather_fusion), kind=kLoop, calls=%fused_computation.11 | loop fusion | flops 9437184 | bytes 37748740 | tf_op jit(solution)/shard_map/mul | solution.py:75
  205.3 73.4 %all_to_all.20 = f32[512,4,768]{2,0,1:T(8,128)} all-to-all(f32[512,4,768]{2,0,1:T(8,128)S(1)} %get-tuple-element.23), channel_id=1, replica_groups=mesh['replica'=4,'fsdp'=8] {'replica'}, dimensions={1} | all-to-all | bytes 12582912 | tf_op jit(solution)/shard_map/all_to_all | solution.py:77
  278.7 5.6 %all-to-all-start.1 = ((f32[512,4,768]{2,0,1:T(8,128)}), f32[512,4,768]{2,0,1:T(8,128)}, u32[]{:S(2)}, u32[]{:S(2)}) async-start(f32[512,4,768]{2,0,1:T(8,128)} %get-tuple-element.24), calls=%async_computation.1 | async-start | bytes 12582912 | tf_op jit(solution)/shard_map/all_to_all | solution.py:76
  285.8 6.1 %broadcast_multiply_fusion = f32[512,4,768]{2,0,1:T(8,128)} fusion(f32[512,4,768]{2,0,1:T(8,128)} %all_to_all.20), kind=kLoop, calls=%fused_computation.25 | loop fusion | flops 1572864 | bytes 12582912 | tf_op jit(solution)/shard_map/mul | solution.py:80
  291.9 6.7 %copy.35 = f32[512,4,768]{0,2,1:T(8,128)} copy(f32[512,4,768]{2,0,1:T(8,128)} %broadcast_multiply_fusion) | data formatting | bytes 12582912 | tf_op jit(solution)/shard_map/mul | solution.py:80
  298.6 53.4 %all-to-all-done.1 = f32[512,4,768]{2,0,1:T(8,128)} async-done(((f32[512,4,768]{2,0,1:T(8,128)}), f32[512,4,768]{2,0,1:T(8,128)}, u32[]{:S(2)}, u32[]{:S(2)}) %all-to-all-start.1) | async-done | bytes 6291488 | tf_op jit(solution)/shard_map/all_to_all | solution.py:76
  352.0 6.6 %copy.32 = f32[512,4,768]{0,2,1:T(8,128)} copy(f32[512,4,768]{2,0,1:T(8,128)} %all-to-all-done.1) | data formatting | bytes 12582912 | tf_op jit(solution)/shard_map/all_to_all | solution.py:76
  358.5 13.6 %fusion.6 = (f32[1,512,3072]{1,2,0:T(8,128)}, f32[1,512,3072]{1,2,0:T(8,128)}) fusion(f32[1,512,3072]{1,2,0:T(8,128)} %copy.36, f32[512,4,768]{0,2,1:T(8,128)} %copy.32, f32[512,4,768]{0,2,1:T(8,128)} %copy.35), kind=kLoop, calls=%fused_computation.14 | loop fusion | flops 7864320 | bytes 31457280 | tf_op jit(solution)/shard_map/sub | solution.py:81
  372.1 6.6 %copy.38 = f32[1,512,3072]{2,1,0:T(8,128)} copy(f32[1,512,3072]{1,2,0:T(8,128)} %get-tuple-element.13) | data formatting | bytes 12582912
  378.7 6.6 %copy.39 = f32[1,512,3072]{2,1,0:T(8,128)} copy(f32[1,512,3072]{1,2,0:T(8,128)} %get-tuple-element.14) | data formatting | bytes 12582912
  385.2 13.8 %fusion.12 = f32[384,3072]{1,0:T(8,128)S(1)} fusion(bf16[1,4096,3072]{2,1,0:T(8,128)(2,1)} %all-gather.2.cloned.1.call-done, bf16[1,384,4096]{2,1,0:T(8,128)(2,1)S(1)} %copy-done), kind=kOutput, calls=%fused_computation.22 | convolution fusion | flops 9664856064 | bytes 33030144 | tf_op jit(solution)/shard_map/dot_general | solution.py:88
  399.1 1.8 slice_bitcast_fusion
  402.1 1.6 fusion.29
  403.7 2.5 copy.46
  408.1 1.9 copy.43
  410.0 1.6 subtract_convert_fusion.1
  411.6 1.5 fusion.17
  413.1 5.2 %fusion.30 = (f32[4,4,384]{2,1,0:T(4,128)S(1)}, f32[4,4,384,384]{2,3,1,0:T(8,128)}) fusion(f32[4,384,384,4]{2,1,3,0:T(8,128)S(1)} %fusion.17, pred[384,384]{0,1:T(8,128)(4,1)S(1)} %copy-done.3), kind=kOutput, calls=%fused_computation.53 | output fusion | flops 14156159 | bytes 19046400 | tf_op jit(solution)/shard_map/sub | solution.py:48
  418.3 6.0 %fusion.16 = bf16[4,128,4,384]{3,1,2,0:T(8,128)(2,1)} fusion(bf16[384,4,128,1]{0,2,3,1:T(8,128)(2,1)S(1)} %bitcast.65, f32[4,4,384,384]{2,3,1,0:T(8,128)} %get-tuple-element.26, f32[4,4,384]{2,1,0:T(4,128)S(1)} %get-tuple-element.25), kind=kOutput, calls=%fused_computation.28 | convolution fusion | flops 609484800 | bytes 11427840 | tf_op jit(solution)/shard_map/kgts,ske->tkge/dot_general | solution.py:50
  424.3 2.6 copy.37
  (29 shorter events, 5.3 us)
Async XLA Ops:
  7.2 378.1 %copy-start = (bf16[1,384,4096]{2,1,0:T(8,128)(2,1)S(1)}, bf16[1,384,4096]{2,1,0:T(8,128)(2,1)}, u32[]{:S(2)}) copy-start(bf16[1,384,4096]{2,1,0:T(8,128)(2,1)} %param.8) | copy-start | bytes 9437188
  7.2 378.0 %all-gather.2.cloned.1.call-start = ((), (), s32[]{:S(2)}) async-start(), calls=%async_computation.4 | async-start | bytes 28311552 | tf_op jit(solution)/shard_map/all_gather | solution.py:90
  35.3 76.4 %all-to-all-start = ((f32[512,4,768]{2,0,1:T(8,128)}), f32[512,4,768]{2,0,1:T(8,128)}, u32[]{:S(2)}, u32[]{:S(2)}) async-start(f32[512,4,768]{2,0,1:T(8,128)} %copy.31), calls=%async_computation | async-start | bytes 12582912 | tf_op jit(solution)/shard_map/all_to_all | solution.py:60
  53.8 63.1 %copy-start.5 = (s32[4]{0:T(128)S(1)}, s32[4]{0:T(128)}, u32[]{:S(2)}) copy-start(s32[4]{0:T(128)} %param.10) | copy-start | bytes 52
  111.7 75.0 %all-to-all-start.2 = ((f32[512,4,768]{2,0,1:T(8,128)}), f32[512,4,768]{2,0,1:T(8,128)}, u32[]{:S(2)}, u32[]{:S(2)}) async-start(f32[512,4,768]{2,0,1:T(8,128)} %copy.34), calls=%async_computation.2 | async-start | bytes 12582912 | tf_op jit(solution)/shard_map/all_to_all | solution.py:67
  278.7 5.6 %copy-start.4 = (s32[1,384]{1,0:T(1,128)S(1)}, s32[1,384]{1,0:T(1,128)}, u32[]{:S(2)}) copy-start(s32[1,384]{1,0:T(1,128)} %param.9) | copy-start | bytes 4612
  278.7 73.3 %all-to-all-start.1 = ((f32[512,4,768]{2,0,1:T(8,128)}), f32[512,4,768]{2,0,1:T(8,128)}, u32[]{:S(2)}, u32[]{:S(2)}) async-start(f32[512,4,768]{2,0,1:T(8,128)} %get-tuple-element.24), calls=%async_computation.1 | async-start | bytes 12582912 | tf_op jit(solution)/shard_map/all_to_all | solution.py:76
  411.6 1.5 copy-start.3
  413.1 5.2 %copy-start.2 = (bf16[384,512]{0,1:T(8,128)(2,1)S(1)}, bf16[384,512]{0,1:T(8,128)(2,1)}, u32[]{:S(2)}) copy-start(bf16[384,512]{0,1:T(8,128)(2,1)} %copy.43) | copy-start | bytes 1179652
  418.3 8.6 %copy-start.1 = (bf16[1,384,4096]{2,1,0:T(8,128)(2,1)S(1)}, bf16[1,384,4096]{2,1,0:T(8,128)(2,1)}, u32[]{:S(2)}) copy-start(bf16[1,384,4096]{2,1,0:T(8,128)(2,1)} %param.8) | copy-start | bytes 9437188
Sparse Core Ops, SparseCore 0:
  9.7 222.5 all-gather.1
where the time goes:
time: 435 us; the launch traced here: 434 us
  waiting for transfers between devices  175 us (40%)
  local copies, waits for them, and re-layouts  83 us (19%)
  blocking collectives  73.4 us (17%)
  other arithmetic  50.2 us (12%)
  matrix products  21.4 us (5%)
  starting transfers between devices  16.2 us (4%)
  between operations  14.2 us (3%)
    all_to_all x1, blocking collectives, outer_step(): lax.all_to_all(mom_pair, 'replica', split_axis=1, concat_axis=1, tiled=True)  73.4 us
    all_to_all x1, waiting for transfers between devices, outer_step(): lax.all_to_all(momentum[0].reshape(shard_rows, count, columns // count),...  63.4 us
    all_to_all x1, waiting for transfers between devices, outer_step(): lax.all_to_all(pseudo.reshape(shard_rows, count, columns // count), 'repl...  57.8 us
    all_to_all x1, waiting for transfers between devices, outer_step(): lax.all_to_all(grad_pair, 'replica', split_axis=1, concat_axis=1, tiled=T...  53.4 us
    unnamed x20, local copies, waits for them, and re-layouts  38.2 us
    dot_general x1, matrix products, attention_step(): jnp.dot(rows, lax.all_gather(weights, 'fsdp', axis=1, tiled=True)[0], pre...  13.8 us
    sub x1, other arithmetic, outer_step(): anchor[0] - OUTER_RATE * (grad_mean + MOMENTUM_RATE * new_momentum)  13.6 us
    mul x1, other arithmetic, outer_step(): mom_pair = 0.5 * (own_mom + jnp.take(own_mom, partner, axis=1))  12 us
  transfers between devices with their start and end apart: 4, of which 3 were waited for; matrix products, arithmetic and copies ran while one was open for 26% of the time, Pallas kernels for 0%

commit v1 on v0

--- a/solution.py
+++ b/solution.py
@@ -53,30 +53,52 @@
     return context.reshape(count, width_q).astype(jnp.bfloat16)
 
 
-def outer_step(partner, weights, anchor, momentum):
+def pairings(count):
+    if count == 0:
+        return [{}]
+    found = []
+
+    def extend(left, pairs):
+        if not left:
+            found.append(dict(pairs))
+            return
+        first = left[0]
+        for mate in left[1:]:
+            rest = [r for r in left if r not in (first, mate)]
+            extend(rest, pairs + [(first, mate), (mate, first)])
+
+    extend(list(range(count)), [])
+    return found
+
+
+def send_to_mate(values, pairs):
+    return [lax.ppermute(value, "replica", sorted(pairs.items())) for value in values]
+
+
+def exchange_any(values, partner, count):
+    me = lax.axis_index("replica")
+    received = [jnp.zeros_like(value) for value in values]
+    order = jnp.arange(count, dtype=jnp.int32)
+    for step in range(1, count):
+        perm = [(r, (r + step) % count) for r in range(count)]
+
+        def one_round(held):
+            came = [lax.ppermute(value, "replica", perm) for value in values]
+            mine = partner[me] == (me + count - step) % count
+            return [jnp.where(mine, new, old) for new, old in zip(came, held)]
+
+        used = jnp.any(partner == (order + step) % count)
+        received = lax.cond(used, one_round, lambda held: held, received)
+    return received
+
+
+def outer_step(exchange, weights, anchor, momentum):
     pseudo = anchor[0] - weights[0].astype(jnp.float32)
-    count = lax.axis_size("replica")
-    shard_rows, columns = pseudo.shape
-    own_grad = lax.all_to_all(
-        pseudo.reshape(shard_rows, count, columns // count),
-        "replica",
-        split_axis=1,
-        concat_axis=1,
-        tiled=True,
+    mate_pseudo, mate_momentum = exchange(
+        [pseudo.astype(jnp.bfloat16), momentum[0].astype(jnp.bfloat16)]
     )
-    own_mom = lax.all_to_all(
-        momentum[0].reshape(shard_rows, count, columns // count),
-        "replica",
-        split_axis=1,
-        concat_axis=1,
-        tiled=True,
-    )
-    grad_pair = 0.5 * (own_grad + jnp.take(own_grad, partner, axis=1))
-    mom_pair = 0.5 * (own_mom + jnp.take(own_mom, partner, axis=1))
-    grad_mean = lax.all_to_all(grad_pair, "replica", split_axis=1, concat_axis=1, tiled=True)
-    mom_mean = lax.all_to_all(mom_pair, "replica", split_axis=1, concat_axis=1, tiled=True)
-    grad_mean = grad_mean.reshape(shard_rows, columns)
-    mom_mean = mom_mean.reshape(shard_rows, columns)
+    grad_mean = 0.5 * (pseudo + mate_pseudo.astype(jnp.float32))
+    mom_mean = 0.5 * (momentum[0] + mate_momentum.astype(jnp.float32))
     new_momentum = MOMENTUM_RATE * mom_mean + grad_mean
     new_params = anchor[0] - OUTER_RATE * (grad_mean + MOMENTUM_RATE * new_momentum)
     return (new_params[None], new_momentum[None])
@@ -93,10 +115,22 @@
     return attend(projected, places)[None]
 
 
+def step(exchange, tokens, positions, weights, anchor, momentum):
+    context = attention_step(tokens, positions, weights)
+    new_params, new_momentum = outer_step(exchange, weights, anchor, momentum)
+    return (context, new_params, new_momentum)
+
+
 def body(tokens, positions, partner, weights, anchor, momentum):
-    context = attention_step(tokens, positions, weights)
-    new_params, new_momentum = outer_step(partner, weights, anchor, momentum)
-    return (context, new_params, new_momentum)
+    count = lax.axis_size("replica")
+    arrays = (tokens, positions, weights, anchor, momentum)
+    if count > 4:
+        return step(lambda values: exchange_any(values, partner, count), *arrays)
+    branches = [
+        lambda *held, pairs=pairs: step(lambda values: send_to_mate(values, pairs), *held)
+        for pairs in pairings(count)
+    ]
+    return lax.switch(partner[0] - 1, branches, *arrays)
 
 
 def solution(mesh):

time: 435 us -> 294 us (0.68)
  blocking collectives: 73.4 us -> 0 us
  local copies, waits for them, and re-layouts: 83 us -> 11.8 us
  waiting for transfers between devices: 175 us -> 200 us
  other arithmetic: 50.2 us -> 27.3 us
  starting transfers between devices: 16.2 us -> 4.57 us
  loops' own time: 0 us -> 9.92 us
    all_to_all x3 -> x0, waiting for transfers between devices: 175 us -> none  [the longest x1 63.4 us: outer_step(): lax.all_to_all(momentum[0].reshape(shard_rows, count, columns // count),...]
    ppermute x0 -> x2, waiting for transfers between devices: none -> 130 us  [send_to_mate(): lax.ppermute(value, 'replica', sorted(pairs.items()))]
    all_to_all x1 -> x0, blocking collectives: 73.4 us -> none  [outer_step(): lax.all_to_all(mom_pair, 'replica', split_axis=1, concat_axis=1, tiled=True)]
    all_gather x1, waiting for transfers between devices: 0.01 us -> 68.9 us  [attention_step(): lax.all_gather(weights, 'fsdp', axis=1, tiled=True)[0]]
    unnamed x20 -> x2, local copies, waits for them, and re-layouts: 38.2 us -> 1.14 us
    sub x2 -> x0, other arithmetic: 22.7 us -> none  [the longest x1 13.6 us: outer_step(): anchor[0] - OUTER_RATE * (grad_mean + MOMENTUM_RATE * new_momentum)]
    mul x2 -> x0, other arithmetic: 18.1 us -> none  [the longest x1 12 us: outer_step(): mom_pair = 0.5 * (own_mom + jnp.take(own_mom, partner, axis=1))]
    all_to_all x3 -> x0, starting transfers between devices: 16.2 us -> none  [the longest x1 5.6 us: outer_step(): lax.all_to_all(grad_pair, 'replica', split_axis=1, concat_axis=1, tiled=T...]
  transfers between devices with their start and end apart: 4 -> 3, of which waited for: 3 -> 3; matrix products, arithmetic and copies ran while one was open for 26% -> 7% of each run, Pallas kernels for 0% -> 0%
where the time goes in v1:
time: 294 us; the launch traced here: 289 us
  waiting for transfers between devices  200 us (68%)
  other arithmetic  27.3 us (9%)
  matrix products  20.6 us (7%)
  between operations  15 us (5%)
  local copies, waits for them, and re-layouts  11.8 us (4%)
  loops' own time  9.92 us (3%)
  starting transfers between devices  4.57 us (2%)
    ppermute x2, waiting for transfers between devices, send_to_mate(): lax.ppermute(value, 'replica', sorted(pairs.items()))  130 us
    all_gather x1, waiting for transfers between devices, attention_step(): lax.all_gather(weights, 'fsdp', axis=1, tiled=True)[0]  68.9 us
    dot_general x1, matrix products, attention_step(): jnp.dot(rows, lax.all_gather(weights, 'fsdp', axis=1, tiled=True)[0], pre...  14.4 us
    broadcast_in_dim x1, other arithmetic, outer_step(): return (new_params[None], new_momentum[None])  11.6 us
    unnamed x1, loops' own time  9.92 us
    another operation x17, local copies, waits for them, and re-layouts  5.97 us
  transfers between devices with their start and end apart: 3, of which 3 were waited for; matrix products, arithmetic and copies ran while one was open for 7% of the time, Pallas kernels for 0%

profile of v1, /device:TPU:0, one launch (start us, length us, event | category | flops | bytes accessed | tf_op | source)
XLA Modules:
  0.0 288.7 jit_solution(14024246329837650516)
XLA Ops:
  7.8 272.6 %conditional.3 = (f32[1,512,3072]{2,1,0:T(8,128)}, f32[1,512,3072]{2,1,0:T(8,128)}, bf16[1,384,2048]{2,1,0:T(8,128)(2,1)S(1)}) conditional(s32[]{:T(128)} %bitcast.51, (f32[1,512,3072]{2,1,0:T(8,128)}, bf16[1,512,3072]{2,1,0:T(8,128)(2,1)}, f32[1,512,3072]{2,1,0:T(8,128)}, bf16[1,384,4096]{2,1,0:T(8,128)(2,1)}, ...), branch_computations={%region_0.3_spmd, %region_3.6_spmd, %region_6.9_spmd} | conditional | flops 10927693824 | bytes 316505920
  7.8 0.0 all-gather.4.cloned.1.call-start
  7.9 0.7 all-gather.4.cloned.1.call-update
  8.6 0.0 copy-start
  8.6 0.0 copy-start.3
  8.6 5.1 %bitcast_convert_fusion = bf16[512,3072]{1,0:T(8,128)(2,1)} fusion(f32[1,512,3072]{2,1,0:T(8,128)} %get-tuple-element.42), kind=kLoop, calls=%fused_computation.9 | loop fusion | flops 1572864 | bytes 9437184 | tf_op jit(solution)/shard_map/cond/branch_0_fun/convert_element_type | solution.py:98
  13.7 2.9 %collective-permute-start.1 = (bf16[512,3072]{1,0:T(8,128)(2,1)}, bf16[512,3072]{1,0:T(8,128)(2,1)}, u32[]{:S(2)}, u32[]{:S(2)}) collective-permute-start(bf16[512,3072]{1,0:T(8,128)(2,1)} %bitcast_convert_fusion), channel_id=1, source_target_pairs={{0,8},{8,0},{16,24},{24,16},{1,9},{9,1},{17,25},{25,17},{2,10},{10... | collective-permute-start | bytes 9437192 | tf_op jit(solution)/shard_map/cond/branch_0_fun/ppermute | solution.py:75
  16.6 2.7 fusion.14
  19.3 1.6 collective-permute-start
  20.9 0.7 fusion.24
  21.7 0.8 multiply_cosine_fusion
  22.4 63.4 %collective-permute-done.1 = bf16[512,3072]{1,0:T(8,128)(2,1)} collective-permute-done((bf16[512,3072]{1,0:T(8,128)(2,1)}, bf16[512,3072]{1,0:T(8,128)(2,1)}, u32[]{:S(2)}, u32[]{:S(2)}) %collective-permute-start.1) | collective-permute-done | bytes 3145760 | tf_op jit(solution)/shard_map/cond/branch_0_fun/ppermute | solution.py:75
  85.8 66.6 %collective-permute-done = bf16[512,3072]{1,0:T(8,128)(2,1)} collective-permute-done((bf16[512,3072]{1,0:T(8,128)(2,1)}, bf16[512,3072]{1,0:T(8,128)(2,1)}, u32[]{:S(2)}, u32[]{:S(2)}) %collective-permute-start) | collective-permute-done | bytes 3145760 | tf_op jit(solution)/shard_map/cond/branch_0_fun/ppermute | solution.py:75
  152.4 11.6 %fusion.16 = (f32[1,512,3072]{2,1,0:T(8,128)}, f32[1,512,3072]{2,1,0:T(8,128)}) fusion(bf16[512,3072]{1,0:T(8,128)(2,1)} %collective-permute-done, bf16[1,512,3072]{2,1,0:T(8,128)(2,1)S(1)} %copy-done, f32[1,512,3072]{2,1,0:T(8,128)} %get-tuple-element.40, bf16[512,3072]{1,0:T(8,128)(2,1)} %collective-permute-done.1, f32[1,512,3072]{2,1,0:T(8,128)} %get-tuple-element.42), kind=kLoop, calls=%fused_computation.25 | loop fusion | flops 20447232 | bytes 34603008 | tf_op jit(solution)/shard_map/cond/branch_0_fun/broadcast_in_dim | solution.py:104
  164.0 68.9 %all-gather.4.cloned.1.call-done = bf16[1,4096,3072]{2,1,0:T(8,128)(2,1)} async-done(((bf16[1,512,3072]{2,1,0:T(8,128)(2,1)}), bf16[1,4096,3072]{2,1,0:T(8,128)(2,1)}) %all-gather.4.cloned.1.call-update) | async-done | bytes 25165840 | tf_op jit(solution)/shard_map/cond/branch_0_fun/all_gather | solution.py:112
  232.9 14.4 %fusion.11 = f32[384,3072]{1,0:T(8,128)S(1)} fusion(bf16[1,4096,3072]{2,1,0:T(8,128)(2,1)} %all-gather.4.cloned.1.call-done, bf16[1,384,4096]{2,1,0:T(8,128)(2,1)} %get-tuple-element.43), kind=kOutput, calls=%fused_computation.19 | convolution fusion | flops 9664856064 | bytes 33030144 | tf_op jit(solution)/shard_map/cond/branch_0_fun/dot_general | solution.py:110
  247.3 0.1 slice.109
  247.4 0.9 slice.71
  248.3 1.8 slice_bitcast_fusion
  250.1 0.9 copy.37
  251.1 2.5 copy.49
  253.6 2.3 reshape.335
  255.9 1.1 subtract_convert_fusion
  256.9 0.4 copy.11
  257.4 0.5 fusion.90
  257.8 0.4 copy.12
  258.3 0.2 subtract_convert_fusion.1
  258.5 1.5 fusion.18
  260.0 5.2 %fusion.91 = (f32[4,4,384]{2,1,0:T(4,128)S(1)}, f32[4,4,384,384]{2,3,1,0:T(8,128)}) fusion(f32[4,384,384,4]{2,1,3,0:T(8,128)S(1)} %fusion.18, pred[384,384]{0,1:T(8,128)(4,1)S(1)} %copy-done.13), kind=kOutput, calls=%fused_computation.142 | output fusion | flops 14156159 | bytes 19046400 | tf_op jit(solution)/shard_map/cond/branch_0_fun/sub | solution.py:48
  265.2 4.7 %fusion.17 = bf16[4,128,4,384]{3,1,2,0:T(8,128)(2,1)S(1)} fusion(bf16[384,4,128,1]{0,2,3,1:T(8,128)(2,1)S(1)} %bitcast.251, f32[4,4,384,384]{2,3,1,0:T(8,128)} %get-tuple-element.79, f32[4,4,384]{2,1,0:T(4,128)S(1)} %get-tuple-element.78), kind=kOutput, calls=%fused_computation.26 | convolution fusion | flops 609484800 | bytes 11427840 | tf_op jit(solution)/shard_map/cond/branch_0_fun/kgts,ske->tkge/dot_general | solution.py:50
  269.9 0.8 copy.40
  280.4 1.1 copy-done.9
  (14 shorter events, 0.1 us)
Async XLA Ops:
  7.8 225.1 %all-gather.4.cloned.1.call-start = ((), (), s32[]{:S(2)}) async-start(), calls=%async_computation | async-start | bytes 28311552 | tf_op jit(solution)/shard_map/cond/branch_0_fun/all_gather | solution.py:112
  8.6 8.0 %copy-start = (bf16[1,512,3072]{2,1,0:T(8,128)(2,1)S(1)}, bf16[1,512,3072]{2,1,0:T(8,128)(2,1)}, u32[]{:S(2)}) copy-start(bf16[1,512,3072]{2,1,0:T(8,128)(2,1)} %get-tuple-element.41) | copy-start | bytes 9437188 | tf_op jit(solution)/shard_map/conditional.1
  8.6 8.0 %copy-start.3 = (f32[1,512,3072]{2,1,0:T(8,128)S(1)}, f32[1,512,3072]{2,1,0:T(8,128)}, u32[]{:S(2)}) copy-start(f32[1,512,3072]{2,1,0:T(8,128)} %get-tuple-element.40) | copy-start | bytes 18874372 | tf_op jit(solution)/shard_map/conditional.1
  13.7 72.2 %collective-permute-start.1 = (bf16[512,3072]{1,0:T(8,128)(2,1)}, bf16[512,3072]{1,0:T(8,128)(2,1)}, u32[]{:S(2)}, u32[]{:S(2)}) collective-permute-start(bf16[512,3072]{1,0:T(8,128)(2,1)} %bitcast_convert_fusion), channel_id=1, source_target_pairs={{0,8},{8,0},{16,24},{24,16},{1,9},{9,1},{17,25},{25,17},{2,10},{10... | collective-permute-start | bytes 9437192 | tf_op jit(solution)/shard_map/cond/branch_0_fun/ppermute | solution.py:75
  16.6 4.3 %copy-start.16 = (s32[1,384]{1,0:T(1,128)S(1)}, s32[1,384]{1,0:T(1,128)}, u32[]{:S(2)}) copy-start(s32[1,384]{1,0:T(1,128)} %get-tuple-element.44) | copy-start | bytes 4612 | tf_op jit(solution)/shard_map/conditional.1
  19.3 133.1 %collective-permute-start = (bf16[512,3072]{1,0:T(8,128)(2,1)}, bf16[512,3072]{1,0:T(8,128)(2,1)}, u32[]{:S(2)}, u32[]{:S(2)}) collective-permute-start(bf16[512,3072]{1,0:T(8,128)(2,1)} %fusion.14), channel_id=1, source_target_pairs={{0,8},{8,0},{16,24},{24,16},{1,9},{9,1},{17,25},{25,17},{2,10},{10... | collective-permute-start | bytes 9437192 | tf_op jit(solution)/shard_map/cond/branch_0_fun/ppermute | solution.py:75
  255.9 1.5 copy-start.6
  258.5 1.5 copy-start.13
  260.0 5.2 %copy-start.10 = (bf16[384,512]{0,1:T(8,128)(2,1)S(1)}, bf16[384,512]{0,1:T(8,128)(2,1)}, u32[]{:S(2)}) copy-start(bf16[384,512]{0,1:T(8,128)(2,1)} %copy.37) | copy-start | bytes 1179652 | tf_op jit(solution)/shard_map/conditional.1
  280.4 1.1 copy-start.9
Sparse Core Ops, SparseCore 0:
  10.3 222.5 all-gather.3

commit v2 on v1

--- a/solution.py
+++ b/solution.py
@@ -1,6 +1,8 @@
 import jax
 import jax.numpy as jnp
 from jax import lax
+from jax.experimental import pallas as pl
+from jax.experimental.pallas import tpu as pltpu
 from jax.sharding import PartitionSpec as P
 
 D = 4096
@@ -53,28 +55,6 @@
     return context.reshape(count, width_q).astype(jnp.bfloat16)
 
 
-def pairings(count):
-    if count == 0:
-        return [{}]
-    found = []
-
-    def extend(left, pairs):
-        if not left:
-            found.append(dict(pairs))
-            return
-        first = left[0]
-        for mate in left[1:]:
-            rest = [r for r in left if r not in (first, mate)]
-            extend(rest, pairs + [(first, mate), (mate, first)])
-
-    extend(list(range(count)), [])
-    return found
-
-
-def send_to_mate(values, pairs):
-    return [lax.ppermute(value, "replica", sorted(pairs.items())) for value in values]
-
-
 def exchange_any(values, partner, count):
     me = lax.axis_index("replica")
     received = [jnp.zeros_like(value) for value in values]
@@ -115,6 +95,486 @@
     return attend(projected, places)[None]
 
 
+LINE = 4
+CORES = 2
+SQUARE = 4
+UNIT = HEAD_DIM
+GROUP = HEADS // KV_HEADS
+HALF_GROUPS = KV_HEADS // CORES
+CHUNKS = (("k0", "k1", "v0", "v1"), ("q0",) * GROUP, ("q1",) * 2, ("q1",) * 2)
+FIRST_UNIT = tuple(sum(len(c) for c in CHUNKS[:j]) for j in range(len(CHUNKS)))
+HALF_UNITS = sum(len(c) for c in CHUNKS)
+PAIR = 2 * UNIT
+MIB = 1024 * 1024
+SMALL = pl.CostEstimate(flops=1, bytes_accessed=1, transcendentals=0)
+HBM = pl.BlockSpec(memory_space=pltpu.HBM)
+MARK = jax.ShapeDtypeStruct((8, 128), jnp.float32)
+
+
+def pairs_of_half(half):
+    per_half = HEADS // CORES // 2
+    pairs = [HEADS // 2 + half, (HEADS + KV_HEADS) // 2 + half]
+    pairs += [half * per_half + at for at in range(per_half)]
+    return jnp.stack([jnp.asarray(pair, jnp.int32) for pair in pairs])
+
+
+def mark_spec():
+    return pl.BlockSpec(MARK.shape, lambda *at: (0, 0))
+
+
+def hand_kernel(lead, tokens, *refs):
+    out, mark = refs[-2:]
+    out[...] = tokens[...]
+    mark[...] = jnp.zeros_like(mark)
+
+
+def hand_tokens(tokens, lead):
+    rows, columns = tokens.shape
+    block = columns // LINE
+    return pl.pallas_call(
+        hand_kernel,
+        grid_spec=pltpu.PrefetchScalarGridSpec(
+            num_scalar_prefetch=1,
+            grid=(LINE - 1,),
+            in_specs=[pl.BlockSpec((rows, block), lambda at, lead: (0, lead[0] + at))],
+            out_specs=(pl.BlockSpec((rows, block), lambda at, lead: (0, at)), mark_spec()),
+        ),
+        out_shape=(jax.ShapeDtypeStruct((rows, columns - block), tokens.dtype), MARK),
+        compiler_params=pltpu.CompilerParams(vmem_limit_bytes=50 * MIB),
+        cost_estimate=SMALL,
+        name="hand_tokens",
+    )(lead, tokens)
+
+
+def pack_kernel(pairs, own, sibling, *refs):
+    out, mark = refs[-2:]
+    out[0] = own[...]
+    out[1] = sibling[...]
+    mark[...] = jnp.zeros_like(mark)
+
+
+def pack(first, count, own, sibling, pairs, after=()):
+    depth = own.shape[0]
+    column = pl.BlockSpec((depth, PAIR), lambda at, pairs: (0, pairs[first + at]))
+    return pl.pallas_call(
+        pack_kernel,
+        grid_spec=pltpu.PrefetchScalarGridSpec(
+            num_scalar_prefetch=1,
+            grid=(count,),
+            in_specs=[column, column] + [HBM] * len(after),
+            out_specs=(
+                pl.BlockSpec((CORES, depth, PAIR), lambda at, pairs: (0, 0, at)),
+                mark_spec(),
+            ),
+        ),
+        out_shape=(jax.ShapeDtypeStruct((CORES, depth, count * PAIR), own.dtype), MARK),
+        compiler_params=pltpu.CompilerParams(vmem_limit_bytes=50 * MIB),
+        cost_estimate=SMALL,
+        name="pack",
+    )(pairs, own, sibling, *after)
+
+
+def touch(value, *after):
+    def kernel(*refs):
+        refs[-1][...] = jnp.zeros_like(refs[-1])
+
+    return pl.pallas_call(
+        kernel,
+        in_specs=[HBM] * (1 + len(after)),
+        out_specs=(HBM, pl.BlockSpec(memory_space=pltpu.VMEM)),
+        out_shape=(jax.ShapeDtypeStruct(value.shape, value.dtype), MARK),
+        input_output_aliases={0: 0},
+        cost_estimate=SMALL,
+        name="touch",
+    )(value, *after)
+
+
+def project_kernel(groups, based, needs_middle, table, *refs):
+    tokens, refs = refs[: 2 * groups], refs[2 * groups :]
+    blocks, refs = refs[:groups], refs[groups:]
+    out, mark = refs[-2:]
+    mark[...] = jnp.zeros_like(mark)
+    rows = tokens[0].shape[0]
+    depth, span = blocks[0].shape[1:]
+    tile = min(span, 512)
+    core = table[0]
+
+    def multiply():
+        for half in range(CORES):
+            here = slice(half * rows, (half + 1) * rows)
+            for left in range(0, span, tile):
+                columns = slice(left, left + tile)
+                total = refs[0][here, columns] if based else None
+                for group in range(groups):
+                    source = tokens[2 * group + half]
+                    for k in range(CORES):
+                        taken = (core + k) % CORES * depth
+                        taken = pl.ds(pl.multiple_of(taken, depth), depth)
+                        part = jnp.dot(
+                            source[:, taken],
+                            blocks[group][k, :, columns],
+                            preferred_element_type=jnp.float32,
+                        )
+                        total = part if total is None else total + part
+                out[here, columns] = total.astype(out.dtype)
+
+    if not needs_middle:
+        multiply()
+        return
+    pl.when(table[1] == 1)(multiply)
+
+    @pl.when(table[1] == 0)
+    def _():
+        out[...] = refs[0][...].astype(out.dtype) if based else jnp.zeros_like(out)
+
+
+def project(span, table, groups, dtype, base=None, needs_middle=True, after=()):
+    first_unit, width = span
+    rows = groups[0][0][0].shape[0]
+    depth = groups[0][2].shape[1]
+    size = (CORES * rows, width * UNIT)
+    token_specs, block_specs, arrays, blocks = [], [], [], []
+    for tokens, slot, held, place in groups:
+        token_specs += [
+            pl.BlockSpec((rows, CORES * depth), lambda i, table, slot=slot: (0, table[slot]))
+        ] * 2
+        block_specs.append(
+            pl.BlockSpec((CORES, depth, width * UNIT), lambda i, table, place=place: (0, 0, place))
+        )
+        arrays += list(tokens)
+        blocks.append(held)
+    bases = () if base is None else (base,)
+    return pl.pallas_call(
+        lambda *refs: project_kernel(len(groups), base is not None, needs_middle, *refs),
+        grid_spec=pltpu.PrefetchScalarGridSpec(
+            num_scalar_prefetch=1,
+            grid=(1,),
+            in_specs=token_specs
+            + block_specs
+            + [pl.BlockSpec(size, lambda i, table: (0, first_unit // width))] * len(bases)
+            + [HBM] * len(after),
+            out_specs=(pl.BlockSpec(size, lambda i, table: (0, 0)), mark_spec()),
+        ),
+        out_shape=(jax.ShapeDtypeStruct(size, dtype), MARK),
+        compiler_params=pltpu.CompilerParams(vmem_limit_bytes=56 * MIB),
+        cost_estimate=SMALL,
+        name="project",
+    )(table, *arrays, *blocks, *bases, *after)
+
+
+def joined_rows(own, came, rows, unit):
+    columns = slice(unit * UNIT, (unit + 1) * UNIT)
+    return (own[rows, columns] + came[rows, columns].astype(jnp.float32)) * D ** (-0.5)
+
+
+def turned(value, cosine, sine):
+    return (value * cosine + pltpu.roll(value, HEAD_DIM // 2, 1) * sine).astype(jnp.bfloat16)
+
+
+def keep_kernel(own, came, cosine, sine, *refs):
+    keys, values, mark = refs[-3:]
+    mark[...] = jnp.zeros_like(mark)
+    count = cosine.shape[1]
+    for block in range(CORES):
+        rows = slice(block * count, (block + 1) * count)
+        for group in range(HALF_GROUPS):
+            key = joined_rows(own, came, rows, group)
+            keys[group, block] = turned(key, cosine[block], sine[block])
+            value = joined_rows(own, came, rows, HALF_GROUPS + group)
+            values[group, block] = value.astype(jnp.bfloat16)
+
+
+def keep_keys(own, came, cosine, sine, after=()):
+    kept = jax.ShapeDtypeStruct((HALF_GROUPS, CORES) + cosine.shape[1:], jnp.bfloat16)
+    whole = pl.BlockSpec(memory_space=pltpu.VMEM)
+    return pl.pallas_call(
+        keep_kernel,
+        in_specs=[whole] * 4 + [HBM] * len(after),
+        out_shape=(kept, kept, MARK),
+        compiler_params=pltpu.CompilerParams(vmem_limit_bytes=24 * MIB),
+        cost_estimate=SMALL,
+        name="keep_keys",
+    )(own, came, cosine, sine, *after)
+
+
+def attend_kernel(heads, group, own, came, cosine, sine, places, keys, values, *refs):
+    outs, mark, hidden = refs[-4:-2], refs[-2], refs[-1]
+    mark[...] = jnp.zeros_like(mark)
+    count = cosine.shape[1]
+    tile = HEAD_DIM
+    for block in reversed(range(CORES)):
+        row = lax.broadcasted_iota(jnp.int32, (count, count), 0)
+        distance = row - lax.broadcasted_iota(jnp.int32, (count, count), 1)
+        visible = (distance >= 0) & (distance <= places[block])
+        hidden[...] = jnp.where(visible, 0.0, -1e30)
+        for head in range(heads):
+            rows = slice(block * count, (block + 1) * count)
+            query = turned(joined_rows(own, came, rows, head), cosine[block], sine[block])
+            for top in range(0, count, tile):
+                width = top + tile
+                scores = lax.dot_general(
+                    query[top:width],
+                    keys[group, block, :width],
+                    (((1,), (1,)), ((), ())),
+                    preferred_element_type=jnp.float32,
+                )
+                scores = scores + hidden[top:width, :width]
+                scores = (scores - jnp.max(scores, -1, keepdims=True)) * HEAD_DIM ** (-0.5)
+                exponent = jnp.exp(scores)
+                share = jnp.sum(exponent, -1, keepdims=True)
+                mixed = jnp.dot(
+                    exponent.astype(jnp.bfloat16),
+                    values[group, block, :width],
+                    preferred_element_type=jnp.float32,
+                )
+                outs[block][top:width, head * UNIT : (head + 1) * UNIT] = (mixed / share).astype(
+                    jnp.bfloat16
+                )
+
+
+def attend_chunk(chunk, own, came, cosine, sine, places, held, after=()):
+    count = cosine.shape[1]
+    heads, group = len(CHUNKS[chunk]), int(CHUNKS[chunk][0][1])
+    out = jax.ShapeDtypeStruct((count, heads * UNIT), jnp.bfloat16)
+    whole = pl.BlockSpec(memory_space=pltpu.VMEM)
+    return pl.pallas_call(
+        lambda *refs: attend_kernel(heads, group, *refs),
+        in_specs=[whole] * 7 + [HBM] * len(after),
+        out_shape=(out, out, MARK),
+        scratch_shapes=[pltpu.VMEM((count, count), jnp.float32)],
+        compiler_params=pltpu.CompilerParams(vmem_limit_bytes=24 * MIB),
+        cost_estimate=SMALL,
+        name="attend_chunk",
+    )(own, came, cosine, sine, places, *held, *after)
+
+
+PARTS = 2
+TILE = 64
+
+
+def sent_kernel(lead, anchor, weights, momentum, *refs):
+    out, mark = refs[-2:]
+    mark[...] = jnp.zeros_like(mark)
+    out[0] = momentum[...].astype(out.dtype)
+    out[1] = (anchor[...] - weights[...].astype(jnp.float32)).astype(out.dtype)
+
+
+def sent_part(part, anchor, weights, momentum, after=()):
+    rows, columns = anchor.shape
+    steps = rows // PARTS // TILE
+    here = pl.BlockSpec((TILE, columns), lambda i, lead: (lead[0] * steps + i, 0))
+    return pl.pallas_call(
+        sent_kernel,
+        grid_spec=pltpu.PrefetchScalarGridSpec(
+            num_scalar_prefetch=1,
+            grid=(steps,),
+            in_specs=[here] * 3 + [HBM] * len(after),
+            out_specs=(pl.BlockSpec((2, TILE, columns), lambda i, lead: (0, i, 0)), mark_spec()),
+        ),
+        out_shape=(
+            jax.ShapeDtypeStruct((2, rows // PARTS, columns), jnp.bfloat16),
+            MARK,
+        ),
+        compiler_params=pltpu.CompilerParams(vmem_limit_bytes=56 * MIB),
+        cost_estimate=SMALL,
+        name="sent_part",
+    )(part, anchor, weights, momentum, *after)
+
+
+def outer_kernel(steps, table, anchor, weights, momentum, *refs):
+    new_params, new_momentum, mark = refs[-3:]
+    mark[...] = jnp.zeros_like(mark)
+    part = pl.program_id(0) // steps
+    for at in range(4):
+
+        @pl.when(table[part] == at)
+        def _():
+            mate = refs[at]
+            start = anchor[...]
+            pseudo = start - weights[...].astype(jnp.float32)
+            grad_mean = 0.5 * (pseudo + mate[1].astype(jnp.float32))
+            mom_mean = 0.5 * (momentum[...] + mate[0].astype(jnp.float32))
+            moved = MOMENTUM_RATE * mom_mean + grad_mean
+            new_momentum[...] = moved
+            new_params[...] = start - OUTER_RATE * (grad_mean + MOMENTUM_RATE * moved)
+
+
+def outer_update(table, anchor, weights, momentum, came, after=()):
+    rows, columns = anchor.shape
+    steps = rows // PARTS // TILE
+    here = pl.BlockSpec((TILE, columns), lambda i, table: (i, 0))
+
+    def chosen(at):
+        return pl.BlockSpec(
+            (2, TILE, columns),
+            lambda i, table: (0, jnp.where(table[i // steps] == at, i % steps, 0), 0),
+        )
+
+    full = jax.ShapeDtypeStruct((rows, columns), jnp.float32)
+    return pl.pallas_call(
+        lambda *refs: outer_kernel(steps, *refs),
+        grid_spec=pltpu.PrefetchScalarGridSpec(
+            num_scalar_prefetch=1,
+            grid=(PARTS * steps,),
+            in_specs=[here] * 3 + [chosen(at) for at in range(4)] + [HBM] * len(after),
+            out_specs=(here, here, pl.BlockSpec(MARK.shape, lambda i, table: (0, 0))),
+        ),
+        out_shape=(full, full, MARK),
+        compiler_params=pltpu.CompilerParams(vmem_limit_bytes=56 * MIB),
+        cost_estimate=SMALL,
+        name="outer_update",
+    )(table, anchor, weights, momentum, *came, *after)
+
+
+def line_step(partner, tokens, positions, weights, anchor, momentum):
+    rows, places = tokens[0], positions[0]
+    own_rows = weights[0]
+    start, moved = anchor[0], momentum[0]
+    count, depth = rows.shape[0], own_rows.shape[0]
+    me = lax.axis_index("fsdp")
+    chip, core = me // CORES, me % CORES
+    last = LINE - 1
+    chunks = len(CHUNKS)
+
+    def over(value, pairs):
+        return lax.ppermute(value, "fsdp", pairs)
+
+    cores = range(CORES)
+    swap = [(f, f ^ 1) for f in range(LINE * CORES)]
+    inward = [(a * CORES + c, b * CORES + c) for a, b in ((0, 1), (last, last - 1)) for c in cores]
+    across = [(a * CORES + c, b * CORES + c) for a, b in ((1, 2), (2, 1)) for c in cores]
+    outward = [(b, a) for a, b in inward]
+    across += [(a * CORES + c, a * CORES + 1 - c) for a in (0, last) for c in cores]
+
+    other_rows = over(own_rows, across)
+    sibling_rows = over(own_rows, swap)
+    lead = (chip < LINE // 2).astype(jnp.int32)
+    handed, mark = hand_tokens(rows, lead[None])
+    handed = over(handed, inward)
+
+    distance = partner[0]
+    part_rows = depth // PARTS
+
+    along = [[(r, r ^ 1) for r in range(SQUARE)], [(r, r ^ 2) for r in range(SQUARE)]]
+    values = (start, own_rows, moved)
+    swapped = (distance == 2).astype(jnp.int32)
+    first = []
+    for part in (swapped, 1 - swapped):
+        made, mark = sent_part(part[None], *values, (mark,))
+        first.append(made)
+    came = [lax.ppermute(first[at], "replica", along[at]) for at in range(2)]
+    table = jnp.stack([jnp.where(distance == 3, 3, distance - 1), jnp.where(distance == 2, 3, 2)])
+
+    pairs = pairs_of_half(core)
+    packed, marks = [], (mark,)
+    for j in range(chunks):
+        made, mark = pack(
+            FIRST_UNIT[j] // 2, len(CHUNKS[j]) // 2, own_rows, sibling_rows, pairs, marks
+        )
+        packed.append(made)
+        marks = (mark,)
+    sibling_tokens = over(rows, swap)
+    both = jnp.stack([places, over(places, swap)])
+    frequency = ROPE_BASE ** (
+        -(jnp.arange(HEAD_DIM // 2, dtype=jnp.float32) * 2.0) / HEAD_DIM
+    )
+    angles = both.astype(jnp.float32)[:, :, None] * frequency
+    cosine, sine = jnp.cos(angles), jnp.sin(angles)
+    cosine = jnp.concatenate([cosine, cosine], -1)
+    sine = jnp.concatenate([-sine, sine], -1)
+    reach = both[:, :, None]
+
+    near_chip = jnp.where(chip < LINE // 2, 0, last)
+    middle = (chip > 0) & (chip < last)
+    chips = jnp.stack([chip, last - chip, last - near_chip, near_chip])
+    handed_chips = jnp.clip(chips - lead, 0, LINE - 2)
+    spots = jnp.concatenate([jnp.stack([core, middle.astype(jnp.int32)]), chips, handed_chips])
+    OWN, OTHER, FAR, NEAR, HANDED = 2, 3, 4, 5, 4
+    every = (0, HALF_UNITS)
+    ours = (rows, sibling_tokens)
+
+    all_own, mark = pack(0, HALF_UNITS // 2, own_rows, sibling_rows, pairs, marks)
+    own_sum, mark = project(
+        every, spots, [(ours, OWN, all_own, 0)], jnp.float32, needs_middle=False,
+        after=(mark, cosine, sine),
+    )
+    handed, mark = touch(handed, mark)
+    theirs = (handed, over(handed, swap))
+    near, far = [over(packed[0], inward)], []
+
+    def stage(j, *after):
+        near[j], mark = touch(near[j], *far[j - 1 :], *after)
+        far.append(over(near[j], across))
+        if j + 1 < chunks:
+            near.append(over(touch(packed[j + 1], mark)[0], inward))
+        return mark
+
+    other_rows, mark = touch(other_rows, mark, near[0])
+    mark = stage(0, mark)
+    other_sibling_rows = over(other_rows, swap)
+    came = [touch(value, mark)[0] for value in came]
+    second = [jnp.where(distance == 3, came[1 - at], first[1 - at]) for at in range(2)]
+    came += [lax.ppermute(second[at], "replica", along[at]) for at in range(2)]
+    handed_sum, mark = project(
+        every, spots, [(theirs, OWN + HANDED, all_own, 0)], jnp.float32, after=(mark, *second)
+    )
+    all_other, mark = pack(0, HALF_UNITS // 2, other_rows, other_sibling_rows, pairs, (mark,))
+    handed_sum, mark = project(
+        every, spots, [(theirs, OTHER + HANDED, all_other, 0)], jnp.float32, handed_sum,
+        after=(mark,),
+    )
+    mark = stage(1, mark)
+    own_sum, mark = project(
+        every, spots, [(ours, OTHER, all_other, 0)], jnp.float32, own_sum, after=(mark,)
+    )
+
+    contexts, owns, backs = [], [], []
+
+    def product(j, *after):
+        result, mark = project(
+            (FIRST_UNIT[j], len(CHUNKS[j])), spots, [(theirs, FAR + HANDED, far[j], 0)],
+            jnp.bfloat16, handed_sum, after=after,
+        )
+        backs.append(over(result, outward))
+        return mark
+
+    def own(j, *after):
+        result, mark = project(
+            (FIRST_UNIT[j], len(CHUNKS[j])), spots,
+            [(ours, FAR, far[j], 0), (ours, NEAR, near[j], 0)], jnp.float32, own_sum, after=after,
+        )
+        owns.append(result)
+        return mark
+
+    def attention(j, *after):
+        left, right, mark = attend_chunk(j, owns[j], backs[j], cosine, sine, reach, held, after)
+        contexts.append((left, over(right, swap)))
+        return mark
+
+    mark = product(0, mark)
+    mark = own(0, mark)
+    mark = stage(2, mark)
+    mark = product(1, mark)
+    mark = own(1, mark)
+    mark = stage(3, mark)
+    mark = product(2, mark)
+    *held, mark = keep_keys(owns[0], backs[0], cosine, sine, (mark,))
+    mark = own(2, mark)
+    mark = product(3, mark)
+    mark = attention(1, mark)
+    mark = own(3, mark, came[2], came[3])
+    mark = attention(2, mark)
+    mark = attention(3, mark)
+    new_params, new_momentum, mark = outer_update(table, start, own_rows, moved, came, (mark,))
+
+    mine = jnp.concatenate([first for first, _ in contexts], 1)
+    came = jnp.concatenate([second for _, second in contexts], 1)
+    context = jnp.where(
+        core == 0, jnp.concatenate([mine, came], 1), jnp.concatenate([came, mine], 1)
+    )
+    return (context[None], new_params[None], new_momentum[None])
+
+
 def step(exchange, tokens, positions, weights, anchor, momentum):
     context = attention_step(tokens, positions, weights)
     new_params, new_momentum = outer_step(exchange, weights, anchor, momentum)
@@ -124,13 +584,9 @@
 def body(tokens, positions, partner, weights, anchor, momentum):
     count = lax.axis_size("replica")
     arrays = (tokens, positions, weights, anchor, momentum)
-    if count > 4:
-        return step(lambda values: exchange_any(values, partner, count), *arrays)
-    branches = [
-        lambda *held, pairs=pairs: step(lambda values: send_to_mate(values, pairs), *held)
-        for pairs in pairings(count)
-    ]
-    return lax.switch(partner[0] - 1, branches, *arrays)
+    if count == SQUARE and lax.axis_size("fsdp") == LINE * CORES:
+        return line_step(partner, *arrays)
+    return step(lambda values: exchange_any(values, partner, count), *arrays)
 
 
 def solution(mesh):

time: 294 us -> 242 us (0.82)
  waiting for transfers between devices: 200 us -> 38 us
  Pallas kernels: 0 us -> 128 us
  starting transfers between devices: 4.57 us -> 42.3 us
  matrix products: 20.6 us -> 0 us
  other arithmetic: 27.3 us -> 12.4 us
  between operations: 15 us -> 1.21 us
  loops' own time: 9.92 us -> 0 us
  local copies, waits for them, and re-layouts: 11.8 us -> 17.3 us
    pallas_call x0 -> x37, Pallas kernels: none -> 128 us  [the longest x12 59.9 us: project(): pl.pallas_call(lambda *refs: project_kernel(len(groups), base is not None...]
    ppermute x2 -> x26, waiting for transfers between devices: 130 us -> 38 us  [the longest x22 38 us: over(): return lax.ppermute(value, 'fsdp', pairs)]
    all_gather x1 -> x0, waiting for transfers between devices: 68.9 us -> none  [attention_step(): lax.all_gather(weights, 'fsdp', axis=1, tiled=True)[0]]
    ppermute x2 -> x26, starting transfers between devices: 4.53 us -> 42.3 us  [the longest x22 36.2 us: over(): return lax.ppermute(value, 'fsdp', pairs)]
    dot_general x3 -> x0, matrix products: 20.6 us -> none  [the longest x1 14.4 us: attention_step(): jnp.dot(rows, lax.all_gather(weights, 'fsdp', axis=1, tiled=True)[0], pre...]
    unnamed x2 -> x69, local copies, waits for them, and re-layouts: 1.14 us -> 16.3 us
    broadcast_in_dim x1, other arithmetic: 11.6 us -> 0.01 us  [line_step(): reach = both[:, :, None]]
    unnamed x1 -> x0, loops' own time: 9.92 us -> none
  transfers between devices with their start and end apart: 3 -> 26, of which waited for: 3 -> 5; matrix products, arithmetic and copies ran while one was open for 7% -> 5% of each run, Pallas kernels for 0% -> 53%
where the time goes in v2:
time: 242 us; the launch traced here: 239 us
  Pallas kernels  128 us (53%)
  starting transfers between devices  42.3 us (17%)
  waiting for transfers between devices  38 us (16%)
  local copies, waits for them, and re-layouts  17.3 us (7%)
  other arithmetic  12.4 us (5%)
    pallas_call x12, Pallas kernels, project(): pl.pallas_call(lambda *refs: project_kernel(len(groups), base is not None...  59.9 us
    ppermute x22, waiting for transfers between devices, over(): return lax.ppermute(value, 'fsdp', pairs)  38 us
    ppermute x22, starting transfers between devices, over(): return lax.ppermute(value, 'fsdp', pairs)  36.2 us
    unnamed x69, local copies, waits for them, and re-layouts  16.3 us
    pallas_call x6, Pallas kernels, pack(): pl.pallas_call(pack_kernel, grid_spec=pltpu.PrefetchScalarGridSpec(num_sc...  16.2 us
    pallas_call x1, Pallas kernels, outer_update(): pl.pallas_call(lambda *refs: outer_kernel(steps, *refs), grid_spec=pltpu....  15.6 us
    pallas_call x3, Pallas kernels, attend_chunk(): pl.pallas_call(lambda *refs: attend_kernel(heads, group, *refs), in_specs...  14.6 us
    pallas_call x2, Pallas kernels, sent_part(): pl.pallas_call(sent_kernel, grid_spec=pltpu.PrefetchScalarGridSpec(num_sc...  10.7 us
  transfers between devices with their start and end apart: 26, of which 5 were waited for; matrix products, arithmetic and copies ran while one was open for 5% of the time, Pallas kernels for 53%

profile of v2, /device:TPU:0, one launch (start us, length us, event | category | flops | bytes accessed | tf_op | source)
XLA Modules:
  0.0 239.1 jit_solution(5702808634012350391)
XLA Ops:
  1.7 3.9 %hand_tokens.1 = (bf16[384,3072]{1,0:T(8,128)(2,1)}, f32[8,128]{1,0:T(8,128)S(1)}) custom-call(s32[1]{0:T(128)} %bitcast.16.lead, bf16[384,4096]{1,0:T(8,128)(2,1)} %bitcast.54), custom_call_target="tpu_custom_call" | custom-call | flops 1 | bytes 1 | tf_op jit(solution)/shard_map/hand_tokens/pallas_call | solution.py:134
  6.2 7.4 %collective-permute-start.4 = (bf16[384,3072]{1,0:T(8,128)(2,1)}, bf16[384,3072]{1,0:T(8,128)(2,1)}, u32[]{:S(2)}, u32[]{:S(2)}) collective-permute-start(bf16[384,3072]{1,0:T(8,128)(2,1)} %get-tuple-element.82), channel_id=1, source_target_pairs={{0,2},{1,3},{6,4},{7,5},{8,10},{9,11},{14,12},{15,13},{16,18},{17,... | collective-permute-start | bytes 7077896 | tf_op jit(solution)/shard_map/ppermute | solution.py:440
  13.8 5.4 %sent_part.2 = (bf16[2,256,3072]{2,1,0:T(8,128)(2,1)}, f32[8,128]{1,0:T(8,128)}) custom-call(s32[1]{0:T(128)S(6)} %convert_element_type.16.lead, f32[512,3072]{1,0:T(8,128)} %bitcast.65, bf16[512,3072]{1,0:T(8,128)(2,1)} %bitcast.45, f32[512,3072]{1,0:T(8,128)} %bitcast.68, f32[8,128]{1,0:T(8,128)} %copy-done.22), custom_call_target="tpu_custom_call" | custom-call | flops 1 | bytes 1 | tf_op jit(solution)/shard_map/sent_part/pallas_call | solution.py:366
  20.7 5.3 %sent_part.3 = (bf16[2,256,3072]{2,1,0:T(8,128)(2,1)}, f32[8,128]{1,0:T(8,128)}) custom-call(s32[1]{0:T(128)S(6)} %sub.30.lead, f32[512,3072]{1,0:T(8,128)} %bitcast.66, bf16[512,3072]{1,0:T(8,128)(2,1)} %bitcast.46, f32[512,3072]{1,0:T(8,128)} %bitcast.69, f32[8,128]{1,0:T(8,128)} %get-tuple-element.77.refs_0_), custom_call_target="tpu_custom_call" | custom-call | flops 1 | bytes 1 | tf_op jit(solution)/shard_map/sent_part/pallas_call | solution.py:366
  28.3 2.6 %pack.6 = (bf16[2,512,512]{2,1,0:T(8,128)(2,1)}, f32[8,128]{1,0:T(8,128)S(1)}) custom-call(s32[6]{0:T(128)S(1)} %stack.72.pairs, bf16[512,3072]{1,0:T(8,128)(2,1)} %bitcast.47, bf16[512,3072]{1,0:T(8,128)(2,1)} %collective-permute-done.1.sibling, f32[8,128]{1,0:T(8,128)S(1)} %copy-done.20), custom_call_target="tpu_custom_call" | custom-call | flops 1 | bytes 1 | tf_op jit(solution)/shard_map/pack/pallas_call | solution.py:159
  43.5 4.2 %pack.10 = (bf16[2,512,1536]{2,1,0:T(8,128)(2,1)S(1)}, f32[8,128]{1,0:T(8,128)S(1)}) custom-call(s32[6]{0:T(128)S(1)} %stack.72.pairs, bf16[512,3072]{1,0:T(8,128)(2,1)} %bitcast.49, bf16[512,3072]{1,0:T(8,128)(2,1)} %collective-permute-done.1.sibling, f32[8,128]{1,0:T(8,128)S(1)} %get-tuple-element.85.refs_0_), custom_call_target="tpu_custom_call" | custom-call | flops 1 | bytes 1 | tf_op jit(solution)/shard_map/pack/pallas_call | solution.py:159
  50.0 7.8 %project.12 = (f32[768,1536]{1,0:T(8,128)}, f32[8,128]{1,0:T(8,128)}) custom-call(s32[10]{0:T(128)} %concatenate.50.refs_0_, bf16[384,4096]{1,0:T(8,128)(2,1)} %bitcast.55, bf16[384,4096]{1,0:T(8,128)(2,1)} %copy-done.23, bf16[2,512,1536]{2,1,0:T(8,128)(2,1)} %copy-done.3, f32[8,128]{1,0:T(8,128)} %copy-done.19, ...), custom_call_target="tpu_custom_call" | custom-call | flops 1 | bytes 1 | tf_op jit(solution)/shard_map/project/pallas_call | solution.py:247
  57.9 6.3 %collective-permute-done.4.refs_0_ = bf16[384,3072]{1,0:T(8,128)(2,1)} collective-permute-done((bf16[384,3072]{1,0:T(8,128)(2,1)}, bf16[384,3072]{1,0:T(8,128)(2,1)}, u32[]{:S(2)}, u32[]{:S(2)}) %collective-permute-start.4) | collective-permute-done | bytes 2359328 | tf_op jit(solution)/shard_map/ppermute | solution.py:440
  64.8 20.7 %collective-permute-done.2.refs_2_.refs_0_ = bf16[2,512,512]{2,1,0:T(8,128)(2,1)} collective-permute-done((bf16[2,512,512]{2,1,0:T(8,128)(2,1)}, bf16[2,512,512]{2,1,0:T(8,128)(2,1)}, u32[]{:S(2)}, u32[]{:S(2)}) %collective-permute-start.2) | collective-permute-done | bytes 1048608 | tf_op jit(solution)/shard_map/ppermute | solution.py:440
  87.8 5.3 %collective-permute-start.6 = (bf16[2,512,512]{2,1,0:T(8,128)(2,1)}, bf16[2,512,512]{2,1,0:T(8,128)(2,1)}, u32[]{:S(2)}, u32[]{:S(2)}) collective-permute-start(bf16[2,512,512]{2,1,0:T(8,128)(2,1)} %get-tuple-element.92), channel_id=1, source_target_pairs={{0,2},{1,3},{6,4},{7,5},{8,10},{9,11},{14,12},{15,13},{16,18},{17,... | collective-permute-start | bytes 3145736 | tf_op jit(solution)/shard_map/ppermute | solution.py:440
  93.7 3.9 %broadcast_select_fusion.refs_6_ = bf16[2,256,3072]{2,1,0:T(8,128)(2,1)} fusion(bf16[2,256,3072]{2,1,0:T(8,128)(2,1)} %get-tuple-element.99.refs_4_, bf16[2,256,3072]{2,1,0:T(8,128)(2,1)} %get-tuple-element.98, pred[]{:T(512)} %bitcast.17), kind=kLoop, calls=%fused_computation | loop fusion | flops 1572864 | bytes 9437185 | tf_op jit(solution)/shard_map/jit(_where)/select_n | solution.py:516
  99.7 3.9 %broadcast_select_fusion.1.refs_5_ = bf16[2,256,3072]{2,1,0:T(8,128)(2,1)} fusion(bf16[2,256,3072]{2,1,0:T(8,128)(2,1)} %get-tuple-element.97.refs_5_, bf16[2,256,3072]{2,1,0:T(8,128)(2,1)} %get-tuple-element.96, pred[]{:T(512)} %bitcast.17), kind=kLoop, calls=%fused_computation.1 | loop fusion | flops 1572864 | bytes 9437185 | tf_op jit(solution)/shard_map/jit(_where)/select_n | solution.py:516
  105.1 5.5 %project.13 = (f32[768,1536]{1,0:T(8,128)}, f32[8,128]{1,0:T(8,128)}) custom-call(s32[10]{0:T(128)} %concatenate.50.refs_0_, bf16[384,3072]{1,0:T(8,128)(2,1)} %get-tuple-element.94.refs_1_, bf16[384,3072]{1,0:T(8,128)(2,1)} %copy-done.24, bf16[2,512,1536]{2,1,0:T(8,128)(2,1)} %copy-done.3, f32[8,128]{1,0:T(8,128)} %get-tuple-element.91.refs_1_.refs_4_, ...), custom_call_target="tpu_custom_call" | custom-call | flops 1 | bytes 1 | tf_op jit(solution)/shard_map/project/pallas_call | solution.py:247
  111.4 4.2 %pack.11 = (bf16[2,512,1536]{2,1,0:T(8,128)(2,1)S(1)}, f32[8,128]{1,0:T(8,128)S(1)}) custom-call(s32[6]{0:T(128)S(1)} %stack.72.pairs, bf16[512,3072]{1,0:T(8,128)(2,1)} %get-tuple-element.95.own, bf16[512,3072]{1,0:T(8,128)(2,1)} %collective-permute-done.9.sibling, f32[8,128]{1,0:T(8,128)S(1)} %copy-done.21), custom_call_target="tpu_custom_call" | custom-call | flops 1 | bytes 1 | tf_op jit(solution)/shard_map/pack/pallas_call | solution.py:159
  117.9 7.0 %project.14 = (f32[768,1536]{1,0:T(8,128)}, f32[8,128]{1,0:T(8,128)}) custom-call(s32[10]{0:T(128)} %concatenate.50.refs_0_, bf16[384,3072]{1,0:T(8,128)(2,1)} %get-tuple-element.94.refs_1_, bf16[384,3072]{1,0:T(8,128)(2,1)} %copy-done.24, bf16[2,512,1536]{2,1,0:T(8,128)(2,1)} %copy-done.4, f32[768,1536]{1,0:T(8,128)} %get-tuple-element.102.refs_4_, ...), custom_call_target="tpu_custom_call" | custom-call | flops 1 | bytes 1 | tf_op jit(solution)/shard_map/project/pallas_call | solution.py:247
  126.2 6.9 %collective-permute-start.13 = (bf16[2,512,256]{2,1,0:T(8,128)(2,1)}, bf16[2,512,256]{2,1,0:T(8,128)(2,1)S(1)}, u32[]{:S(2)}, u32[]{:S(2)}) collective-permute-start(bf16[2,512,256]{2,1,0:T(8,128)(2,1)} %get-tuple-element.111), channel_id=1, source_target_pairs={{0,2},{1,3},{6,4},{7,5},{8,10},{9,11},{14,12},{15,13},{16,18},{17,... | collective-permute-start | bytes 1572872 | tf_op jit(solution)/shard_map/ppermute | solution.py:440
  133.1 6.9 %project.15 = (f32[768,1536]{1,0:T(8,128)}, f32[8,128]{1,0:T(8,128)}) custom-call(s32[10]{0:T(128)} %concatenate.50.refs_0_, bf16[384,4096]{1,0:T(8,128)(2,1)} %bitcast.56, bf16[384,4096]{1,0:T(8,128)(2,1)} %copy-done.23, bf16[2,512,1536]{2,1,0:T(8,128)(2,1)} %copy-done.4, f32[768,1536]{1,0:T(8,128)} %get-tuple-element.106.refs_4_, ...), custom_call_target="tpu_custom_call" | custom-call | flops 1 | bytes 1 | tf_op jit(solution)/shard_map/project/pallas_call | solution.py:247
  140.0 3.9 %project.16 = (bf16[768,512]{1,0:T(8,128)(2,1)}, f32[8,128]{1,0:T(8,128)}) custom-call(s32[10]{0:T(128)} %concatenate.50.refs_0_, bf16[384,3072]{1,0:T(8,128)(2,1)} %get-tuple-element.94.refs_1_, bf16[384,3072]{1,0:T(8,128)(2,1)} %copy-done.24, bf16[2,512,512]{2,1,0:T(8,128)(2,1)} %collective-permute-done.7.refs_1_.refs_3_.refs_5_, ...), custom_call_target="tpu_custom_call" | custom-call | flops 1 | bytes 1 | tf_op jit(solution)/shard_map/project/pallas_call | solution.py:247
  143.9 4.9 %project.17 = (f32[768,512]{1,0:T(8,128)}, f32[8,128]{1,0:T(8,128)}) custom-call(s32[10]{0:T(128)} %concatenate.50.refs_0_, bf16[384,4096]{1,0:T(8,128)(2,1)} %bitcast.57, bf16[384,4096]{1,0:T(8,128)(2,1)} %copy-done.23, bf16[384,4096]{1,0:T(8,128)(2,1)} %bitcast.58, bf16[384,4096]{1,0:T(8,128)(2,1)} %copy-done.23, ...), custom_call_target="tpu_custom_call" | custom-call | flops 1 | bytes 1 | tf_op jit(solution)/shard_map/project/pallas_call | solution.py:247
  151.2 6.5 %collective-permute-start.17 = (bf16[2,512,256]{2,1,0:T(8,128)(2,1)}, bf16[2,512,256]{2,1,0:T(8,128)(2,1)S(1)}, u32[]{:S(2)}, u32[]{:S(2)}) collective-permute-start(bf16[2,512,256]{2,1,0:T(8,128)(2,1)} %get-tuple-element.123), channel_id=1, source_target_pairs={{0,2},{1,3},{6,4},{7,5},{8,10},{9,11},{14,12},{15,13},{16,18},{17,... | collective-permute-start | bytes 1572872 | tf_op jit(solution)/shard_map/ppermute | solution.py:440
  159.1 3.8 %project.18 = (bf16[768,512]{1,0:T(8,128)(2,1)}, f32[8,128]{1,0:T(8,128)}) custom-call(s32[10]{0:T(128)} %concatenate.50.refs_0_, bf16[384,3072]{1,0:T(8,128)(2,1)} %get-tuple-element.94.refs_1_, bf16[384,3072]{1,0:T(8,128)(2,1)} %copy-done.24, bf16[2,512,512]{2,1,0:T(8,128)(2,1)} %copy-done.25, f32[768,1536]{1,0:T(8,128)} %get-tuple-element.109.refs_4_, ...), custom_call_target="tpu_custom_call" | custom-call | flops 1 | bytes 1 | tf_op jit(solution)/shard_map/project/pallas_call | solution.py:247
  162.9 5.1 %collective-permute-done.17.refs_0_ = bf16[2,512,256]{2,1,0:T(8,128)(2,1)S(1)} collective-permute-done((bf16[2,512,256]{2,1,0:T(8,128)(2,1)}, bf16[2,512,256]{2,1,0:T(8,128)(2,1)S(1)}, u32[]{:S(2)}, u32[]{:S(2)}) %collective-permute-start.17) | collective-permute-done | bytes 524320 | tf_op jit(solution)/shard_map/ppermute | solution.py:440
  169.3 4.9 %project.19 = (f32[768,512]{1,0:T(8,128)}, f32[8,128]{1,0:T(8,128)}) custom-call(s32[10]{0:T(128)} %concatenate.50.refs_0_, bf16[384,4096]{1,0:T(8,128)(2,1)} %bitcast.59, bf16[384,4096]{1,0:T(8,128)(2,1)} %copy-done.23, bf16[384,4096]{1,0:T(8,128)(2,1)} %bitcast.60, bf16[384,4096]{1,0:T(8,128)(2,1)} %copy-done.23, bf16[2,512,512]{2,1,0:T(8,128)(2,1)} %copy-done.25, ...), custom_call_target="tpu_custom_call" | custom-call | flops 1 | bytes 1 | tf_op jit(solution)/shard_map/project/pallas_call | solution.py:247
  175.9 3.5 %project.20 = (bf16[768,256]{1,0:T(8,128)(2,1)}, f32[8,128]{1,0:T(8,128)}) custom-call(s32[10]{0:T(128)} %concatenate.50.refs_0_, bf16[384,3072]{1,0:T(8,128)(2,1)} %get-tuple-element.94.refs_1_, bf16[384,3072]{1,0:T(8,128)(2,1)} %copy-done.24, bf16[2,512,256]{2,1,0:T(8,128)(2,1)} %copy-done.26, f32[768,1536]{1,0:T(8,128)} %get-tuple-element.109.refs_4_, ...), custom_call_target="tpu_custom_call" | custom-call | flops 1 | bytes 1 | tf_op jit(solution)/shard_map/project/pallas_call | solution.py:247
  183.2 4.0 %project.21 = (f32[768,256]{1,0:T(8,128)}, f32[8,128]{1,0:T(8,128)}) custom-call(s32[10]{0:T(128)} %concatenate.50.refs_0_, bf16[384,4096]{1,0:T(8,128)(2,1)} %bitcast.61, bf16[384,4096]{1,0:T(8,128)(2,1)} %copy-done.23, bf16[384,4096]{1,0:T(8,128)(2,1)} %bitcast.62, bf16[384,4096]{1,0:T(8,128)(2,1)} %copy-done.23, bf16[2,512,256]{2,1,0:T(8,128)(2,1)} %copy-done.26, ...), custom_call_target="tpu_custom_call" | custom-call | flops 1 | bytes 1 | tf_op jit(solution)/shard_map/project/pallas_call | solution.py:247
  187.2 3.4 %project.22 = (bf16[768,256]{1,0:T(8,128)(2,1)}, f32[8,128]{1,0:T(8,128)}) custom-call(s32[10]{0:T(128)} %concatenate.50.refs_0_, bf16[384,3072]{1,0:T(8,128)(2,1)} %get-tuple-element.94.refs_1_, bf16[384,3072]{1,0:T(8,128)(2,1)} %copy-done.24, bf16[2,512,256]{2,1,0:T(8,128)(2,1)} %collective-permute-done.18.refs_3_.refs_5_, ...), custom_call_target="tpu_custom_call" | custom-call | flops 1 | bytes 1 | tf_op jit(solution)/shard_map/project/pallas_call | solution.py:247
  192.1 4.9 %collective-permute-done.14.refs_1_ = bf16[768,512]{1,0:T(8,128)(2,1)S(1)} collective-permute-done((bf16[768,512]{1,0:T(8,128)(2,1)}, bf16[768,512]{1,0:T(8,128)(2,1)S(1)}, u32[]{:S(2)}, u32[]{:S(2)}) %collective-permute-start.14) | collective-permute-done | bytes 786464 | tf_op jit(solution)/shard_map/ppermute | solution.py:440
  197.7 6.9 %attend_chunk.3 = (bf16[384,512]{1,0:T(8,128)(2,1)S(1)}, bf16[384,512]{1,0:T(8,128)(2,1)}, f32[8,128]{1,0:T(8,128)S(1)}) custom-call(f32[768,512]{1,0:T(8,128)S(1)} %copy-done.5, bf16[768,512]{1,0:T(8,128)(2,1)S(1)} %collective-permute-done.14.refs_1_, f32[2,384,128]{2,1,0:T(8,128)S(1)} %copy-done.1, f32[2,384,128]{2,1,0:T(8,128)S(1)} %copy-done.2, ...), custom_call_target="tpu_custom_call" | custom-call | flops 1 | bytes 1 | tf_op jit(solution)/shard_map/attend_chunk/pallas_call | solution.py:340
  205.9 4.1 %project.23 = (f32[768,256]{1,0:T(8,128)}, f32[8,128]{1,0:T(8,128)}) custom-call(s32[10]{0:T(128)} %concatenate.50.refs_0_, bf16[384,4096]{1,0:T(8,128)(2,1)} %bitcast.63, bf16[384,4096]{1,0:T(8,128)(2,1)} %copy-done.23, bf16[384,4096]{1,0:T(8,128)(2,1)} %bitcast.64, bf16[384,4096]{1,0:T(8,128)(2,1)} %copy-done.23, ...), custom_call_target="tpu_custom_call" | custom-call | flops 1 | bytes 1 | tf_op jit(solution)/shard_map/project/pallas_call | solution.py:247
  210.8 4.4 %attend_chunk.4 = (bf16[384,256]{1,0:T(8,128)(2,1)S(1)}, bf16[384,256]{1,0:T(8,128)(2,1)S(1)}, f32[8,128]{1,0:T(8,128)S(1)}) custom-call(f32[768,256]{1,0:T(8,128)S(1)} %copy-done.8, bf16[768,256]{1,0:T(8,128)(2,1)} %collective-permute-done.19.refs_1_, f32[2,384,128]{2,1,0:T(8,128)S(1)} %copy-done.1, f32[2,384,128]{2,1,0:T(8,128)S(1)} %copy-done.2, ...), custom_call_target="tpu_custom_call" | custom-call | flops 1 | bytes 1 | tf_op jit(solution)/shard_map/attend_chunk/pallas_call | solution.py:340
  215.7 3.3 %attend_chunk.5 = (bf16[384,256]{1,0:T(8,128)(2,1)S(1)}, bf16[384,256]{1,0:T(8,128)(2,1)S(1)}, f32[8,128]{1,0:T(8,128)S(1)}) custom-call(f32[768,256]{1,0:T(8,128)S(1)} %copy-done.9, bf16[768,256]{1,0:T(8,128)(2,1)S(1)} %collective-permute-done.22.refs_1_, f32[2,384,128]{2,1,0:T(8,128)S(1)} %copy-done.1, f32[2,384,128]{2,1,0:T(8,128)S(1)} %copy-done.2, ...), custom_call_target="tpu_custom_call" | custom-call | flops 1 | bytes 1 | tf_op jit(solution)/shard_map/attend_chunk/pallas_call | solution.py:340
  219.7 15.6 %outer_update.1 = (f32[512,3072]{1,0:T(8,128)}, f32[512,3072]{1,0:T(8,128)}, f32[8,128]{1,0:T(8,128)}) custom-call(s32[2]{0:T(128)} %pad_add_fusion.1.refs_0_, f32[512,3072]{1,0:T(8,128)} %bitcast.67, bf16[512,3072]{1,0:T(8,128)(2,1)} %bitcast.50, f32[512,3072]{1,0:T(8,128)} %bitcast.70, bf16[2,256,3072]{2,1,0:T(8,128)(2,1)} %get-tuple-element.99.refs_4_, ...), custom_call_target="tpu_custom_call" | custom-call | flops 1 | bytes 1 | tf_op jit(solution)/shard_map/outer_update/pallas_call | solution.py:414
  (142 shorter events, 51.1 us)
Async XLA Ops:
  0.6 25.4 %collective-permute-start.1 = (bf16[512,3072]{1,0:T(8,128)(2,1)}, bf16[512,3072]{1,0:T(8,128)(2,1)}, u32[]{:S(2)}, u32[]{:S(2)}) collective-permute-start(bf16[512,3072]{1,0:T(8,128)(2,1)} %bitcast.43), channel_id=1, source_target_pairs={{0,1},{1,0},{2,3},{3,2},{4,5},{5,4},{6,7},{7,6},{8,9},{9,8},{10,11... | collective-permute-start | bytes 9437192 | tf_op jit(solution)/shard_map/ppermute | solution.py:440
  1.1 29.8 %collective-permute-start = (bf16[384,4096]{1,0:T(8,128)(2,1)}, bf16[384,4096]{1,0:T(8,128)(2,1)S(1)}, u32[]{:S(2)}, u32[]{:S(2)}) collective-permute-start(bf16[384,4096]{1,0:T(8,128)(2,1)} %bitcast.53), channel_id=1, source_target_pairs={{0,1},{1,0},{2,3},{3,2},{4,5},{5,4},{6,7},{7,6},{8,9},{9,8},{10,11... | collective-permute-start | bytes 9437192 | tf_op jit(solution)/shard_map/ppermute | solution.py:440
  1.2 63.5 %collective-permute-start.3 = (bf16[512,3072]{1,0:T(8,128)(2,1)}, bf16[512,3072]{1,0:T(8,128)(2,1)}, u32[]{:S(2)}, u32[]{:S(2)}) collective-permute-start(bf16[512,3072]{1,0:T(8,128)(2,1)} %bitcast.44), channel_id=1, source_target_pairs={{2,4},{3,5},{4,2},{5,3},{0,1},{1,0},{6,7},{7,6},{10,12},{11,13},{1... | collective-permute-start | bytes 9437192 | tf_op jit(solution)/shard_map/ppermute | solution.py:440
  1.7 12.0 %copy-start.29 = (s32[1,384]{1,0:T(1,128)S(1)}, s32[1,384]{1,0:T(1,128)}, u32[]{:S(2)}) copy-start(s32[1,384]{1,0:T(1,128)} %param.7) | copy-start | bytes 4612
  1.7 12.1 %copy-start.30 = (s32[4]{0:T(128)S(1)}, s32[4]{0:T(128)}, u32[]{:S(2)}) copy-start(s32[4]{0:T(128)} %param.8) | copy-start | bytes 52
  6.2 58.0 %collective-permute-start.4 = (bf16[384,3072]{1,0:T(8,128)(2,1)}, bf16[384,3072]{1,0:T(8,128)(2,1)}, u32[]{:S(2)}, u32[]{:S(2)}) collective-permute-start(bf16[384,3072]{1,0:T(8,128)(2,1)} %get-tuple-element.82), channel_id=1, source_target_pairs={{0,2},{1,3},{6,4},{7,5},{8,10},{9,11},{14,12},{15,13},{16,18},{17,... | collective-permute-start | bytes 7077896 | tf_op jit(solution)/shard_map/ppermute | solution.py:440
  13.6 5.5 %collective-permute-start.5 = (s32[384]{0:T(512)S(1)}, s32[384]{0:T(512)S(1)}, u32[]{:S(2)}, u32[]{:S(2)}) collective-permute-start(s32[384]{0:T(512)S(1)} %reduce), channel_id=1, source_target_pairs={{0,1},{1,0},{2,3},{3,2},{4,5},{5,4},{6,7},{7,6},{8,9},{9,8},{10,11... | collective-permute-start | bytes 4616 | tf_op jit(solution)/shard_map/ppermute | solution.py:440
  19.1 74.0 %collective-permute-start.11 = (bf16[2,256,3072]{2,1,0:T(8,128)(2,1)}, bf16[2,256,3072]{2,1,0:T(8,128)(2,1)}, u32[]{:S(2)}, u32[]{:S(2)}) collective-permute-start(bf16[2,256,3072]{2,1,0:T(8,128)(2,1)} %get-tuple-element.98), channel_id=1, source_target_pairs={{0,8},{8,0},{16,24},{24,16},{1,9},{9,1},{17,25},{25,17},{2,10},{10... | collective-permute-start | bytes 9437192 | tf_op jit(solution)/shard_map/ppermute | solution.py:465
  26.0 71.6 %collective-permute-start.10 = (bf16[2,256,3072]{2,1,0:T(8,128)(2,1)}, bf16[2,256,3072]{2,1,0:T(8,128)(2,1)}, u32[]{:S(2)}, u32[]{:S(2)}) collective-permute-start(bf16[2,256,3072]{2,1,0:T(8,128)(2,1)} %get-tuple-element.96), channel_id=1, source_target_pairs={{0,16},{8,24},{16,0},{24,8},{1,17},{9,25},{17,1},{25,9},{2,18},{10... | collective-permute-start | bytes 9437192 | tf_op jit(solution)/shard_map/ppermute | solution.py:465
  30.9 54.5 %collective-permute-start.2 = (bf16[2,512,512]{2,1,0:T(8,128)(2,1)}, bf16[2,512,512]{2,1,0:T(8,128)(2,1)}, u32[]{:S(2)}, u32[]{:S(2)}) collective-permute-start(bf16[2,512,512]{2,1,0:T(8,128)(2,1)} %get-tuple-element.81), channel_id=1, source_target_pairs={{0,2},{1,3},{6,4},{7,5},{8,10},{9,11},{14,12},{15,13},{16,18},{17,... | collective-permute-start | bytes 3145736 | tf_op jit(solution)/shard_map/ppermute | solution.py:440
  86.1 24.6 %collective-permute-start.9 = (bf16[512,3072]{1,0:T(8,128)(2,1)}, bf16[512,3072]{1,0:T(8,128)(2,1)}, u32[]{:S(2)}, u32[]{:S(2)}) collective-permute-start(bf16[512,3072]{1,0:T(8,128)(2,1)} %get-tuple-element.95.own), channel_id=1, source_target_pairs={{0,1},{1,0},{2,3},{3,2},{4,5},{5,4},{6,7},{7,6},{8,9},{9,8},{10,11... | collective-permute-start | bytes 9437192 | tf_op jit(solution)/shard_map/ppermute | solution.py:440
  86.1 17.6 %collective-permute-start.8 = (bf16[384,3072]{1,0:T(8,128)(2,1)}, bf16[384,3072]{1,0:T(8,128)(2,1)S(1)}, u32[]{:S(2)}, u32[]{:S(2)}) collective-permute-start(bf16[384,3072]{1,0:T(8,128)(2,1)} %get-tuple-element.94.refs_1_), channel_id=1, source_target_pairs={{0,1},{1,0},{2,3},{3,2},{4,5},{5,4},{6,7},{7,6},{8,9},{9,8},{10,11... | collective-permute-start | bytes 7077896 | tf_op jit(solution)/shard_map/ppermute | solution.py:440
  87.8 37.1 %collective-permute-start.6 = (bf16[2,512,512]{2,1,0:T(8,128)(2,1)}, bf16[2,512,512]{2,1,0:T(8,128)(2,1)}, u32[]{:S(2)}, u32[]{:S(2)}) collective-permute-start(bf16[2,512,512]{2,1,0:T(8,128)(2,1)} %get-tuple-element.92), channel_id=1, source_target_pairs={{0,2},{1,3},{6,4},{7,5},{8,10},{9,11},{14,12},{15,13},{16,18},{17,... | collective-permute-start | bytes 3145736 | tf_op jit(solution)/shard_map/ppermute | solution.py:440
  93.1 31.7 %collective-permute-start.7 = (bf16[2,512,512]{2,1,0:T(8,128)(2,1)}, bf16[2,512,512]{2,1,0:T(8,128)(2,1)}, u32[]{:S(2)}, u32[]{:S(2)}) collective-permute-start(bf16[2,512,512]{2,1,0:T(8,128)(2,1)} %get-tuple-element.93.refs_6_), channel_id=1, source_target_pairs={{2,4},{3,5},{4,2},{5,3},{0,1},{1,0},{6,7},{7,6},{10,12},{11,13},{1... | collective-permute-start | bytes 3145736 | tf_op jit(solution)/shard_map/ppermute | solution.py:440
  97.6 108.3 %collective-permute-start.21 = (bf16[2,256,3072]{2,1,0:T(8,128)(2,1)}, bf16[2,256,3072]{2,1,0:T(8,128)(2,1)}, u32[]{:S(2)}, u32[]{:S(2)}) collective-permute-start(bf16[2,256,3072]{2,1,0:T(8,128)(2,1)} %broadcast_select_fusion.refs_6_), channel_id=1, source_target_pairs={{0,16},{8,24},{16,0},{24,8},{1,17},{9,25},{17,1},{25,9},{2,18},{10... | collective-permute-start | bytes 9437192 | tf_op jit(solution)/shard_map/ppermute | solution.py:517
  103.6 102.3 %collective-permute-start.20 = (bf16[2,256,3072]{2,1,0:T(8,128)(2,1)}, bf16[2,256,3072]{2,1,0:T(8,128)(2,1)}, u32[]{:S(2)}, u32[]{:S(2)}) collective-permute-start(bf16[2,256,3072]{2,1,0:T(8,128)(2,1)} %broadcast_select_fusion.1.refs_5_), channel_id=1, source_target_pairs={{0,8},{8,0},{16,24},{24,16},{1,9},{9,1},{17,25},{25,17},{2,10},{10... | collective-permute-start | bytes 9437192 | tf_op jit(solution)/shard_map/ppermute | solution.py:517
  125.5 23.4 %collective-permute-start.12 = (bf16[2,512,512]{2,1,0:T(8,128)(2,1)}, bf16[2,512,512]{2,1,0:T(8,128)(2,1)S(1)}, u32[]{:S(2)}, u32[]{:S(2)}) collective-permute-start(bf16[2,512,512]{2,1,0:T(8,128)(2,1)} %get-tuple-element.105.refs_6_), channel_id=1, source_target_pairs={{2,4},{3,5},{4,2},{5,3},{0,1},{1,0},{6,7},{7,6},{10,12},{11,13},{1... | collective-permute-start | bytes 3145736 | tf_op jit(solution)/shard_map/ppermute | solution.py:440
  126.2 22.7 %collective-permute-start.13 = (bf16[2,512,256]{2,1,0:T(8,128)(2,1)}, bf16[2,512,256]{2,1,0:T(8,128)(2,1)S(1)}, u32[]{:S(2)}, u32[]{:S(2)}) collective-permute-start(bf16[2,512,256]{2,1,0:T(8,128)(2,1)} %get-tuple-element.111), channel_id=1, source_target_pairs={{0,2},{1,3},{6,4},{7,5},{8,10},{9,11},{14,12},{15,13},{16,18},{17,... | collective-permute-start | bytes 1572872 | tf_op jit(solution)/shard_map/ppermute | solution.py:440
  151.2 16.9 %collective-permute-start.17 = (bf16[2,512,256]{2,1,0:T(8,128)(2,1)}, bf16[2,512,256]{2,1,0:T(8,128)(2,1)S(1)}, u32[]{:S(2)}, u32[]{:S(2)}) collective-permute-start(bf16[2,512,256]{2,1,0:T(8,128)(2,1)} %get-tuple-element.123), channel_id=1, source_target_pairs={{0,2},{1,3},{6,4},{7,5},{8,10},{9,11},{14,12},{15,13},{16,18},{17,... | collective-permute-start | bytes 1572872 | tf_op jit(solution)/shard_map/ppermute | solution.py:440
  157.7 16.6 %collective-permute-start.16 = (bf16[2,512,256]{2,1,0:T(8,128)(2,1)}, bf16[2,512,256]{2,1,0:T(8,128)(2,1)S(1)}, u32[]{:S(2)}, u32[]{:S(2)}) collective-permute-start(bf16[2,512,256]{2,1,0:T(8,128)(2,1)} %get-tuple-element.121.refs_6_), channel_id=1, source_target_pairs={{2,4},{3,5},{4,2},{5,3},{0,1},{1,0},{6,7},{7,6},{10,12},{11,13},{1... | collective-permute-start | bytes 1572872 | tf_op jit(solution)/shard_map/ppermute | solution.py:440
  157.8 22.4 %collective-permute-start.15 = (bf16[768,512]{1,0:T(8,128)(2,1)}, bf16[768,512]{1,0:T(8,128)(2,1)S(1)}, u32[]{:S(2)}, u32[]{:S(2)}) collective-permute-start(bf16[768,512]{1,0:T(8,128)(2,1)} %get-tuple-element.120), channel_id=1, source_target_pairs={{2,0},{3,1},{4,6},{5,7},{10,8},{11,9},{12,14},{13,15},{18,16},{19,... | collective-permute-start | bytes 2359304 | tf_op jit(solution)/shard_map/ppermute | solution.py:440
  168.1 6.2 %copy-start.28 = (bf16[2,512,256]{2,1,0:T(8,128)(2,1)}, bf16[2,512,256]{2,1,0:T(8,128)(2,1)S(1)}, u32[]{:S(2)}) copy-start(bf16[2,512,256]{2,1,0:T(8,128)(2,1)S(1)} %collective-permute-done.17.refs_0_) | copy-start | bytes 1572868
  168.1 29.0 %collective-permute-start.14 = (bf16[768,512]{1,0:T(8,128)(2,1)}, bf16[768,512]{1,0:T(8,128)(2,1)S(1)}, u32[]{:S(2)}, u32[]{:S(2)}) collective-permute-start(bf16[768,512]{1,0:T(8,128)(2,1)} %get-tuple-element.118), channel_id=1, source_target_pairs={{2,0},{3,1},{4,6},{5,7},{10,8},{11,9},{12,14},{13,15},{18,16},{19,... | collective-permute-start | bytes 2359304 | tf_op jit(solution)/shard_map/ppermute | solution.py:440
  175.7 11.5 %collective-permute-start.18 = (bf16[2,512,256]{2,1,0:T(8,128)(2,1)}, bf16[2,512,256]{2,1,0:T(8,128)(2,1)}, u32[]{:S(2)}, u32[]{:S(2)}) collective-permute-start(bf16[2,512,256]{2,1,0:T(8,128)(2,1)} %get-tuple-element.129.refs_6_), channel_id=1, source_target_pairs={{2,4},{3,5},{4,2},{5,3},{0,1},{1,0},{6,7},{7,6},{10,12},{11,13},{1... | collective-permute-start | bytes 1572872 | tf_op jit(solution)/shard_map/ppermute | solution.py:440
  175.9 5.6 %copy-start.1 = (f32[2,384,128]{2,1,0:T(8,128)S(1)}, f32[2,384,128]{2,1,0:T(8,128)}, u32[]{:S(2)}) copy-start(f32[2,384,128]{2,1,0:T(8,128)} %get-tuple-element.160.refs_5_.cosine.refs_2_) | copy-start | bytes 1179652
  175.9 5.6 %copy-start.2 = (f32[2,384,128]{2,1,0:T(8,128)S(1)}, f32[2,384,128]{2,1,0:T(8,128)}, u32[]{:S(2)}) copy-start(f32[2,384,128]{2,1,0:T(8,128)} %get-tuple-element.161.refs_6_.sine.refs_3_) | copy-start | bytes 1179652
  180.2 29.9 %collective-permute-start.19 = (bf16[768,256]{1,0:T(8,128)(2,1)}, bf16[768,256]{1,0:T(8,128)(2,1)}, u32[]{:S(2)}, u32[]{:S(2)}) collective-permute-start(bf16[768,256]{1,0:T(8,128)(2,1)} %get-tuple-element.135), channel_id=1, source_target_pairs={{2,0},{3,1},{4,6},{5,7},{10,8},{11,9},{12,14},{13,15},{18,16},{19,... | collective-permute-start | bytes 1179656 | tf_op jit(solution)/shard_map/ppermute | solution.py:440
  187.2 9.8 %copy-start.5 = (f32[768,512]{1,0:T(8,128)S(1)}, f32[768,512]{1,0:T(8,128)}, u32[]{:S(2)}) copy-start(f32[768,512]{1,0:T(8,128)} %get-tuple-element.117.refs_0_) | copy-start | bytes 4718596
  190.6 25.1 %collective-permute-start.22 = (bf16[768,256]{1,0:T(8,128)(2,1)}, bf16[768,256]{1,0:T(8,128)(2,1)S(1)}, u32[]{:S(2)}, u32[]{:S(2)}) collective-permute-start(bf16[768,256]{1,0:T(8,128)(2,1)} %get-tuple-element.140), channel_id=1, source_target_pairs={{2,0},{3,1},{4,6},{5,7},{10,8},{11,9},{12,14},{13,15},{18,16},{19,... | collective-permute-start | bytes 1179656 | tf_op jit(solution)/shard_map/ppermute | solution.py:440
  205.2 30.1 %collective-permute-start.23 = (bf16[384,512]{1,0:T(8,128)(2,1)}, bf16[384,512]{1,0:T(8,128)(2,1)}, u32[]{:S(2)}, u32[]{:S(2)}) collective-permute-start(bf16[384,512]{1,0:T(8,128)(2,1)} %get-tuple-element.143), channel_id=1, source_target_pairs={{0,1},{1,0},{2,3},{3,2},{4,5},{5,4},{6,7},{7,6},{8,9},{9,8},{10,11... | collective-permute-start | bytes 1179656 | tf_op jit(solution)/shard_map/ppermute | solution.py:440
  215.2 21.2 %collective-permute-start.24 = (bf16[384,256]{1,0:T(8,128)(2,1)S(1)}, bf16[384,256]{1,0:T(8,128)(2,1)S(1)}, u32[]{:S(2)}, u32[]{:S(2)}) collective-permute-start(bf16[384,256]{1,0:T(8,128)(2,1)S(1)} %get-tuple-element.144), channel_id=1, source_target_pairs={{0,1},{1,0},{2,3},{3,2},{4,5},{5,4},{6,7},{7,6},{8,9},{9,8},{10,11... | collective-permute-start | bytes 589832 | tf_op jit(solution)/shard_map/ppermute | solution.py:440
  219.7 16.8 %collective-permute-start.25 = (bf16[384,256]{1,0:T(8,128)(2,1)S(1)}, bf16[384,256]{1,0:T(8,128)(2,1)S(1)}, u32[]{:S(2)}, u32[]{:S(2)}) collective-permute-start(bf16[384,256]{1,0:T(8,128)(2,1)S(1)} %get-tuple-element.145), channel_id=1, source_target_pairs={{0,1},{1,0},{2,3},{3,2},{4,5},{5,4},{6,7},{7,6},{8,9},{9,8},{10,11... | collective-permute-start | bytes 589832 | tf_op jit(solution)/shard_map/ppermute | solution.py:440
  (25 other events, 40.5 us)

commit v3 on v1

--- a/solution.py
+++ b/solution.py
@@ -1,6 +1,8 @@
 import jax
 import jax.numpy as jnp
 from jax import lax
+from jax.experimental import pallas as pl
+from jax.experimental.pallas import tpu as pltpu
 from jax.sharding import PartitionSpec as P
 
 D = 4096
@@ -53,28 +55,6 @@
     return context.reshape(count, width_q).astype(jnp.bfloat16)
 
 
-def pairings(count):
-    if count == 0:
-        return [{}]
-    found = []
-
-    def extend(left, pairs):
-        if not left:
-            found.append(dict(pairs))
-            return
-        first = left[0]
-        for mate in left[1:]:
-            rest = [r for r in left if r not in (first, mate)]
-            extend(rest, pairs + [(first, mate), (mate, first)])
-
-    extend(list(range(count)), [])
-    return found
-
-
-def send_to_mate(values, pairs):
-    return [lax.ppermute(value, "replica", sorted(pairs.items())) for value in values]
-
-
 def exchange_any(values, partner, count):
     me = lax.axis_index("replica")
     received = [jnp.zeros_like(value) for value in values]
@@ -115,6 +95,673 @@
     return attend(projected, places)[None]
 
 
+LINE = 4
+CORES = 2
+SQUARE = 4
+UNIT = HEAD_DIM
+GROUP = HEADS // KV_HEADS
+HALF_GROUPS = KV_HEADS // CORES
+CHUNKS = (("k0", "k1", "v0", "v1"), ("q0",) * GROUP, ("q1",) * 2, ("q1",) * 2)
+FIRST_UNIT = tuple(sum(len(c) for c in CHUNKS[:j]) for j in range(len(CHUNKS)))
+HALF_UNITS = sum(len(c) for c in CHUNKS)
+PAIR = 2 * UNIT
+MIB = 1024 * 1024
+SMALL = pl.CostEstimate(flops=1, bytes_accessed=1, transcendentals=0)
+HBM = pl.BlockSpec(memory_space=pltpu.HBM)
+SMEM = pl.BlockSpec(memory_space=pltpu.SMEM)
+VMEM = pl.BlockSpec(memory_space=pltpu.VMEM)
+MARK = jax.ShapeDtypeStruct((8, 128), jnp.float32)
+
+
+def pairs_of_half(half):
+    per_half = HEADS // CORES // 2
+    pairs = [HEADS // 2 + half, (HEADS + KV_HEADS) // 2 + half]
+    pairs += [half * per_half + at for at in range(per_half)]
+    return jnp.stack([jnp.asarray(pair, jnp.int32) for pair in pairs])
+
+
+def pass_on(pieces, sem):
+    count = len(pieces)
+    inward = [
+        pltpu.make_async_copy(source, stop, sem.at[at])
+        for at, (source, stop, _) in enumerate(pieces)
+    ]
+    onward = [
+        pltpu.make_async_copy(stop, target, sem.at[count + at])
+        for at, (_, stop, target) in enumerate(pieces)
+    ]
+    for copy in inward:
+        copy.start()
+    for at in range(count):
+        inward[at].wait()
+        onward[at].start()
+    for copy in onward:
+        copy.wait()
+
+
+def hand_kernel(lead, tokens, out, mark, held, sem):
+    mark[...] = jnp.zeros_like(mark)
+    block = tokens.shape[1] // LINE
+    pieces = []
+    for at in range(LINE - 1):
+        source = pl.multiple_of((lead[0] + at) * block, block)
+        here = slice(at * block, (at + 1) * block)
+        pieces.append((tokens.at[:, pl.ds(source, block)], held.at[:, here], out.at[:, here]))
+    pass_on(pieces, sem)
+
+
+def hand_tokens(tokens, lead):
+    rows, columns = tokens.shape
+    size = (rows, columns // LINE * (LINE - 1))
+    return pl.pallas_call(
+        hand_kernel,
+        in_specs=[SMEM, HBM],
+        out_specs=(HBM, VMEM),
+        out_shape=(jax.ShapeDtypeStruct(size, tokens.dtype), MARK),
+        scratch_shapes=[
+            pltpu.VMEM(size, tokens.dtype),
+            pltpu.SemaphoreType.DMA((2 * (LINE - 1),)),
+        ],
+        compiler_params=pltpu.CompilerParams(vmem_limit_bytes=60 * MIB),
+        cost_estimate=SMALL,
+        name="hand_tokens",
+    )(lead, tokens)
+
+
+def pack_kernel(first, count, pairs, own, sibling, *refs):
+    out, mark, held, sem = refs[-4:]
+    mark[...] = jnp.zeros_like(mark)
+    pieces = []
+    for at in range(count):
+        source = pl.multiple_of(pairs[first + at] * PAIR, PAIR)
+        for k, rows in enumerate((own, sibling)):
+            here = slice(at * PAIR, (at + 1) * PAIR)
+            pieces.append((rows.at[:, pl.ds(source, PAIR)], held.at[k, :, here], out.at[k, :, here]))
+    pass_on(pieces, sem)
+
+
+def pack(first, count, own, sibling, pairs, after=()):
+    size = (CORES, own.shape[0], count * PAIR)
+    return pl.pallas_call(
+        lambda *refs: pack_kernel(first, count, *refs),
+        in_specs=[SMEM] + [HBM] * (2 + len(after)),
+        out_specs=(HBM, VMEM),
+        out_shape=(jax.ShapeDtypeStruct(size, own.dtype), MARK),
+        scratch_shapes=[
+            pltpu.VMEM(size, own.dtype),
+            pltpu.SemaphoreType.DMA((2 * CORES * count,)),
+        ],
+        compiler_params=pltpu.CompilerParams(vmem_limit_bytes=60 * MIB),
+        cost_estimate=SMALL,
+        name="pack",
+    )(pairs, own, sibling, *after)
+
+
+def touch(value, *after):
+    def kernel(*refs):
+        refs[-1][...] = jnp.zeros_like(refs[-1])
+
+    return pl.pallas_call(
+        kernel,
+        in_specs=[HBM] * (1 + len(after)),
+        out_specs=(HBM, VMEM),
+        out_shape=(jax.ShapeDtypeStruct(value.shape, value.dtype), MARK),
+        input_output_aliases={0: 0},
+        compiler_params=pltpu.CompilerParams(vmem_limit_bytes=60 * MIB),
+        cost_estimate=SMALL,
+        name="touch",
+    )(value, *after)
+
+
+def project_kernel(span, wide, parts, groups, slot, handed, riding, table, pairs, *refs):
+    first_unit, width = span
+    tokens, refs = refs[:CORES], refs[CORES:]
+    sources = refs[: wide * CORES + (groups - wide) * parts]
+    rider = refs[len(sources)] if riding else None
+    out, mark, taken, held, total, sem = refs[-6:]
+    mark[...] = jnp.zeros_like(mark)
+    rows, depth = tokens[0].shape[0], held.shape[2]
+    core, middle = table[0], table[1] == 1
+    if out.dtype == jnp.float32:
+        total = out
+
+    def copies(group):
+        found = []
+        place = pl.multiple_of(table[slot + group] * CORES * depth, CORES * depth)
+        for half in range(CORES):
+            found.append(
+                (
+                    tokens[half].at[:, pl.ds(place, CORES * depth)],
+                    taken.at[group, half * rows : (half + 1) * rows],
+                )
+            )
+        for k in range(CORES):
+            if group < wide:
+                source = sources[group * CORES + k]
+                for pair in range(width // 2):
+                    column = pl.multiple_of(pairs[first_unit // 2 + pair] * PAIR, PAIR)
+                    found.append(
+                        (
+                            source.at[:, pl.ds(column, PAIR)],
+                            held.at[group, k, :, pair * PAIR : (pair + 1) * PAIR],
+                        )
+                    )
+            else:
+                left = 0
+                for part in range(parts):
+                    source = sources[wide * CORES + (group - wide) * parts + part]
+                    here = slice(left, left + source.shape[2])
+                    found.append((source.at[k], held.at[group, k, :, here]))
+                    left += source.shape[2]
+        return [
+            pltpu.make_async_copy(*ends, sem.at[group, number]) for number, ends in enumerate(found)
+        ]
+
+    def start(group):
+        for copy in copies(group):
+            copy.start()
+
+    def multiply(group):
+        for copy in copies(group):
+            copy.wait()
+        value = None if group == 0 else total[...]
+        for k in range(CORES):
+            columns = pl.ds(pl.multiple_of((core + k) % CORES * depth, depth), depth)
+            part = jnp.dot(
+                taken[group, :, columns], held[group, k], preferred_element_type=jnp.float32
+            )
+            value = part if value is None else value + part
+        if group == groups - 1:
+            out[...] = value.astype(out.dtype)
+        else:
+            total[...] = value
+
+    def every_group(run):
+        if not handed:
+            run(0)
+
+        @pl.when(middle)
+        def _():
+            for group in range(0 if handed else 1, groups):
+                run(group)
+
+    if handed:
+
+        @pl.when(jnp.logical_not(middle))
+        def _():
+            out[...] = jnp.zeros_like(out)
+            if riding:
+                load = pltpu.make_async_copy(rider, held.at[0, :, :, : rider.shape[2]], sem.at[0, 0])
+                load.start()
+                load.wait()
+                for k in range(CORES):
+                    left = k * rider.shape[2]
+                    out[:depth, left : left + rider.shape[2]] = held[0, k, :, : rider.shape[2]]
+
+    every_group(start)
+    every_group(multiply)
+
+
+def project(chunks, table, pairs, tokens, slot, wide, packed, dtype, after=(), rider=None):
+    width = sum(len(CHUNKS[chunk]) for chunk in chunks)
+    span = (FIRST_UNIT[chunks[0]], width)
+    rows, depth = tokens[0].shape[0], packed[0][0].shape[1]
+    groups = len(wide) + len(packed)
+    sources = [half for both in wide for half in both]
+    sources += [part for parts in packed for part in parts]
+    sources += [] if rider is None else [rider]
+    size = (CORES * rows, width * UNIT)
+    handed = dtype != jnp.float32
+    return pl.pallas_call(
+        lambda *refs: project_kernel(
+            span, len(wide), len(chunks), groups, slot, handed, rider is not None, *refs
+        ),
+        in_specs=[SMEM] * 2 + [HBM] * (CORES + len(sources) + len(after)),
+        out_specs=(VMEM, VMEM),
+        out_shape=(jax.ShapeDtypeStruct(size, dtype), MARK),
+        scratch_shapes=[
+            pltpu.VMEM((groups, CORES * rows, CORES * depth), tokens[0].dtype),
+            pltpu.VMEM((groups, CORES, depth, width * UNIT), tokens[0].dtype),
+            pltpu.VMEM(size if handed else (8, 128), jnp.float32),
+            pltpu.SemaphoreType.DMA((groups, CORES * (1 + width // 2))),
+        ],
+        compiler_params=pltpu.CompilerParams(vmem_limit_bytes=60 * MIB),
+        cost_estimate=SMALL,
+        name="project",
+    )(table, pairs, *tokens, *sources, *after)
+
+
+def whole_spec(array):
+    return pl.BlockSpec(array.shape, lambda i: (0,) * len(array.shape))
+
+
+def unpack_kernel(came, *refs):
+    out, mark, held, sem = refs[-4:]
+    mark[...] = jnp.zeros_like(mark)
+    depth, width = out.shape[1:]
+    pass_on(
+        [
+            (came.at[:depth, k * width : (k + 1) * width], held.at[k], out.at[k])
+            for k in range(CORES)
+        ],
+        sem,
+    )
+
+
+def unpack(came, depth, after=()):
+    size = (CORES, depth, came.shape[1] // CORES)
+    return pl.pallas_call(
+        unpack_kernel,
+        in_specs=[HBM] * (1 + len(after)),
+        out_specs=(HBM, VMEM),
+        out_shape=(jax.ShapeDtypeStruct(size, came.dtype), MARK),
+        scratch_shapes=[
+            pltpu.VMEM(size, came.dtype),
+            pltpu.SemaphoreType.DMA((2 * CORES,)),
+        ],
+        compiler_params=pltpu.CompilerParams(vmem_limit_bytes=60 * MIB),
+        cost_estimate=SMALL,
+        name="unpack",
+    )(came, *after)
+
+
+def joined_rows(own, came, rows, unit):
+    columns = slice(unit * UNIT, (unit + 1) * UNIT)
+    each = came[0].shape[1] // UNIT
+    there = slice(unit % each * UNIT, (unit % each + 1) * UNIT)
+    rest = came[unit // each][rows, there]
+    return (own[rows, columns] + rest.astype(jnp.float32)) * D ** (-0.5)
+
+
+def turned(value, cosine, sine):
+    return (value * cosine + pltpu.roll(value, HEAD_DIM // 2, 1) * sine).astype(jnp.bfloat16)
+
+
+def kept_rows(total, rows, unit):
+    return total[rows, unit * UNIT : (unit + 1) * UNIT] * D ** (-0.5)
+
+
+def keep_kernel(table, own, came, cosine, sine, *refs):
+    keys, values, mark = refs[-4:-1]
+    mark[...] = jnp.zeros_like(mark)
+    count = cosine.shape[1]
+    total = refs[-1]
+    total[...] = own[...] + jnp.where(table[1] == 1, 0.0, came[...].astype(jnp.float32))
+    for block in range(CORES):
+        rows = slice(block * count, (block + 1) * count)
+        for group in range(HALF_GROUPS):
+            key = kept_rows(total, rows, group)
+            keys[group, block] = turned(key, cosine[block], sine[block])
+            value = kept_rows(total, rows, HALF_GROUPS + group)
+            values[group, block] = value.astype(jnp.bfloat16)
+
+
+def keep_keys(table, own, came, cosine, sine, after=()):
+    kept = jax.ShapeDtypeStruct((HALF_GROUPS, CORES) + cosine.shape[1:], jnp.bfloat16)
+    return pl.pallas_call(
+        keep_kernel,
+        grid=(1,),
+        in_specs=[SMEM] + [whole_spec(a) for a in (own, came, cosine, sine)] + [HBM] * len(after),
+        out_specs=(whole_spec(kept), whole_spec(kept), whole_spec(MARK)),
+        out_shape=(kept, kept, MARK),
+        scratch_shapes=[pltpu.VMEM(own.shape, jnp.float32)],
+        compiler_params=pltpu.CompilerParams(vmem_limit_bytes=60 * MIB),
+        cost_estimate=SMALL,
+        name="keep_keys",
+    )(table, own, came, cosine, sine, *after)
+
+
+def attend_kernel(heads, group, parts, own, cosine, sine, places, keys, values, *refs):
+    came = refs[:parts]
+    outs, mark, hidden = refs[-4:-2], refs[-2], refs[-1]
+    mark[...] = jnp.zeros_like(mark)
+    count = cosine.shape[1]
+    tile = HEAD_DIM
+    for block in reversed(range(CORES)):
+        row = lax.broadcasted_iota(jnp.int32, (count, count), 0)
+        distance = row - lax.broadcasted_iota(jnp.int32, (count, count), 1)
+        visible = (distance >= 0) & (distance <= places[block])
+        hidden[...] = jnp.where(visible, 0.0, -1e30)
+        rows = slice(block * count, (block + 1) * count)
+        queries = [
+            turned(joined_rows(own, came, rows, head), cosine[block], sine[block])
+            for head in range(heads)
+        ]
+        for top in range(0, count, tile):
+            width = top + tile
+            scores = lax.dot_general(
+                jnp.concatenate([query[top:width] for query in queries], 0),
+                keys[group, block, :width],
+                (((1,), (1,)), ((), ())),
+                preferred_element_type=jnp.float32,
+            )
+            scores = scores + jnp.concatenate([hidden[top:width, :width]] * heads, 0)
+            scores = (scores - jnp.max(scores, -1, keepdims=True)) * HEAD_DIM ** (-0.5)
+            exponent = jnp.exp(scores)
+            share = jnp.sum(exponent, -1, keepdims=True)
+            mixed = jnp.dot(
+                exponent.astype(jnp.bfloat16),
+                values[group, block, :width],
+                preferred_element_type=jnp.float32,
+            )
+            mixed = (mixed / share).astype(jnp.bfloat16)
+            for head in range(heads):
+                outs[block][top:width, head * UNIT : (head + 1) * UNIT] = mixed[
+                    head * tile : (head + 1) * tile
+                ]
+
+
+def attend_chunks(chunks, own, came, cosine, sine, places, held, after=()):
+    count = cosine.shape[1]
+    heads, group = sum(len(CHUNKS[j]) for j in chunks), int(CHUNKS[chunks[0]][0][1])
+    out = jax.ShapeDtypeStruct((count, heads * UNIT), jnp.bfloat16)
+    return pl.pallas_call(
+        lambda *refs: attend_kernel(heads, group, len(came), *refs),
+        grid=(1,),
+        in_specs=[whole_spec(a) for a in (own, cosine, sine, places, *held, *came)]
+        + [HBM] * len(after),
+        out_specs=(whole_spec(out), whole_spec(out), whole_spec(MARK)),
+        out_shape=(out, out, MARK),
+        scratch_shapes=[pltpu.VMEM((count, count), jnp.float32)],
+        compiler_params=pltpu.CompilerParams(vmem_limit_bytes=60 * MIB),
+        cost_estimate=SMALL,
+        name="attend_chunks",
+    )(own, cosine, sine, places, *held, *came, *after)
+
+
+PARTS = 2
+TILE = 64
+
+
+def sent_kernel(part, anchor, weights, momentum, *refs):
+    out, mark, start, own, moved, made, sem = refs[-7:]
+    mark[...] = jnp.zeros_like(mark)
+    tiles = made.shape[1] // TILE
+    loads, stores = [], []
+    for tile in range(tiles):
+        here = pl.ds(tile * TILE, TILE)
+        there = pl.ds(pl.multiple_of((part[0] * tiles + tile) * TILE, TILE), TILE)
+        loads.append(
+            [
+                pltpu.make_async_copy(source.at[there], target.at[here], sem.at[at, tile])
+                for at, (source, target) in enumerate(
+                    ((anchor, start), (weights, own), (momentum, moved))
+                )
+            ]
+        )
+        stores.append(pltpu.make_async_copy(made.at[:, here], out.at[:, here], sem.at[3, tile]))
+    for tile in range(tiles):
+        for copy in loads[tile]:
+            copy.start()
+    for tile in range(tiles):
+        here = slice(tile * TILE, (tile + 1) * TILE)
+        for copy in loads[tile]:
+            copy.wait()
+        made[0, here] = moved[here].astype(made.dtype)
+        made[1, here] = (start[here] - own[here].astype(jnp.float32)).astype(made.dtype)
+        stores[tile].start()
+    for copy in stores:
+        copy.wait()
+
+
+def sent_part(part, anchor, weights, momentum, after=()):
+    rows, columns = anchor.shape
+    size = (rows // PARTS, columns)
+    return pl.pallas_call(
+        sent_kernel,
+        in_specs=[SMEM] + [HBM] * (3 + len(after)),
+        out_specs=(HBM, VMEM),
+        out_shape=(jax.ShapeDtypeStruct((2,) + size, jnp.bfloat16), MARK),
+        scratch_shapes=[
+            pltpu.VMEM(size, jnp.float32),
+            pltpu.VMEM(size, weights.dtype),
+            pltpu.VMEM(size, jnp.float32),
+            pltpu.VMEM((2,) + size, jnp.bfloat16),
+            pltpu.SemaphoreType.DMA((4, size[0] // TILE)),
+        ],
+        compiler_params=pltpu.CompilerParams(vmem_limit_bytes=60 * MIB),
+        cost_estimate=SMALL,
+        name="sent_part",
+    )(part, anchor, weights, momentum, *after)
+
+
+def relay_kernel(onward, came, piece, *refs):
+    out, mark, held, sem = refs[-4:]
+    mark[...] = jnp.zeros_like(mark)
+
+    @pl.when(onward[0] == 1)
+    def _():
+        half = came.shape[1] // 2
+        parts = [pl.ds(0, half), pl.ds(half, half)]
+        pass_on([(came.at[:, part], held.at[:, part], out.at[:, part]) for part in parts], sem)
+
+
+def relay(onward, came, piece, after=()):
+    return pl.pallas_call(
+        relay_kernel,
+        in_specs=[SMEM] + [HBM] * (2 + len(after)),
+        out_specs=(HBM, VMEM),
+        out_shape=(jax.ShapeDtypeStruct(piece.shape, piece.dtype), MARK),
+        scratch_shapes=[pltpu.VMEM(piece.shape, piece.dtype), pltpu.SemaphoreType.DMA((4,))],
+        input_output_aliases={2: 0},
+        compiler_params=pltpu.CompilerParams(vmem_limit_bytes=60 * MIB),
+        cost_estimate=SMALL,
+        name="relay",
+    )(onward, came, piece, *after)
+
+
+def outer_kernel(table, anchor, weights, momentum, *refs):
+    came = refs[:4]
+    new_params, new_momentum, mark, start, own, moved, mate, sem = refs[-8:]
+    mark[...] = jnp.zeros_like(mark)
+    rows = start.shape[0]
+    tiles = rows // TILE
+    per_part = tiles // PARTS
+
+    def mate_copy(tile, source):
+        there = pl.ds(tile % per_part * TILE, TILE)
+        here = pl.ds(tile * TILE, TILE)
+        return pltpu.make_async_copy(source.at[:, there], mate.at[:, here], sem.at[3, tile])
+
+    loads, stores = [], []
+    for tile in range(tiles):
+        here = pl.ds(tile * TILE, TILE)
+        loads.append(
+            [
+                pltpu.make_async_copy(source.at[here], target.at[here], sem.at[at, tile])
+                for at, (source, target) in enumerate(
+                    ((anchor, start), (weights, own), (momentum, moved))
+                )
+            ]
+        )
+        stores.append(
+            [
+                pltpu.make_async_copy(source.at[here], target.at[here], sem.at[4 + at, tile])
+                for at, (source, target) in enumerate(((start, new_params), (moved, new_momentum)))
+            ]
+        )
+    for tile in range(tiles):
+        for copy in loads[tile]:
+            copy.start()
+        for at, source in enumerate(came):
+
+            @pl.when(table[tile // per_part] == at)
+            def _():
+                mate_copy(tile, source).start()
+
+    for tile in range(tiles):
+        for copy in loads[tile]:
+            copy.wait()
+        mate_copy(tile, came[0]).wait()
+        here = slice(tile * TILE, (tile + 1) * TILE)
+        begun = start[here]
+        pseudo = begun - own[here].astype(jnp.float32)
+        grad_mean = 0.5 * (pseudo + mate[1, here].astype(jnp.float32))
+        mom_mean = 0.5 * (moved[here] + mate[0, here].astype(jnp.float32))
+        made = MOMENTUM_RATE * mom_mean + grad_mean
+        moved[here] = made
+        start[here] = begun - OUTER_RATE * (grad_mean + MOMENTUM_RATE * made)
+        for copy in stores[tile]:
+            copy.start()
+    for tile in range(tiles):
+        for copy in stores[tile]:
+            copy.wait()
+
+
+def outer_update(table, anchor, weights, momentum, came, after=()):
+    size = anchor.shape
+    full = jax.ShapeDtypeStruct(size, jnp.float32)
+    return pl.pallas_call(
+        outer_kernel,
+        in_specs=[SMEM] + [HBM] * (3 + len(came) + len(after)),
+        out_specs=(HBM, HBM, VMEM),
+        out_shape=(full, full, MARK),
+        scratch_shapes=[
+            pltpu.VMEM(size, jnp.float32),
+            pltpu.VMEM(size, weights.dtype),
+            pltpu.VMEM(size, jnp.float32),
+            pltpu.VMEM((2,) + size, jnp.bfloat16),
+            pltpu.SemaphoreType.DMA((6, size[0] // TILE)),
+        ],
+        compiler_params=pltpu.CompilerParams(vmem_limit_bytes=60 * MIB),
+        cost_estimate=SMALL,
+        name="outer_update",
+    )(table, anchor, weights, momentum, *came, *after)
+
+
+def line_step(partner, tokens, positions, weights, anchor, momentum):
+    rows, places = tokens[0], positions[0]
+    own_rows = weights[0]
+    start, moved = anchor[0], momentum[0]
+    count, depth = rows.shape[0], own_rows.shape[0]
+    me = lax.axis_index("fsdp")
+    chip, core = me // CORES, me % CORES
+    last = LINE - 1
+    chunks = len(CHUNKS)
+
+    def over(value, pairs):
+        return lax.ppermute(value, "fsdp", pairs)
+
+    cores = range(CORES)
+    swap = [(f, f ^ 1) for f in range(LINE * CORES)]
+    inward = [(a * CORES + c, b * CORES + c) for a, b in ((0, 1), (last, last - 1)) for c in cores]
+    across = [(a * CORES + c, b * CORES + c) for a, b in ((1, 2), (2, 1)) for c in cores]
+    outward = [(b, a) for a, b in inward] + inward
+    across += [(a * CORES + c, a * CORES + 1 - c) for a in (0, last) for c in cores]
+
+    other_rows = over(own_rows, across)
+    sibling_rows = over(own_rows, swap)
+    lead = (chip < LINE // 2).astype(jnp.int32)
+    handed, mark = hand_tokens(rows, lead[None])
+    handed = over(handed, inward)
+
+    distance = partner[0]
+    part_rows = depth // PARTS
+
+    along = [[(r, r ^ 1) for r in range(SQUARE)], [(r, r ^ 2) for r in range(SQUARE)]]
+    values = (start, own_rows, moved)
+    swapped = (distance == 2).astype(jnp.int32)
+    first = []
+    for part in (swapped, 1 - swapped):
+        made, mark = sent_part(part[None], *values, (mark,))
+        first.append(made)
+    came = [lax.ppermute(first[at], "replica", along[at]) for at in range(2)]
+    table = jnp.stack([jnp.where(distance == 3, 3, distance - 1), jnp.where(distance == 2, 3, 2)])
+
+    pairs = pairs_of_half(core)
+    packed, marks = [], (mark,)
+    for j in range(chunks):
+        made, mark = pack(
+            FIRST_UNIT[j] // 2, len(CHUNKS[j]) // 2, own_rows, sibling_rows, pairs, marks
+        )
+        packed.append(made)
+        marks = (mark,)
+    sibling_tokens = over(rows, swap)
+    both = jnp.stack([places, over(places, swap)])
+    frequency = ROPE_BASE ** (
+        -(jnp.arange(HEAD_DIM // 2, dtype=jnp.float32) * 2.0) / HEAD_DIM
+    )
+    angles = both.astype(jnp.float32)[:, :, None] * frequency
+    cosine, sine = jnp.cos(angles), jnp.sin(angles)
+    cosine = jnp.concatenate([cosine, cosine], -1)
+    sine = jnp.concatenate([-sine, sine], -1)
+    reach = both[:, :, None]
+
+    near_chip = jnp.where(chip < LINE // 2, 0, last)
+    middle = (chip > 0) & (chip < last)
+    chips = jnp.stack([chip, last - chip, last - near_chip, near_chip])
+    handed_chips = jnp.clip(chips - lead, 0, LINE - 2)
+    spots = jnp.concatenate([jnp.stack([core, middle.astype(jnp.int32)]), chips, handed_chips])
+    OURS, HANDED = 2, 2 + LINE
+    ours = (rows, sibling_tokens)
+
+    handed, mark = touch(handed, mark, cosine, sine)
+    theirs = (handed, over(handed, swap))
+    near, far = [over(packed[0], inward)], []
+
+    def stage(j, *after):
+        near[j], mark = touch(near[j], *far[j - 1 :], *after)
+        far.append(over(near[j], across))
+        if j + 2 < chunks:
+            near.append(over(touch(packed[j + 1], mark)[0], inward))
+        return mark
+
+    other_rows, mark = touch(other_rows, mark, near[0])
+    mark = stage(0, mark)
+    wide = ((own_rows, sibling_rows), (other_rows, over(other_rows, swap)))
+    onward = (distance == 3).astype(jnp.int32)[None]
+
+    contexts, owns, backs = [], [], []
+
+    def product(j, *after):
+        rider = packed[-1] if j == 0 else None
+        result, mark = project(
+            (j,), spots, pairs, theirs, HANDED, wide, ((far[j],),), jnp.bfloat16, after, rider
+        )
+        backs.append(over(result, outward))
+        return mark
+
+    def own(js, *after):
+        packed = (tuple(far[j] for j in js), tuple(near[j] for j in js))
+        result, mark = project(js, spots, pairs, ours, OURS, wide, packed, jnp.float32, after)
+        owns.append(result)
+        return mark
+
+    def attention(at, js, *after):
+        left, right, mark = attend_chunks(
+            js, owns[at], [backs[j] for j in js], cosine, sine, reach, held, after
+        )
+        contexts.append((left, over(right, swap)))
+        return mark
+
+    mark = stage(1, mark, *came)
+    for at in range(2):
+        made, mark = relay(onward, came[1 - at], first[1 - at], (mark,))
+        came.append(lax.ppermute(made, "replica", along[at]))
+    mark = product(0, mark)
+    mark = own((0,), mark)
+    mark = stage(2, mark)
+    mark = product(1, mark)
+    made, mark = unpack(backs[0], depth, (mark, far[2]))
+    near.append(made)
+    far.append(over(made, across))
+    mark = product(2, mark)
+    mark = own((1,), mark)
+    mark = product(3, mark, backs[1])
+    *held, mark = keep_keys(spots, owns[0], backs[0], cosine, sine, (mark,))
+    mark = attention(1, (1,), mark)
+    mark = own((2, 3), mark)
+    mark = attention(2, (2, 3), mark, came[2], came[3])
+    new_params, new_momentum, mark = outer_update(table, start, own_rows, moved, came, (mark,))
+
+    mine = jnp.concatenate([first for first, _ in contexts], 1)
+    came = jnp.concatenate([second for _, second in contexts], 1)
+    context = jnp.where(
+        core == 0, jnp.concatenate([mine, came], 1), jnp.concatenate([came, mine], 1)
+    )
+    return (context[None], new_params[None], new_momentum[None])
+
+
 def step(exchange, tokens, positions, weights, anchor, momentum):
     context = attention_step(tokens, positions, weights)
     new_params, new_momentum = outer_step(exchange, weights, anchor, momentum)
@@ -124,13 +771,9 @@
 def body(tokens, positions, partner, weights, anchor, momentum):
     count = lax.axis_size("replica")
     arrays = (tokens, positions, weights, anchor, momentum)
-    if count > 4:
-        return step(lambda values: exchange_any(values, partner, count), *arrays)
-    branches = [
-        lambda *held, pairs=pairs: step(lambda values: send_to_mate(values, pairs), *held)
-        for pairs in pairings(count)
-    ]
-    return lax.switch(partner[0] - 1, branches, *arrays)
+    if count == SQUARE and lax.axis_size("fsdp") == LINE * CORES:
+        return line_step(partner, *arrays)
+    return step(lambda values: exchange_any(values, partner, count), *arrays)
 
 
 def solution(mesh):

time: 294 us -> 227 us (0.77); the launches traced: 289 us -> 226 us
  waiting for transfers between devices: 200 us -> 67.8 us
  Pallas kernels: 0 us -> 91.2 us
  starting transfers between devices: 4.57 us -> 54.5 us
  other arithmetic: 27.3 us -> 4.71 us
  matrix products: 20.6 us -> 0 us
  between operations: 15 us -> 1.17 us
  loops' own time: 9.92 us -> 0 us
  local copies, waits for them, and re-layouts: 11.8 us -> 7.06 us
    pallas_call x0 -> x28, Pallas kernels: none -> 91.2 us  [the longest x7 22.2 us: project(): pl.pallas_call(lambda *refs: project_kernel(span, len(wide), len(chunks),...]
    all_gather x1 -> x0, waiting for transfers between devices: 68.9 us -> none  [attention_step(): lax.all_gather(weights, 'fsdp', axis=1, tiled=True)[0]]
    ppermute x2 -> x24, waiting for transfers between devices: 130 us -> 67.8 us  [the longest x20 61.9 us: over(): return lax.ppermute(value, 'fsdp', pairs)]
    ppermute x2 -> x24, starting transfers between devices: 4.53 us -> 54.5 us  [the longest x20 48.3 us: over(): return lax.ppermute(value, 'fsdp', pairs)]
    dot_general x3 -> x0, matrix products: 20.6 us -> none  [the longest x1 14.4 us: attention_step(): jnp.dot(rows, lax.all_gather(weights, 'fsdp', axis=1, tiled=True)[0], pre...]
    broadcast_in_dim x1, other arithmetic: 11.6 us -> 0.01 us  [line_step(): reach = both[:, :, None]]
    unnamed x1 -> x0, loops' own time: 9.92 us -> none
    convert_element_type x3 -> x0, other arithmetic: 7.76 us -> none  [the longest x1 5.08 us: outer_step(): momentum[0].astype(jnp.bfloat16)]
  transfers between devices with their start and end apart: 3 -> 24, of which waited for: 3 -> 5; matrix products, arithmetic and copies ran while one was open for 7% -> 3% of each run, Pallas kernels for 0% -> 40%
where the time goes in v3:
time: 227 us; the launch traced here: 226 us
  Pallas kernels  91.2 us (40%)
  waiting for transfers between devices  67.8 us (30%)
  starting transfers between devices  54.5 us (24%)
  local copies, waits for them, and re-layouts  7.06 us (3%)
  other arithmetic  4.71 us (2%)
    ppermute x20, waiting for transfers between devices, over(): return lax.ppermute(value, 'fsdp', pairs)  61.9 us
    ppermute x20, starting transfers between devices, over(): return lax.ppermute(value, 'fsdp', pairs)  48.3 us
    pallas_call x7, Pallas kernels, project(): pl.pallas_call(lambda *refs: project_kernel(span, len(wide), len(chunks),...  22.2 us
    pallas_call x1, Pallas kernels, outer_update(): pl.pallas_call(outer_kernel, in_specs=[SMEM] + [HBM] * (3 + len(came) + l...  14 us
    pallas_call x4, Pallas kernels, pack(): pl.pallas_call(lambda *refs: pack_kernel(first, count, *refs), in_specs=[...  12.6 us
    pallas_call x2, Pallas kernels, attend_chunks(): pl.pallas_call(lambda *refs: attend_kernel(heads, group, len(came), *refs...  11.2 us
    pallas_call x2, Pallas kernels, sent_part(): pl.pallas_call(sent_kernel, in_specs=[SMEM] + [HBM] * (3 + len(after)), o...  11.1 us
    pallas_call x2, Pallas kernels, relay(): pl.pallas_call(relay_kernel, in_specs=[SMEM] + [HBM] * (2 + len(after)),...  7.41 us
  transfers between devices with their start and end apart: 24, of which 5 were waited for; matrix products, arithmetic and copies ran while one was open for 3% of the time, Pallas kernels for 40%

profile of v3, /device:TPU:0, one launch (start us, length us, event | category | flops | bytes accessed | tf_op | source)
XLA Modules:
  0.0 226.5 jit_solution(18444925044576877969)
XLA Ops:
  1.2 3.2 %hand_tokens.1 = (bf16[384,3072]{1,0:T(8,128)(2,1)}, f32[8,128]{1,0:T(8,128)}) custom-call(s32[1]{0:T(128)} %bitcast.14.lead, bf16[384,4096]{1,0:T(8,128)(2,1)} %bitcast.48), custom_call_target="tpu_custom_call" | custom-call | flops 1 | bytes 1 | tf_op jit(solution)/shard_map/hand_tokens/pallas_call | solution.py:156
  4.5 7.5 %collective-permute-start.3 = (bf16[384,3072]{1,0:T(8,128)(2,1)}, bf16[384,3072]{1,0:T(8,128)(2,1)}, u32[]{:S(2)}, u32[]{:S(2)}) collective-permute-start(bf16[384,3072]{1,0:T(8,128)(2,1)} %get-tuple-element.60), channel_id=1, source_target_pairs={{0,2},{1,3},{6,4},{7,5},{8,10},{9,11},{14,12},{15,13},{16,18},{17,... | collective-permute-start | bytes 7077896 | tf_op jit(solution)/shard_map/ppermute | solution.py:643
  12.0 5.5 %sent_part.2 = (bf16[2,256,3072]{2,1,0:T(8,128)(2,1)}, f32[8,128]{1,0:T(8,128)}) custom-call(s32[1]{0:T(128)S(6)} %convert_element_type.20.part, f32[512,3072]{1,0:T(8,128)} %bitcast.42, bf16[512,3072]{1,0:T(8,128)(2,1)} %bitcast.28, f32[512,3072]{1,0:T(8,128)} %bitcast.45, f32[8,128]{1,0:T(8,128)} %get-tuple-element.61.refs_0_), custom_call_target="tpu_custom_call" | custom-call | flops 1 | bytes 1 | tf_op jit(solution)/shard_map/sent_part/pallas_call | solution.py:510
  17.5 5.5 %sent_part.3 = (bf16[2,256,3072]{2,1,0:T(8,128)(2,1)}, f32[8,128]{1,0:T(8,128)}) custom-call(s32[1]{0:T(128)S(6)} %sub.28.part, f32[512,3072]{1,0:T(8,128)} %bitcast.43, bf16[512,3072]{1,0:T(8,128)(2,1)} %bitcast.29, f32[512,3072]{1,0:T(8,128)} %bitcast.46, f32[8,128]{1,0:T(8,128)} %get-tuple-element.62.refs_0_), custom_call_target="tpu_custom_call" | custom-call | flops 1 | bytes 1 | tf_op jit(solution)/shard_map/sent_part/pallas_call | solution.py:510
  27.8 3.2 %pack.4 = (bf16[2,512,512]{2,1,0:T(8,128)(2,1)}, f32[8,128]{1,0:T(8,128)}) custom-call(s32[6]{0:T(128)} %stack.70.refs_0_.refs_1_, bf16[512,3072]{1,0:T(8,128)(2,1)} %bitcast.30, bf16[512,3072]{1,0:T(8,128)(2,1)} %copy-done, f32[8,128]{1,0:T(8,128)} %get-tuple-element.63.refs_3_), custom_call_target="tpu_custom_call" | custom-call | flops 1 | bytes 1 | tf_op jit(solution)/shard_map/pack/pallas_call | solution.py:185
  35.1 3.3 %pack.5 = (bf16[2,512,512]{2,1,0:T(8,128)(2,1)}, f32[8,128]{1,0:T(8,128)}) custom-call(s32[6]{0:T(128)} %stack.70.refs_0_.refs_1_, bf16[512,3072]{1,0:T(8,128)(2,1)} %bitcast.31, bf16[512,3072]{1,0:T(8,128)(2,1)} %copy-done, f32[8,128]{1,0:T(8,128)} %get-tuple-element.64.refs_3_), custom_call_target="tpu_custom_call" | custom-call | flops 1 | bytes 1 | tf_op jit(solution)/shard_map/pack/pallas_call | solution.py:185
  38.4 3.0 %pack.6 = (bf16[2,512,256]{2,1,0:T(8,128)(2,1)}, f32[8,128]{1,0:T(8,128)}) custom-call(s32[6]{0:T(128)} %stack.70.refs_0_.refs_1_, bf16[512,3072]{1,0:T(8,128)(2,1)} %bitcast.32, bf16[512,3072]{1,0:T(8,128)(2,1)} %copy-done, f32[8,128]{1,0:T(8,128)} %get-tuple-element.65.refs_3_), custom_call_target="tpu_custom_call" | custom-call | flops 1 | bytes 1 | tf_op jit(solution)/shard_map/pack/pallas_call | solution.py:185
  41.5 3.0 %pack.7 = (bf16[2,512,256]{2,1,0:T(8,128)(2,1)}, f32[8,128]{1,0:T(8,128)}) custom-call(s32[6]{0:T(128)} %stack.70.refs_0_.refs_1_, bf16[512,3072]{1,0:T(8,128)(2,1)} %bitcast.33, bf16[512,3072]{1,0:T(8,128)(2,1)} %copy-done, f32[8,128]{1,0:T(8,128)} %get-tuple-element.66.refs_3_), custom_call_target="tpu_custom_call" | custom-call | flops 1 | bytes 1 | tf_op jit(solution)/shard_map/pack/pallas_call | solution.py:185
  44.5 17.9 %collective-permute-done.3.refs_0_ = bf16[384,3072]{1,0:T(8,128)(2,1)} collective-permute-done((bf16[384,3072]{1,0:T(8,128)(2,1)}, bf16[384,3072]{1,0:T(8,128)(2,1)}, u32[]{:S(2)}, u32[]{:S(2)}) %collective-permute-start.3) | collective-permute-done | bytes 2359328 | tf_op jit(solution)/shard_map/ppermute | solution.py:643
  63.0 21.1 %collective-permute-done.5.refs_2_.refs_0_ = bf16[2,512,512]{2,1,0:T(8,128)(2,1)S(1)} collective-permute-done((bf16[2,512,512]{2,1,0:T(8,128)(2,1)}, bf16[2,512,512]{2,1,0:T(8,128)(2,1)S(1)}, u32[]{:S(2)}, u32[]{:S(2)}) %collective-permute-start.5) | collective-permute-done | bytes 1048608 | tf_op jit(solution)/shard_map/ppermute | solution.py:643
  87.4 6.0 %collective-permute-done.10.refs_4_.came.refs_1_ = bf16[2,256,3072]{2,1,0:T(8,128)(2,1)} collective-permute-done((bf16[2,256,3072]{2,1,0:T(8,128)(2,1)}, bf16[2,256,3072]{2,1,0:T(8,128)(2,1)}, u32[]{:S(2)}, u32[]{:S(2)}) %collective-permute-start.10) | collective-permute-done | bytes 3145760 | tf_op jit(solution)/shard_map/ppermute | solution.py:668
  93.3 2.3 %collective-permute-start.7 = (bf16[2,512,512]{2,1,0:T(8,128)(2,1)}, bf16[2,512,512]{2,1,0:T(8,128)(2,1)}, u32[]{:S(2)}, u32[]{:S(2)}) collective-permute-start(bf16[2,512,512]{2,1,0:T(8,128)(2,1)} %get-tuple-element.74), channel_id=1, source_target_pairs={{0,2},{1,3},{6,4},{7,5},{8,10},{9,11},{14,12},{15,13},{16,18},{17,... | collective-permute-start | bytes 3145736 | tf_op jit(solution)/shard_map/ppermute | solution.py:643
  95.7 21.1 %collective-permute-done.7.refs_0_ = bf16[2,512,512]{2,1,0:T(8,128)(2,1)} collective-permute-done((bf16[2,512,512]{2,1,0:T(8,128)(2,1)}, bf16[2,512,512]{2,1,0:T(8,128)(2,1)}, u32[]{:S(2)}, u32[]{:S(2)}) %collective-permute-start.7) | collective-permute-done | bytes 1048608 | tf_op jit(solution)/shard_map/ppermute | solution.py:643
  117.4 3.7 %relay.2 = (bf16[2,256,3072]{2,1,0:T(8,128)(2,1)}, f32[8,128]{1,0:T(8,128)}) custom-call(s32[1]{0:T(128)S(6)} %convert_element_type.22.onward, bf16[2,256,3072]{2,1,0:T(8,128)(2,1)} %collective-permute-done.10.refs_4_.came.refs_1_, bf16[2,256,3072]{2,1,0:T(8,128)(2,1)} %get-tuple-element.77.piece, ...), custom_call_target="tpu_custom_call", output_to_operand_aliasing={{0}: (2, {})} | custom-call | flops 1 | bytes 1 | tf_op jit(solution)/shard_map/relay/pallas_call | solution.py:540
  121.1 3.7 %relay.3 = (bf16[2,256,3072]{2,1,0:T(8,128)(2,1)}, f32[8,128]{1,0:T(8,128)}) custom-call(s32[1]{0:T(128)S(6)} %convert_element_type.22.onward, bf16[2,256,3072]{2,1,0:T(8,128)(2,1)} %collective-permute-done.9.refs_3_.came.refs_0_, bf16[2,256,3072]{2,1,0:T(8,128)(2,1)} %get-tuple-element.76.piece, ...), custom_call_target="tpu_custom_call", output_to_operand_aliasing={{0}: (2, {})} | custom-call | flops 1 | bytes 1 | tf_op jit(solution)/shard_map/relay/pallas_call | solution.py:540
  128.5 5.6 %collective-permute-start.13 = (bf16[2,512,256]{2,1,0:T(8,128)(2,1)}, bf16[2,512,256]{2,1,0:T(8,128)(2,1)}, u32[]{:S(2)}, u32[]{:S(2)}) collective-permute-start(bf16[2,512,256]{2,1,0:T(8,128)(2,1)} %get-tuple-element.82), channel_id=1, source_target_pairs={{0,2},{1,3},{6,4},{7,5},{8,10},{9,11},{14,12},{15,13},{16,18},{17,... | collective-permute-start | bytes 1572872 | tf_op jit(solution)/shard_map/ppermute | solution.py:643
  134.8 2.8 %project.7 = (bf16[768,512]{1,0:T(8,128)(2,1)}, f32[8,128]{1,0:T(8,128)}) custom-call(s32[10]{0:T(128)} %concatenate.46.refs_0_.table, s32[6]{0:T(128)} %stack.70.refs_0_.refs_1_, bf16[384,3072]{1,0:T(8,128)(2,1)} %get-tuple-element.79.refs_2_, bf16[384,3072]{1,0:T(8,128)(2,1)} %collective-permute-done.12.refs_3_, bf16[512,3072]{1,0:T(8,128)(2,1)} %bitcast.34, ...), custom_call_target="tpu_custom_call" | custom-call | flops 1 | bytes 1 | tf_op jit(solution)/shard_map/project/pallas_call | solution.py:315
  137.7 2.0 collective-permute-start.15
  139.7 4.7 %project.8 = (f32[768,512]{1,0:T(8,128)}, f32[8,128]{1,0:T(8,128)}) custom-call(s32[10]{0:T(128)} %concatenate.46.refs_0_.table, s32[6]{0:T(128)} %stack.70.refs_0_.refs_1_, bf16[384,4096]{1,0:T(8,128)(2,1)} %bitcast.50, bf16[384,4096]{1,0:T(8,128)(2,1)} %collective-permute-done.refs_3_, bf16[512,3072]{1,0:T(8,128)(2,1)} %bitcast.35, ...), custom_call_target="tpu_custom_call" | custom-call | flops 1 | bytes 1 | tf_op jit(solution)/shard_map/project/pallas_call | solution.py:315
  144.4 1.6 collective-permute-done.13.refs_0_
  146.6 1.8 project.9
  148.4 12.4 %collective-permute-start.17 = (bf16[768,512]{1,0:T(8,128)(2,1)}, bf16[768,512]{1,0:T(8,128)(2,1)S(1)}, u32[]{:S(2)}, u32[]{:S(2)}) collective-permute-start(bf16[768,512]{1,0:T(8,128)(2,1)} %get-tuple-element.98), channel_id=1, source_target_pairs={{2,0},{3,1},{4,6},{5,7},{0,2},{1,3},{6,4},{7,5},{10,8},{11,9},{12,... | collective-permute-start | bytes 2359304 | tf_op jit(solution)/shard_map/ppermute | solution.py:643
  161.9 2.4 %unpack.1 = (bf16[2,512,256]{2,1,0:T(8,128)(2,1)}, f32[8,128]{1,0:T(8,128)}) custom-call(bf16[768,512]{1,0:T(8,128)(2,1)} %copy-done.4, f32[8,128]{1,0:T(8,128)} %get-tuple-element.91.refs_0_, bf16[2,512,256]{2,1,0:T(8,128)(2,1)} %copy-done.3), custom_call_target="tpu_custom_call" | custom-call | flops 1 | bytes 1 | tf_op jit(solution)/shard_map/unpack/pallas_call | solution.py:353
  165.9 8.7 %collective-permute-start.18 = (bf16[768,256]{1,0:T(8,128)(2,1)}, bf16[768,256]{1,0:T(8,128)(2,1)S(1)}, u32[]{:S(2)}, u32[]{:S(2)}) collective-permute-start(bf16[768,256]{1,0:T(8,128)(2,1)} %get-tuple-element.106), channel_id=1, source_target_pairs={{2,0},{3,1},{4,6},{5,7},{0,2},{1,3},{6,4},{7,5},{10,8},{11,9},{12,... | collective-permute-start | bytes 1179656 | tf_op jit(solution)/shard_map/ppermute | solution.py:643
  174.6 4.9 %project.11 = (f32[768,512]{1,0:T(8,128)}, f32[8,128]{1,0:T(8,128)}) custom-call(s32[10]{0:T(128)} %concatenate.46.refs_0_.table, s32[6]{0:T(128)} %stack.70.refs_0_.refs_1_, bf16[384,4096]{1,0:T(8,128)(2,1)} %bitcast.51, bf16[384,4096]{1,0:T(8,128)(2,1)} %collective-permute-done.refs_3_, bf16[512,3072]{1,0:T(8,128)(2,1)} %bitcast.38, ...), custom_call_target="tpu_custom_call" | custom-call | flops 1 | bytes 1 | tf_op jit(solution)/shard_map/project/pallas_call | solution.py:315
  180.6 1.6 project.12
  182.1 6.8 %collective-permute-start.19 = (bf16[768,256]{1,0:T(8,128)(2,1)}, bf16[768,256]{1,0:T(8,128)(2,1)S(1)}, u32[]{:S(2)}, u32[]{:S(2)}) collective-permute-start(bf16[768,256]{1,0:T(8,128)(2,1)} %get-tuple-element.107), channel_id=1, source_target_pairs={{2,0},{3,1},{4,6},{5,7},{0,2},{1,3},{6,4},{7,5},{10,8},{11,9},{12,... | collective-permute-start | bytes 1179656 | tf_op jit(solution)/shard_map/ppermute | solution.py:643
  189.8 3.0 %keep_keys.1 = (bf16[2,2,384,128]{3,2,1,0:T(8,128)(2,1)}, bf16[2,2,384,128]{3,2,1,0:T(8,128)(2,1)}, f32[8,128]{1,0:T(8,128)}) custom-call(s32[10]{0:T(128)} %concatenate.46.refs_0_.table, f32[768,512]{1,0:T(8,128)} %get-tuple-element.95.own, bf16[768,512]{1,0:T(8,128)(2,1)} %copy-done.4, f32[2,384,128]{2,1,0:T(8,128)} %get-tuple-element.122.refs_2_.cosine.refs_1_, ...), custom_call_target="tpu_custom_call" | custom-call | flops 1 | bytes 1 | tf_op jit(solution)/shard_map/keep_keys/pallas_call | solution.py:401
  192.9 5.6 %attend_chunks.2 = (bf16[384,512]{1,0:T(8,128)(2,1)}, bf16[384,512]{1,0:T(8,128)(2,1)}, f32[8,128]{1,0:T(8,128)}) custom-call(f32[768,512]{1,0:T(8,128)} %get-tuple-element.94.refs_0_, f32[2,384,128]{2,1,0:T(8,128)} %get-tuple-element.122.refs_2_.cosine.refs_1_, f32[2,384,128]{2,1,0:T(8,128)} %get-tuple-element.123.refs_3_.sine.refs_2_, ...), custom_call_target="tpu_custom_call" | custom-call | flops 1 | bytes 1 | tf_op jit(solution)/shard_map/attend_chunks/pallas_call | solution.py:458
  198.5 4.9 %project.13 = (f32[768,512]{1,0:T(8,128)}, f32[8,128]{1,0:T(8,128)}) custom-call(s32[10]{0:T(128)} %concatenate.46.refs_0_.table, s32[6]{0:T(128)} %stack.70.refs_0_.refs_1_, bf16[384,4096]{1,0:T(8,128)(2,1)} %bitcast.52, bf16[384,4096]{1,0:T(8,128)(2,1)} %collective-permute-done.refs_3_, bf16[512,3072]{1,0:T(8,128)(2,1)} %bitcast.40, ...), custom_call_target="tpu_custom_call" | custom-call | flops 1 | bytes 1 | tf_op jit(solution)/shard_map/project/pallas_call | solution.py:315
  204.3 5.6 %attend_chunks.3 = (bf16[384,512]{1,0:T(8,128)(2,1)}, bf16[384,512]{1,0:T(8,128)(2,1)}, f32[8,128]{1,0:T(8,128)}) custom-call(f32[768,512]{1,0:T(8,128)} %get-tuple-element.105.refs_0_, f32[2,384,128]{2,1,0:T(8,128)} %get-tuple-element.122.refs_2_.cosine.refs_1_, f32[2,384,128]{2,1,0:T(8,128)} %get-tuple-element.123.refs_3_.sine.refs_2_, ...), custom_call_target="tpu_custom_call" | custom-call | flops 1 | bytes 1 | tf_op jit(solution)/shard_map/attend_chunks/pallas_call | solution.py:458
  211.1 14.0 %outer_update.1 = (f32[512,3072]{1,0:T(8,128)}, f32[512,3072]{1,0:T(8,128)}, f32[8,128]{1,0:T(8,128)}) custom-call(s32[2]{0:T(128)} %pad_add_fusion.1.table, f32[512,3072]{1,0:T(8,128)} %bitcast.44, bf16[512,3072]{1,0:T(8,128)(2,1)} %bitcast.41, f32[512,3072]{1,0:T(8,128)} %bitcast.47, bf16[2,256,3072]{2,1,0:T(8,128)(2,1)} %collective-permute-done.9.refs_3_.came.refs_0_, ...), custom_call_target="tpu_custom_call" | custom-call | flops 1 | bytes 1 | tf_op jit(solution)/shard_map/outer_update/pallas_call | solution.py:614
  (82 shorter events, 26.8 us)
Async XLA Ops:
  0.6 11.3 %copy-start.12 = (s32[4]{0:T(128)S(1)}, s32[4]{0:T(128)}, u32[]{:S(2)}) copy-start(s32[4]{0:T(128)} %param.8) | copy-start | bytes 52
  0.6 25.5 %collective-permute-start.1 = (bf16[512,3072]{1,0:T(8,128)(2,1)}, bf16[512,3072]{1,0:T(8,128)(2,1)S(1)}, u32[]{:S(2)}, u32[]{:S(2)}) collective-permute-start(bf16[512,3072]{1,0:T(8,128)(2,1)} %bitcast.26), channel_id=1, source_target_pairs={{0,1},{1,0},{2,3},{3,2},{4,5},{5,4},{6,7},{7,6},{8,9},{9,8},{10,11... | collective-permute-start | bytes 9437192 | tf_op jit(solution)/shard_map/ppermute | solution.py:643
  1.2 61.9 %collective-permute-start.2 = (bf16[512,3072]{1,0:T(8,128)(2,1)}, bf16[512,3072]{1,0:T(8,128)(2,1)}, u32[]{:S(2)}, u32[]{:S(2)}) collective-permute-start(bf16[512,3072]{1,0:T(8,128)(2,1)} %bitcast.27), channel_id=1, source_target_pairs={{2,4},{3,5},{4,2},{5,3},{0,1},{1,0},{6,7},{7,6},{10,12},{11,13},{1... | collective-permute-start | bytes 9437192 | tf_op jit(solution)/shard_map/ppermute | solution.py:643
  4.5 58.0 %collective-permute-start.3 = (bf16[384,3072]{1,0:T(8,128)(2,1)}, bf16[384,3072]{1,0:T(8,128)(2,1)}, u32[]{:S(2)}, u32[]{:S(2)}) collective-permute-start(bf16[384,3072]{1,0:T(8,128)(2,1)} %get-tuple-element.60), channel_id=1, source_target_pairs={{0,2},{1,3},{6,4},{7,5},{8,10},{9,11},{14,12},{15,13},{16,18},{17,... | collective-permute-start | bytes 7077896 | tf_op jit(solution)/shard_map/ppermute | solution.py:643
  17.5 8.6 %copy-start.11 = (s32[1,384]{1,0:T(1,128)S(1)}, s32[1,384]{1,0:T(1,128)}, u32[]{:S(2)}) copy-start(s32[1,384]{1,0:T(1,128)} %param.7) | copy-start | bytes 4612
  23.1 70.3 %collective-permute-start.10 = (bf16[2,256,3072]{2,1,0:T(8,128)(2,1)}, bf16[2,256,3072]{2,1,0:T(8,128)(2,1)}, u32[]{:S(2)}, u32[]{:S(2)}) collective-permute-start(bf16[2,256,3072]{2,1,0:T(8,128)(2,1)} %get-tuple-element.77.piece), channel_id=1, source_target_pairs={{0,16},{8,24},{16,0},{24,8},{1,17},{9,25},{17,1},{25,9},{2,18},{10... | collective-permute-start | bytes 9437192 | tf_op jit(solution)/shard_map/ppermute | solution.py:668
  24.6 71.0 %collective-permute-start.9 = (bf16[2,256,3072]{2,1,0:T(8,128)(2,1)}, bf16[2,256,3072]{2,1,0:T(8,128)(2,1)}, u32[]{:S(2)}, u32[]{:S(2)}) collective-permute-start(bf16[2,256,3072]{2,1,0:T(8,128)(2,1)} %get-tuple-element.76.piece), channel_id=1, source_target_pairs={{0,8},{8,0},{16,24},{24,16},{1,9},{9,1},{17,25},{25,17},{2,10},{10... | collective-permute-start | bytes 9437192 | tf_op jit(solution)/shard_map/ppermute | solution.py:668
  26.2 1.7 copy-start
  26.2 4.9 %collective-permute-start.4 = (s32[384]{0:T(512)S(1)}, s32[384]{0:T(512)S(1)}, u32[]{:S(2)}, u32[]{:S(2)}) collective-permute-start(s32[384]{0:T(512)S(1)} %reduce), channel_id=1, source_target_pairs={{0,1},{1,0},{2,3},{3,2},{4,5},{5,4},{6,7},{7,6},{8,9},{9,8},{10,11... | collective-permute-start | bytes 4616 | tf_op jit(solution)/shard_map/ppermute | solution.py:643
  31.1 53.0 %collective-permute-start.5 = (bf16[2,512,512]{2,1,0:T(8,128)(2,1)}, bf16[2,512,512]{2,1,0:T(8,128)(2,1)S(1)}, u32[]{:S(2)}, u32[]{:S(2)}) collective-permute-start(bf16[2,512,512]{2,1,0:T(8,128)(2,1)} %get-tuple-element.69), channel_id=1, source_target_pairs={{0,2},{1,3},{6,4},{7,5},{8,10},{9,11},{14,12},{15,13},{16,18},{17,... | collective-permute-start | bytes 3145736 | tf_op jit(solution)/shard_map/ppermute | solution.py:643
  85.7 42.8 %collective-permute-start.6 = (bf16[512,3072]{1,0:T(8,128)(2,1)}, bf16[512,3072]{1,0:T(8,128)(2,1)S(1)}, u32[]{:S(2)}, u32[]{:S(2)}) collective-permute-start(bf16[512,3072]{1,0:T(8,128)(2,1)} %get-tuple-element.70.refs_6_), channel_id=1, source_target_pairs={{0,1},{1,0},{2,3},{3,2},{4,5},{5,4},{6,7},{7,6},{8,9},{9,8},{10,11... | collective-permute-start | bytes 9437192 | tf_op jit(solution)/shard_map/ppermute | solution.py:643
  85.7 42.2 %collective-permute-start.12 = (bf16[384,3072]{1,0:T(8,128)(2,1)}, bf16[384,3072]{1,0:T(8,128)(2,1)}, u32[]{:S(2)}, u32[]{:S(2)}) collective-permute-start(bf16[384,3072]{1,0:T(8,128)(2,1)} %get-tuple-element.79.refs_2_), channel_id=1, source_target_pairs={{0,1},{1,0},{2,3},{3,2},{4,5},{5,4},{6,7},{7,6},{8,9},{9,8},{10,11... | collective-permute-start | bytes 7077896 | tf_op jit(solution)/shard_map/ppermute | solution.py:643
  86.2 51.5 %collective-permute-start = (bf16[384,4096]{1,0:T(8,128)(2,1)}, bf16[384,4096]{1,0:T(8,128)(2,1)}, u32[]{:S(2)}, u32[]{:S(2)}) collective-permute-start(bf16[384,4096]{1,0:T(8,128)(2,1)} %bitcast.49), channel_id=1, source_target_pairs={{0,1},{1,0},{2,3},{3,2},{4,5},{5,4},{6,7},{7,6},{8,9},{9,8},{10,11... | collective-permute-start | bytes 9437192 | tf_op jit(solution)/shard_map/ppermute | solution.py:643
  93.3 23.5 %collective-permute-start.7 = (bf16[2,512,512]{2,1,0:T(8,128)(2,1)}, bf16[2,512,512]{2,1,0:T(8,128)(2,1)}, u32[]{:S(2)}, u32[]{:S(2)}) collective-permute-start(bf16[2,512,512]{2,1,0:T(8,128)(2,1)} %get-tuple-element.74), channel_id=1, source_target_pairs={{0,2},{1,3},{6,4},{7,5},{8,10},{9,11},{14,12},{15,13},{16,18},{17,... | collective-permute-start | bytes 3145736 | tf_op jit(solution)/shard_map/ppermute | solution.py:643
  95.6 21.2 %collective-permute-start.8 = (bf16[2,512,512]{2,1,0:T(8,128)(2,1)}, bf16[2,512,512]{2,1,0:T(8,128)(2,1)}, u32[]{:S(2)}, u32[]{:S(2)}) collective-permute-start(bf16[2,512,512]{2,1,0:T(8,128)(2,1)} %get-tuple-element.75.refs_9_), channel_id=1, source_target_pairs={{2,4},{3,5},{4,2},{5,3},{0,1},{1,0},{6,7},{7,6},{10,12},{11,13},{1... | collective-permute-start | bytes 3145736 | tf_op jit(solution)/shard_map/ppermute | solution.py:643
  124.8 78.6 %collective-permute-start.21 = (bf16[2,256,3072]{2,1,0:T(8,128)(2,1)}, bf16[2,256,3072]{2,1,0:T(8,128)(2,1)}, u32[]{:S(2)}, u32[]{:S(2)}) collective-permute-start(bf16[2,256,3072]{2,1,0:T(8,128)(2,1)} %get-tuple-element.110), channel_id=1, source_target_pairs={{0,16},{8,24},{16,0},{24,8},{1,17},{9,25},{17,1},{25,9},{2,18},{10... | collective-permute-start | bytes 9437192 | tf_op jit(solution)/shard_map/ppermute | solution.py:740
  126.4 77.0 %collective-permute-start.20 = (bf16[2,256,3072]{2,1,0:T(8,128)(2,1)}, bf16[2,256,3072]{2,1,0:T(8,128)(2,1)}, u32[]{:S(2)}, u32[]{:S(2)}) collective-permute-start(bf16[2,256,3072]{2,1,0:T(8,128)(2,1)} %get-tuple-element.109), channel_id=1, source_target_pairs={{0,8},{8,0},{16,24},{24,16},{1,9},{9,1},{17,25},{25,17},{2,10},{10... | collective-permute-start | bytes 9437192 | tf_op jit(solution)/shard_map/ppermute | solution.py:740
  127.9 18.1 %collective-permute-start.11 = (bf16[2,512,512]{2,1,0:T(8,128)(2,1)}, bf16[2,512,512]{2,1,0:T(8,128)(2,1)}, u32[]{:S(2)}, u32[]{:S(2)}) collective-permute-start(bf16[2,512,512]{2,1,0:T(8,128)(2,1)} %get-tuple-element.78.refs_9_), channel_id=1, source_target_pairs={{2,4},{3,5},{4,2},{5,3},{0,1},{1,0},{6,7},{7,6},{10,12},{11,13},{1... | collective-permute-start | bytes 3145736 | tf_op jit(solution)/shard_map/ppermute | solution.py:643
  128.5 6.3 %copy-start.1 = (bf16[512,3072]{1,0:T(8,128)(2,1)}, bf16[512,3072]{1,0:T(8,128)(2,1)S(1)}, u32[]{:S(2)}) copy-start(bf16[512,3072]{1,0:T(8,128)(2,1)S(1)} %collective-permute-done.6.refs_7_) | copy-start | bytes 9437188
  128.5 17.5 %collective-permute-start.13 = (bf16[2,512,256]{2,1,0:T(8,128)(2,1)}, bf16[2,512,256]{2,1,0:T(8,128)(2,1)}, u32[]{:S(2)}, u32[]{:S(2)}) collective-permute-start(bf16[2,512,256]{2,1,0:T(8,128)(2,1)} %get-tuple-element.82), channel_id=1, source_target_pairs={{0,2},{1,3},{6,4},{7,5},{8,10},{9,11},{14,12},{15,13},{16,18},{17,... | collective-permute-start | bytes 1572872 | tf_op jit(solution)/shard_map/ppermute | solution.py:643
  137.7 23.2 %collective-permute-start.15 = (bf16[768,512]{1,0:T(8,128)(2,1)}, bf16[768,512]{1,0:T(8,128)(2,1)S(1)}, u32[]{:S(2)}, u32[]{:S(2)}) collective-permute-start(bf16[768,512]{1,0:T(8,128)(2,1)} %get-tuple-element.89), channel_id=1, source_target_pairs={{2,0},{3,1},{4,6},{5,7},{0,2},{1,3},{6,4},{7,5},{10,8},{11,9},{12,... | collective-permute-start | bytes 2359304 | tf_op jit(solution)/shard_map/ppermute | solution.py:643
  146.6 14.2 %collective-permute-start.14 = (bf16[2,512,256]{2,1,0:T(8,128)(2,1)}, bf16[2,512,256]{2,1,0:T(8,128)(2,1)S(1)}, u32[]{:S(2)}, u32[]{:S(2)}) collective-permute-start(bf16[2,512,256]{2,1,0:T(8,128)(2,1)} %get-tuple-element.88.refs_10_), channel_id=1, source_target_pairs={{2,4},{3,5},{4,2},{5,3},{0,1},{1,0},{6,7},{7,6},{10,12},{11,13},{1... | collective-permute-start | bytes 1572872 | tf_op jit(solution)/shard_map/ppermute | solution.py:643
  148.4 31.1 %collective-permute-start.17 = (bf16[768,512]{1,0:T(8,128)(2,1)}, bf16[768,512]{1,0:T(8,128)(2,1)S(1)}, u32[]{:S(2)}, u32[]{:S(2)}) collective-permute-start(bf16[768,512]{1,0:T(8,128)(2,1)} %get-tuple-element.98), channel_id=1, source_target_pairs={{2,0},{3,1},{4,6},{5,7},{0,2},{1,3},{6,4},{7,5},{10,8},{11,9},{12,... | collective-permute-start | bytes 2359304 | tf_op jit(solution)/shard_map/ppermute | solution.py:643
  160.8 1.0 copy-start.4
  164.3 15.2 %collective-permute-start.16 = (bf16[2,512,256]{2,1,0:T(8,128)(2,1)}, bf16[2,512,256]{2,1,0:T(8,128)(2,1)S(1)}, u32[]{:S(2)}, u32[]{:S(2)}) collective-permute-start(bf16[2,512,256]{2,1,0:T(8,128)(2,1)} %get-tuple-element.96.refs_11_), channel_id=1, source_target_pairs={{2,4},{3,5},{4,2},{5,3},{0,1},{1,0},{6,7},{7,6},{10,12},{11,13},{1... | collective-permute-start | bytes 1572872 | tf_op jit(solution)/shard_map/ppermute | solution.py:643
  165.9 37.5 %collective-permute-start.18 = (bf16[768,256]{1,0:T(8,128)(2,1)}, bf16[768,256]{1,0:T(8,128)(2,1)S(1)}, u32[]{:S(2)}, u32[]{:S(2)}) collective-permute-start(bf16[768,256]{1,0:T(8,128)(2,1)} %get-tuple-element.106), channel_id=1, source_target_pairs={{2,0},{3,1},{4,6},{5,7},{0,2},{1,3},{6,4},{7,5},{10,8},{11,9},{12,... | collective-permute-start | bytes 1179656 | tf_op jit(solution)/shard_map/ppermute | solution.py:643
  179.5 1.0 copy-start.6
  182.1 21.3 %collective-permute-start.19 = (bf16[768,256]{1,0:T(8,128)(2,1)}, bf16[768,256]{1,0:T(8,128)(2,1)S(1)}, u32[]{:S(2)}, u32[]{:S(2)}) collective-permute-start(bf16[768,256]{1,0:T(8,128)(2,1)} %get-tuple-element.107), channel_id=1, source_target_pairs={{2,0},{3,1},{4,6},{5,7},{0,2},{1,3},{6,4},{7,5},{10,8},{11,9},{12,... | collective-permute-start | bytes 1179656 | tf_op jit(solution)/shard_map/ppermute | solution.py:643
  198.5 26.6 %collective-permute-start.22 = (bf16[384,512]{1,0:T(8,128)(2,1)}, bf16[384,512]{1,0:T(8,128)(2,1)S(1)}, u32[]{:S(2)}, u32[]{:S(2)}) collective-permute-start(bf16[384,512]{1,0:T(8,128)(2,1)} %get-tuple-element.112), channel_id=1, source_target_pairs={{0,1},{1,0},{2,3},{3,2},{4,5},{5,4},{6,7},{7,6},{8,9},{9,8},{10,11... | collective-permute-start | bytes 1179656 | tf_op jit(solution)/shard_map/ppermute | solution.py:643
  209.9 15.2 %collective-permute-start.23 = (bf16[384,512]{1,0:T(8,128)(2,1)}, bf16[384,512]{1,0:T(8,128)(2,1)S(1)}, u32[]{:S(2)}, u32[]{:S(2)}) collective-permute-start(bf16[384,512]{1,0:T(8,128)(2,1)} %get-tuple-element.113), channel_id=1, source_target_pairs={{0,1},{1,0},{2,3},{3,2},{4,5},{5,4},{6,7},{7,6},{8,9},{9,8},{10,11... | collective-permute-start | bytes 1179656 | tf_op jit(solution)/shard_map/ppermute | solution.py:643
  211.1 14.0 %copy-start.9 = (bf16[384,512]{1,0:T(8,128)(2,1)S(1)}, bf16[384,512]{1,0:T(8,128)(2,1)}, u32[]{:S(2)}) copy-start(bf16[384,512]{1,0:T(8,128)(2,1)} %get-tuple-element.103) | copy-start | bytes 1179652
  211.1 14.0 %copy-start.10 = (bf16[384,512]{1,0:T(8,128)(2,1)S(1)}, bf16[384,512]{1,0:T(8,128)(2,1)}, u32[]{:S(2)}) copy-start(bf16[384,512]{1,0:T(8,128)(2,1)} %get-tuple-element.111) | copy-start | bytes 1179652
  (5 other events, 4.3 us)

commit v4 on v3

--- a/solution.py
+++ b/solution.py
@@ -473,56 +473,66 @@
 TILE = 64
 
 
-def sent_kernel(part, anchor, weights, momentum, *refs):
-    out, mark, start, own, moved, made, sem = refs[-7:]
+def sent_kernel(swapped, anchor, weights, momentum, *refs):
+    *outs, mark, start, own, moved, made, sem = refs[-8:]
     mark[...] = jnp.zeros_like(mark)
-    tiles = made.shape[1] // TILE
-    loads, stores = [], []
-    for tile in range(tiles):
+    tiles = made.shape[2] // TILE
+    places = [(part, tile) for part in range(PARTS) for tile in range(tiles)]
+
+    def rows(part, tile):
+        return pl.ds((part * tiles + tile) * TILE, TILE)
+
+    def loads(part, tile):
+        from_part = part + swapped[0] * (1 - 2 * part)
+        there = pl.ds(pl.multiple_of((from_part * tiles + tile) * TILE, TILE), TILE)
+        return [
+            pltpu.make_async_copy(
+                source.at[there], target.at[rows(part, tile)], sem.at[at, part * tiles + tile]
+            )
+            for at, (source, target) in enumerate(
+                ((anchor, start), (weights, own), (momentum, moved))
+            )
+        ]
+
+    def store(part, tile):
         here = pl.ds(tile * TILE, TILE)
-        there = pl.ds(pl.multiple_of((part[0] * tiles + tile) * TILE, TILE), TILE)
-        loads.append(
-            [
-                pltpu.make_async_copy(source.at[there], target.at[here], sem.at[at, tile])
-                for at, (source, target) in enumerate(
-                    ((anchor, start), (weights, own), (momentum, moved))
-                )
-            ]
+        return pltpu.make_async_copy(
+            made.at[part, :, here], outs[part].at[:, here], sem.at[3, part * tiles + tile]
         )
-        stores.append(pltpu.make_async_copy(made.at[:, here], out.at[:, here], sem.at[3, tile]))
-    for tile in range(tiles):
-        for copy in loads[tile]:
+
+    for place in places:
+        for copy in loads(*place):
             copy.start()
-    for tile in range(tiles):
-        here = slice(tile * TILE, (tile + 1) * TILE)
-        for copy in loads[tile]:
+    for part, tile in places:
+        for copy in loads(part, tile):
             copy.wait()
-        made[0, here] = moved[here].astype(made.dtype)
-        made[1, here] = (start[here] - own[here].astype(jnp.float32)).astype(made.dtype)
-        stores[tile].start()
-    for copy in stores:
-        copy.wait()
-
-
-def sent_part(part, anchor, weights, momentum, after=()):
+        here, there = rows(part, tile), pl.ds(tile * TILE, TILE)
+        made[part, 0, there] = moved[here].astype(made.dtype)
+        made[part, 1, there] = (start[here] - own[here].astype(jnp.float32)).astype(made.dtype)
+        store(part, tile).start()
+    for place in places:
+        store(*place).wait()
+
+
+def sent_parts(swapped, anchor, weights, momentum, after=()):
     rows, columns = anchor.shape
-    size = (rows // PARTS, columns)
+    part = jax.ShapeDtypeStruct((2, rows // PARTS, columns), jnp.bfloat16)
     return pl.pallas_call(
         sent_kernel,
         in_specs=[SMEM] + [HBM] * (3 + len(after)),
-        out_specs=(HBM, VMEM),
-        out_shape=(jax.ShapeDtypeStruct((2,) + size, jnp.bfloat16), MARK),
+        out_specs=(HBM, HBM, VMEM),
+        out_shape=(part, part, MARK),
         scratch_shapes=[
-            pltpu.VMEM(size, jnp.float32),
-            pltpu.VMEM(size, weights.dtype),
-            pltpu.VMEM(size, jnp.float32),
-            pltpu.VMEM((2,) + size, jnp.bfloat16),
-            pltpu.SemaphoreType.DMA((4, size[0] // TILE)),
+            pltpu.VMEM(anchor.shape, jnp.float32),
+            pltpu.VMEM(anchor.shape, weights.dtype),
+            pltpu.VMEM(anchor.shape, jnp.float32),
+            pltpu.VMEM((PARTS,) + part.shape, jnp.bfloat16),
+            pltpu.SemaphoreType.DMA((4, rows // TILE)),
         ],
         compiler_params=pltpu.CompilerParams(vmem_limit_bytes=60 * MIB),
         cost_estimate=SMALL,
-        name="sent_part",
-    )(part, anchor, weights, momentum, *after)
+        name="sent_parts",
+    )(swapped, anchor, weights, momentum, *after)
 
 
 def relay_kernel(onward, came, piece, *refs):
@@ -550,12 +560,11 @@
     )(onward, came, piece, *after)
 
 
-def outer_kernel(table, anchor, weights, momentum, *refs):
-    came = refs[:4]
-    new_params, new_momentum, mark, start, own, moved, mate, sem = refs[-8:]
-    mark[...] = jnp.zeros_like(mark)
-    rows = start.shape[0]
-    tiles = rows // TILE
+def outer_step_of(table, arrays, came, outs, scratch):
+    anchor, weights, momentum = arrays
+    new_params, new_momentum = outs
+    start, own, moved, mate, sem = scratch
+    tiles = start.shape[0] // TILE
     per_part = tiles // PARTS
 
     def mate_copy(tile, source):
@@ -563,70 +572,84 @@
         here = pl.ds(tile * TILE, TILE)
         return pltpu.make_async_copy(source.at[:, there], mate.at[:, here], sem.at[3, tile])
 
-    loads, stores = [], []
-    for tile in range(tiles):
+    def loads(tile):
         here = pl.ds(tile * TILE, TILE)
-        loads.append(
-            [
-                pltpu.make_async_copy(source.at[here], target.at[here], sem.at[at, tile])
-                for at, (source, target) in enumerate(
-                    ((anchor, start), (weights, own), (momentum, moved))
-                )
-            ]
+        pairs = ((anchor, start), (weights, own), (momentum, moved))
+        return [
+            pltpu.make_async_copy(source.at[here], target.at[here], sem.at[at, tile])
+            for at, (source, target) in enumerate(pairs)
+        ]
+
+    def stores(tile):
+        here = pl.ds(tile * TILE, TILE)
+        pairs = ((start, new_params), (moved, new_momentum))
+        return [
+            pltpu.make_async_copy(source.at[here], target.at[here], sem.at[4 + at, tile])
+            for at, (source, target) in enumerate(pairs)
+        ]
+
+    def begin():
+        for tile in range(tiles):
+            for copy in loads(tile):
+                copy.start()
+            for at, source in enumerate(came):
+
+                @pl.when(table[tile // per_part] == at)
+                def _():
+                    mate_copy(tile, source).start()
+
+    def finish():
+        for tile in range(tiles):
+            for copy in loads(tile):
+                copy.wait()
+            mate_copy(tile, came[0]).wait()
+            here = slice(tile * TILE, (tile + 1) * TILE)
+            begun = start[here]
+            pseudo = begun - own[here].astype(jnp.float32)
+            grad_mean = 0.5 * (pseudo + mate[1, here].astype(jnp.float32))
+            mom_mean = 0.5 * (moved[here] + mate[0, here].astype(jnp.float32))
+            made = MOMENTUM_RATE * mom_mean + grad_mean
+            moved[here] = made
+            start[here] = begun - OUTER_RATE * (grad_mean + MOMENTUM_RATE * made)
+            for copy in stores(tile):
+                copy.start()
+        for tile in range(tiles):
+            for copy in stores(tile):
+                copy.wait()
+
+    return begin, finish
+
+
+def outer_update(choice, arrays, came, after=()):
+    shape = arrays[0].shape
+    full = jax.ShapeDtypeStruct(shape, jnp.float32)
+
+    def kernel(choice, *refs):
+        arrays, came, refs = refs[:3], refs[3:7], refs[7 + len(after) :]
+        new_params, new_momentum, mark, *scratch = refs
+        mark[...] = jnp.zeros_like(mark)
+        begin, finish = outer_step_of(
+            choice, arrays, came, (new_params, new_momentum), scratch
         )
-        stores.append(
-            [
-                pltpu.make_async_copy(source.at[here], target.at[here], sem.at[4 + at, tile])
-                for at, (source, target) in enumerate(((start, new_params), (moved, new_momentum)))
-            ]
-        )
-    for tile in range(tiles):
-        for copy in loads[tile]:
-            copy.start()
-        for at, source in enumerate(came):
-
-            @pl.when(table[tile // per_part] == at)
-            def _():
-                mate_copy(tile, source).start()
-
-    for tile in range(tiles):
-        for copy in loads[tile]:
-            copy.wait()
-        mate_copy(tile, came[0]).wait()
-        here = slice(tile * TILE, (tile + 1) * TILE)
-        begun = start[here]
-        pseudo = begun - own[here].astype(jnp.float32)
-        grad_mean = 0.5 * (pseudo + mate[1, here].astype(jnp.float32))
-        mom_mean = 0.5 * (moved[here] + mate[0, here].astype(jnp.float32))
-        made = MOMENTUM_RATE * mom_mean + grad_mean
-        moved[here] = made
-        start[here] = begun - OUTER_RATE * (grad_mean + MOMENTUM_RATE * made)
-        for copy in stores[tile]:
-            copy.start()
-    for tile in range(tiles):
-        for copy in stores[tile]:
-            copy.wait()
-
-
-def outer_update(table, anchor, weights, momentum, came, after=()):
-    size = anchor.shape
-    full = jax.ShapeDtypeStruct(size, jnp.float32)
-    return pl.pallas_call(
-        outer_kernel,
+        begin()
+        finish()
+
+    return pl.pallas_call(
+        kernel,
         in_specs=[SMEM] + [HBM] * (3 + len(came) + len(after)),
         out_specs=(HBM, HBM, VMEM),
         out_shape=(full, full, MARK),
         scratch_shapes=[
-            pltpu.VMEM(size, jnp.float32),
-            pltpu.VMEM(size, weights.dtype),
-            pltpu.VMEM(size, jnp.float32),
-            pltpu.VMEM((2,) + size, jnp.bfloat16),
-            pltpu.SemaphoreType.DMA((6, size[0] // TILE)),
+            pltpu.VMEM(shape, jnp.float32),
+            pltpu.VMEM(shape, arrays[1].dtype),
+            pltpu.VMEM(shape, jnp.float32),
+            pltpu.VMEM((2,) + shape, jnp.bfloat16),
+            pltpu.SemaphoreType.DMA((6, shape[0] // TILE)),
         ],
         compiler_params=pltpu.CompilerParams(vmem_limit_bytes=60 * MIB),
         cost_estimate=SMALL,
         name="outer_update",
-    )(table, anchor, weights, momentum, *came, *after)
+    )(choice, *arrays, *came, *after)
 
 
 def line_step(partner, tokens, positions, weights, anchor, momentum):
@@ -646,14 +669,15 @@
     swap = [(f, f ^ 1) for f in range(LINE * CORES)]
     inward = [(a * CORES + c, b * CORES + c) for a, b in ((0, 1), (last, last - 1)) for c in cores]
     across = [(a * CORES + c, b * CORES + c) for a, b in ((1, 2), (2, 1)) for c in cores]
-    outward = [(b, a) for a, b in inward] + inward
+    outward = [(b, a) for a, b in inward]
+    both_ways = inward + outward
     across += [(a * CORES + c, a * CORES + 1 - c) for a in (0, last) for c in cores]
 
     other_rows = over(own_rows, across)
     sibling_rows = over(own_rows, swap)
     lead = (chip < LINE // 2).astype(jnp.int32)
     handed, mark = hand_tokens(rows, lead[None])
-    handed = over(handed, inward)
+    handed = over(handed, both_ways)
 
     distance = partner[0]
     part_rows = depth // PARTS
@@ -661,10 +685,7 @@
     along = [[(r, r ^ 1) for r in range(SQUARE)], [(r, r ^ 2) for r in range(SQUARE)]]
     values = (start, own_rows, moved)
     swapped = (distance == 2).astype(jnp.int32)
-    first = []
-    for part in (swapped, 1 - swapped):
-        made, mark = sent_part(part[None], *values, (mark,))
-        first.append(made)
+    *first, mark = sent_parts(swapped[None], *values, (mark,))
     came = [lax.ppermute(first[at], "replica", along[at]) for at in range(2)]
     table = jnp.stack([jnp.where(distance == 3, 3, distance - 1), jnp.where(distance == 2, 3, 2)])
 
@@ -718,7 +739,7 @@
         result, mark = project(
             (j,), spots, pairs, theirs, HANDED, wide, ((far[j],),), jnp.bfloat16, after, rider
         )
-        backs.append(over(result, outward))
+        backs.append(over(result, both_ways))
         return mark
 
     def own(js, *after):
@@ -734,25 +755,25 @@
         contexts.append((left, over(right, swap)))
         return mark
 
-    mark = stage(1, mark, *came)
     for at in range(2):
         made, mark = relay(onward, came[1 - at], first[1 - at], (mark,))
         came.append(lax.ppermute(made, "replica", along[at]))
+    mark = stage(1, mark)
     mark = product(0, mark)
     mark = own((0,), mark)
     mark = stage(2, mark)
     mark = product(1, mark)
+    mark = own((1,), mark)
     made, mark = unpack(backs[0], depth, (mark, far[2]))
     near.append(made)
     far.append(over(made, across))
     mark = product(2, mark)
-    mark = own((1,), mark)
+    *held, mark = keep_keys(spots, owns[0], backs[0], cosine, sine, (mark,))
     mark = product(3, mark, backs[1])
-    *held, mark = keep_keys(spots, owns[0], backs[0], cosine, sine, (mark,))
     mark = attention(1, (1,), mark)
     mark = own((2, 3), mark)
-    mark = attention(2, (2, 3), mark, came[2], came[3])
-    new_params, new_momentum, mark = outer_update(table, start, own_rows, moved, came, (mark,))
+    mark = attention(2, (2, 3), mark)
+    new_params, new_momentum, mark = outer_update(table, values, came, (mark,))
 
     mine = jnp.concatenate([first for first, _ in contexts], 1)
     came = jnp.concatenate([second for _, second in contexts], 1)

time: 227 us -> 215 us (0.947)
  waiting for transfers between devices: 67.8 us -> 60.4 us
  starting transfers between devices: 54.5 us -> 51.2 us
    ppermute x20, waiting for transfers between devices: 61.9 us -> 57.9 us  [over(): return lax.ppermute(value, 'fsdp', pairs)]
    ppermute x2, waiting for transfers between devices: 5.96 us -> 2.49 us  [line_step(): came = [lax.ppermute(first[at], 'replica', along[at]) for at in range(2)]]
    ppermute x20, starting transfers between devices: 48.3 us -> 45.2 us  [over(): return lax.ppermute(value, 'fsdp', pairs)]
    pallas_call x3 -> x2, Pallas kernels: 25.1 us -> 23.1 us  [the longest x1 14 us: outer_update(): pl.pallas_call(kernel, in_specs=[SMEM] + [HBM] * (3 + len(came) + len(aft...]
  transfers between devices with their start and end apart: 24 -> 24, of which waited for: 5 -> 5; matrix products, arithmetic and copies ran while one was open for 3% -> 3% of each run, Pallas kernels for 40% -> 42%
where the time goes in v4:
time: 215 us; the launch traced here: 214 us
  Pallas kernels  89.4 us (42%)
  waiting for transfers between devices  60.4 us (28%)
  starting transfers between devices  51.2 us (24%)
  local copies, waits for them, and re-layouts  7.16 us (3%)
  other arithmetic  4.71 us (2%)
    ppermute x20, waiting for transfers between devices, over(): return lax.ppermute(value, 'fsdp', pairs)  57.9 us
    ppermute x20, starting transfers between devices, over(): return lax.ppermute(value, 'fsdp', pairs)  45.2 us
    pallas_call x7, Pallas kernels, project(): pl.pallas_call(lambda *refs: project_kernel(span, len(wide), len(chunks),...  22.3 us
    pallas_call x1, Pallas kernels, outer_update(): pl.pallas_call(kernel, in_specs=[SMEM] + [HBM] * (3 + len(came) + len(aft...  14 us
    pallas_call x4, Pallas kernels, pack(): pl.pallas_call(lambda *refs: pack_kernel(first, count, *refs), in_specs=[...  12.7 us
    pallas_call x2, Pallas kernels, attend_chunks(): pl.pallas_call(lambda *refs: attend_kernel(heads, group, len(came), *refs...  11.2 us
    pallas_call x1, Pallas kernels, sent_parts(): pl.pallas_call(sent_kernel, in_specs=[SMEM] + [HBM] * (3 + len(after)), o...  9.06 us
    pallas_call x2, Pallas kernels, relay(): pl.pallas_call(relay_kernel, in_specs=[SMEM] + [HBM] * (2 + len(after)),...  7.43 us
  transfers between devices with their start and end apart: 24, of which 5 were waited for; matrix products, arithmetic and copies ran while one was open for 3% of the time, Pallas kernels for 42%

profile of v4, /device:TPU:0, one launch (start us, length us, event | category | flops | bytes accessed | tf_op | source)
XLA Modules:
  0.0 214.0 jit_solution(18267481069611683337)
XLA Ops:
  1.2 3.2 %hand_tokens.1 = (bf16[384,3072]{1,0:T(8,128)(2,1)}, f32[8,128]{1,0:T(8,128)}) custom-call(s32[1]{0:T(128)} %bitcast.14.lead, bf16[384,4096]{1,0:T(8,128)(2,1)} %bitcast.41), custom_call_target="tpu_custom_call" | custom-call | flops 1 | bytes 1 | tf_op jit(solution)/shard_map/hand_tokens/pallas_call | solution.py:156
  4.5 4.2 %collective-permute-start.3 = (bf16[384,3072]{1,0:T(8,128)(2,1)}, bf16[384,3072]{1,0:T(8,128)(2,1)}, u32[]{:S(2)}, u32[]{:S(2)}) collective-permute-start(bf16[384,3072]{1,0:T(8,128)(2,1)} %get-tuple-element.59), channel_id=1, source_target_pairs={{0,2},{1,3},{6,4},{7,5},{2,0},{3,1},{4,6},{5,7},{8,10},{9,11},{14,... | collective-permute-start | bytes 7077896 | tf_op jit(solution)/shard_map/ppermute | solution.py:666
  8.7 9.1 %sent_parts.1 = (bf16[2,256,3072]{2,1,0:T(8,128)(2,1)}, bf16[2,256,3072]{2,1,0:T(8,128)(2,1)}, f32[8,128]{1,0:T(8,128)}) custom-call(s32[1]{0:T(128)S(6)} %convert_element_type.20.swapped, f32[512,3072]{1,0:T(8,128)} %bitcast.46, bf16[512,3072]{1,0:T(8,128)(2,1)} %bitcast.28, f32[512,3072]{1,0:T(8,128)} %bitcast.48, f32[8,128]{1,0:T(8,128)} %get-tuple-element.60.refs_0_), custom_call_target="tpu_custom_call" | custom-call | flops 1 | bytes 1 | tf_op jit(solution)/shard_map/sent_parts/pallas_call | solution.py:520
  22.6 3.2 %pack.4 = (bf16[2,512,512]{2,1,0:T(8,128)(2,1)}, f32[8,128]{1,0:T(8,128)}) custom-call(s32[6]{0:T(128)} %stack.70.refs_0_.refs_1_, bf16[512,3072]{1,0:T(8,128)(2,1)} %bitcast.29, bf16[512,3072]{1,0:T(8,128)(2,1)} %copy-done, f32[8,128]{1,0:T(8,128)} %get-tuple-element.61.refs_3_), custom_call_target="tpu_custom_call" | custom-call | flops 1 | bytes 1 | tf_op jit(solution)/shard_map/pack/pallas_call | solution.py:185
  25.8 2.0 collective-permute-start.5
  30.5 3.3 %pack.5 = (bf16[2,512,512]{2,1,0:T(8,128)(2,1)}, f32[8,128]{1,0:T(8,128)}) custom-call(s32[6]{0:T(128)} %stack.70.refs_0_.refs_1_, bf16[512,3072]{1,0:T(8,128)(2,1)} %bitcast.30, bf16[512,3072]{1,0:T(8,128)(2,1)} %copy-done, f32[8,128]{1,0:T(8,128)} %get-tuple-element.62.refs_3_), custom_call_target="tpu_custom_call" | custom-call | flops 1 | bytes 1 | tf_op jit(solution)/shard_map/pack/pallas_call | solution.py:185
  33.8 3.1 %pack.6 = (bf16[2,512,256]{2,1,0:T(8,128)(2,1)}, f32[8,128]{1,0:T(8,128)}) custom-call(s32[6]{0:T(128)} %stack.70.refs_0_.refs_1_, bf16[512,3072]{1,0:T(8,128)(2,1)} %bitcast.31, bf16[512,3072]{1,0:T(8,128)(2,1)} %copy-done, f32[8,128]{1,0:T(8,128)} %get-tuple-element.63.refs_3_), custom_call_target="tpu_custom_call" | custom-call | flops 1 | bytes 1 | tf_op jit(solution)/shard_map/pack/pallas_call | solution.py:185
  36.9 3.1 %pack.7 = (bf16[2,512,256]{2,1,0:T(8,128)(2,1)}, f32[8,128]{1,0:T(8,128)}) custom-call(s32[6]{0:T(128)} %stack.70.refs_0_.refs_1_, bf16[512,3072]{1,0:T(8,128)(2,1)} %bitcast.32, bf16[512,3072]{1,0:T(8,128)(2,1)} %copy-done, f32[8,128]{1,0:T(8,128)} %get-tuple-element.64.refs_3_), custom_call_target="tpu_custom_call" | custom-call | flops 1 | bytes 1 | tf_op jit(solution)/shard_map/pack/pallas_call | solution.py:185
  39.9 20.7 %collective-permute-done.3.refs_0_ = bf16[384,3072]{1,0:T(8,128)(2,1)} collective-permute-done((bf16[384,3072]{1,0:T(8,128)(2,1)}, bf16[384,3072]{1,0:T(8,128)(2,1)}, u32[]{:S(2)}, u32[]{:S(2)}) %collective-permute-start.3) | collective-permute-done | bytes 2359328 | tf_op jit(solution)/shard_map/ppermute | solution.py:666
  61.2 21.1 %collective-permute-done.5.refs_2_.refs_0_ = bf16[2,512,512]{2,1,0:T(8,128)(2,1)S(1)} collective-permute-done((bf16[2,512,512]{2,1,0:T(8,128)(2,1)}, bf16[2,512,512]{2,1,0:T(8,128)(2,1)S(1)}, u32[]{:S(2)}, u32[]{:S(2)}) %collective-permute-start.5) | collective-permute-done | bytes 1048608 | tf_op jit(solution)/shard_map/ppermute | solution.py:666
  85.6 2.5 %collective-permute-done.10.came.refs_4_ = bf16[2,256,3072]{2,1,0:T(8,128)(2,1)} collective-permute-done((bf16[2,256,3072]{2,1,0:T(8,128)(2,1)}, bf16[2,256,3072]{2,1,0:T(8,128)(2,1)}, u32[]{:S(2)}, u32[]{:S(2)}) %collective-permute-start.10) | collective-permute-done | bytes 3145760 | tf_op jit(solution)/shard_map/ppermute | solution.py:689
  88.1 3.2 %collective-permute-start.7 = (bf16[2,512,512]{2,1,0:T(8,128)(2,1)}, bf16[2,512,512]{2,1,0:T(8,128)(2,1)}, u32[]{:S(2)}, u32[]{:S(2)}) collective-permute-start(bf16[2,512,512]{2,1,0:T(8,128)(2,1)} %get-tuple-element.72), channel_id=1, source_target_pairs={{0,2},{1,3},{6,4},{7,5},{8,10},{9,11},{14,12},{15,13},{16,18},{17,... | collective-permute-start | bytes 3145736 | tf_op jit(solution)/shard_map/ppermute | solution.py:666
  91.3 3.7 %relay.2 = (bf16[2,256,3072]{2,1,0:T(8,128)(2,1)}, f32[8,128]{1,0:T(8,128)}) custom-call(s32[1]{0:T(128)S(6)} %convert_element_type.22.onward, bf16[2,256,3072]{2,1,0:T(8,128)(2,1)} %collective-permute-done.10.came.refs_4_, bf16[2,256,3072]{2,1,0:T(8,128)(2,1)} %get-tuple-element.75.piece, ...), custom_call_target="tpu_custom_call", output_to_operand_aliasing={{0}: (2, {})} | custom-call | flops 1 | bytes 1 | tf_op jit(solution)/shard_map/relay/pallas_call | solution.py:550
  95.0 3.7 %relay.3 = (bf16[2,256,3072]{2,1,0:T(8,128)(2,1)}, f32[8,128]{1,0:T(8,128)}) custom-call(s32[1]{0:T(128)S(6)} %convert_element_type.22.onward, bf16[2,256,3072]{2,1,0:T(8,128)(2,1)} %collective-permute-done.9.came.refs_3_, bf16[2,256,3072]{2,1,0:T(8,128)(2,1)} %get-tuple-element.74.piece, ...), custom_call_target="tpu_custom_call", output_to_operand_aliasing={{0}: (2, {})} | custom-call | flops 1 | bytes 1 | tf_op jit(solution)/shard_map/relay/pallas_call | solution.py:550
  98.8 14.5 %collective-permute-done.7.refs_0_ = bf16[2,512,512]{2,1,0:T(8,128)(2,1)} collective-permute-done((bf16[2,512,512]{2,1,0:T(8,128)(2,1)}, bf16[2,512,512]{2,1,0:T(8,128)(2,1)}, u32[]{:S(2)}, u32[]{:S(2)}) %collective-permute-start.7) | collective-permute-done | bytes 1048608 | tf_op jit(solution)/shard_map/ppermute | solution.py:666
  117.5 5.7 %collective-permute-start.13 = (bf16[2,512,256]{2,1,0:T(8,128)(2,1)}, bf16[2,512,256]{2,1,0:T(8,128)(2,1)}, u32[]{:S(2)}, u32[]{:S(2)}) collective-permute-start(bf16[2,512,256]{2,1,0:T(8,128)(2,1)} %get-tuple-element.82), channel_id=1, source_target_pairs={{0,2},{1,3},{6,4},{7,5},{8,10},{9,11},{14,12},{15,13},{16,18},{17,... | collective-permute-start | bytes 1572872 | tf_op jit(solution)/shard_map/ppermute | solution.py:666
  123.9 2.8 %project.7 = (bf16[768,512]{1,0:T(8,128)(2,1)}, f32[8,128]{1,0:T(8,128)}) custom-call(s32[10]{0:T(128)} %concatenate.46.refs_0_.table, s32[6]{0:T(128)} %stack.70.refs_0_.refs_1_, bf16[384,3072]{1,0:T(8,128)(2,1)} %get-tuple-element.79.refs_2_, bf16[384,3072]{1,0:T(8,128)(2,1)} %collective-permute-done.12.refs_3_, bf16[512,3072]{1,0:T(8,128)(2,1)} %bitcast.33, ...), custom_call_target="tpu_custom_call" | custom-call | flops 1 | bytes 1 | tf_op jit(solution)/shard_map/project/pallas_call | solution.py:315
  126.7 2.0 collective-permute-start.14
  128.7 4.7 %project.8 = (f32[768,512]{1,0:T(8,128)}, f32[8,128]{1,0:T(8,128)}) custom-call(s32[10]{0:T(128)} %concatenate.46.refs_0_.table, s32[6]{0:T(128)} %stack.70.refs_0_.refs_1_, bf16[384,4096]{1,0:T(8,128)(2,1)} %bitcast.43, bf16[384,4096]{1,0:T(8,128)(2,1)} %collective-permute-done.refs_3_, bf16[512,3072]{1,0:T(8,128)(2,1)} %bitcast.34, ...), custom_call_target="tpu_custom_call" | custom-call | flops 1 | bytes 1 | tf_op jit(solution)/shard_map/project/pallas_call | solution.py:315
  133.4 1.6 collective-permute-done.13.refs_0_
  135.6 1.8 project.9
  137.4 13.2 %collective-permute-start.16 = (bf16[768,512]{1,0:T(8,128)(2,1)}, bf16[768,512]{1,0:T(8,128)(2,1)S(1)}, u32[]{:S(2)}, u32[]{:S(2)}) collective-permute-start(bf16[768,512]{1,0:T(8,128)(2,1)} %get-tuple-element.97), channel_id=1, source_target_pairs={{0,2},{1,3},{6,4},{7,5},{2,0},{3,1},{4,6},{5,7},{8,10},{9,11},{14,... | collective-permute-start | bytes 2359304 | tf_op jit(solution)/shard_map/ppermute | solution.py:666
  150.5 4.7 %project.10 = (f32[768,512]{1,0:T(8,128)}, f32[8,128]{1,0:T(8,128)}) custom-call(s32[10]{0:T(128)} %concatenate.46.refs_0_.table, s32[6]{0:T(128)} %stack.70.refs_0_.refs_1_, bf16[384,4096]{1,0:T(8,128)(2,1)} %bitcast.44, bf16[384,4096]{1,0:T(8,128)(2,1)} %collective-permute-done.refs_3_, bf16[512,3072]{1,0:T(8,128)(2,1)} %bitcast.36, ...), custom_call_target="tpu_custom_call" | custom-call | flops 1 | bytes 1 | tf_op jit(solution)/shard_map/project/pallas_call | solution.py:315
  156.4 2.4 %unpack.1 = (bf16[2,512,256]{2,1,0:T(8,128)(2,1)}, f32[8,128]{1,0:T(8,128)}) custom-call(bf16[768,512]{1,0:T(8,128)(2,1)} %copy-done.4, f32[8,128]{1,0:T(8,128)} %get-tuple-element.92.refs_0_, bf16[2,512,256]{2,1,0:T(8,128)(2,1)} %copy-done.3), custom_call_target="tpu_custom_call" | custom-call | flops 1 | bytes 1 | tf_op jit(solution)/shard_map/unpack/pallas_call | solution.py:353
  158.8 1.8 project.11
  160.6 8.4 %collective-permute-start.18 = (bf16[768,256]{1,0:T(8,128)(2,1)}, bf16[768,256]{1,0:T(8,128)(2,1)S(1)}, u32[]{:S(2)}, u32[]{:S(2)}) collective-permute-start(bf16[768,256]{1,0:T(8,128)(2,1)} %get-tuple-element.104), channel_id=1, source_target_pairs={{0,2},{1,3},{6,4},{7,5},{2,0},{3,1},{4,6},{5,7},{8,10},{9,11},{14,... | collective-permute-start | bytes 1179656 | tf_op jit(solution)/shard_map/ppermute | solution.py:666
  169.0 3.0 %keep_keys.1 = (bf16[2,2,384,128]{3,2,1,0:T(8,128)(2,1)}, bf16[2,2,384,128]{3,2,1,0:T(8,128)(2,1)}, f32[8,128]{1,0:T(8,128)}) custom-call(s32[10]{0:T(128)} %concatenate.46.refs_0_.table, f32[768,512]{1,0:T(8,128)} %get-tuple-element.89.own, bf16[768,512]{1,0:T(8,128)(2,1)} %copy-done.4, f32[2,384,128]{2,1,0:T(8,128)} %get-tuple-element.120.refs_2_.cosine.refs_1_, ...), custom_call_target="tpu_custom_call" | custom-call | flops 1 | bytes 1 | tf_op jit(solution)/shard_map/keep_keys/pallas_call | solution.py:401
  174.7 4.8 %collective-permute-start.19 = (bf16[768,256]{1,0:T(8,128)(2,1)}, bf16[768,256]{1,0:T(8,128)(2,1)S(1)}, u32[]{:S(2)}, u32[]{:S(2)}) collective-permute-start(bf16[768,256]{1,0:T(8,128)(2,1)} %get-tuple-element.105), channel_id=1, source_target_pairs={{0,2},{1,3},{6,4},{7,5},{2,0},{3,1},{4,6},{5,7},{8,10},{9,11},{14,... | collective-permute-start | bytes 1179656 | tf_op jit(solution)/shard_map/ppermute | solution.py:666
  180.4 5.6 %attend_chunks.2 = (bf16[384,512]{1,0:T(8,128)(2,1)}, bf16[384,512]{1,0:T(8,128)(2,1)}, f32[8,128]{1,0:T(8,128)}) custom-call(f32[768,512]{1,0:T(8,128)} %get-tuple-element.88.refs_0_, f32[2,384,128]{2,1,0:T(8,128)} %get-tuple-element.120.refs_2_.cosine.refs_1_, f32[2,384,128]{2,1,0:T(8,128)} %get-tuple-element.121.refs_3_.sine.refs_2_, ...), custom_call_target="tpu_custom_call" | custom-call | flops 1 | bytes 1 | tf_op jit(solution)/shard_map/attend_chunks/pallas_call | solution.py:458
  186.1 4.9 %project.13 = (f32[768,512]{1,0:T(8,128)}, f32[8,128]{1,0:T(8,128)}) custom-call(s32[10]{0:T(128)} %concatenate.46.refs_0_.table, s32[6]{0:T(128)} %stack.70.refs_0_.refs_1_, bf16[384,4096]{1,0:T(8,128)(2,1)} %bitcast.45, bf16[384,4096]{1,0:T(8,128)(2,1)} %collective-permute-done.refs_3_, bf16[512,3072]{1,0:T(8,128)(2,1)} %bitcast.39, ...), custom_call_target="tpu_custom_call" | custom-call | flops 1 | bytes 1 | tf_op jit(solution)/shard_map/project/pallas_call | solution.py:315
  191.9 5.6 %attend_chunks.3 = (bf16[384,512]{1,0:T(8,128)(2,1)}, bf16[384,512]{1,0:T(8,128)(2,1)}, f32[8,128]{1,0:T(8,128)}) custom-call(f32[768,512]{1,0:T(8,128)} %get-tuple-element.103.refs_0_, f32[2,384,128]{2,1,0:T(8,128)} %get-tuple-element.120.refs_2_.cosine.refs_1_, f32[2,384,128]{2,1,0:T(8,128)} %get-tuple-element.121.refs_3_.sine.refs_2_, ...), custom_call_target="tpu_custom_call" | custom-call | flops 1 | bytes 1 | tf_op jit(solution)/shard_map/attend_chunks/pallas_call | solution.py:458
  198.6 14.0 %outer_update.1 = (f32[512,3072]{1,0:T(8,128)}, f32[512,3072]{1,0:T(8,128)}, f32[8,128]{1,0:T(8,128)}) custom-call(s32[2]{0:T(128)} %pad_add_fusion.1.choice, f32[512,3072]{1,0:T(8,128)} %bitcast.47, bf16[512,3072]{1,0:T(8,128)(2,1)} %bitcast.40, f32[512,3072]{1,0:T(8,128)} %bitcast.49, bf16[2,256,3072]{2,1,0:T(8,128)(2,1)} %collective-permute-done.9.came.refs_3_, ...), custom_call_target="tpu_custom_call" | custom-call | flops 1 | bytes 1 | tf_op jit(solution)/shard_map/outer_update/pallas_call | solution.py:637
  (81 shorter events, 25.5 us)
Async XLA Ops:
  0.6 8.1 %copy-start.12 = (s32[4]{0:T(128)S(1)}, s32[4]{0:T(128)}, u32[]{:S(2)}) copy-start(s32[4]{0:T(128)} %param.8) | copy-start | bytes 52
  0.6 20.3 %collective-permute-start.1 = (bf16[512,3072]{1,0:T(8,128)(2,1)}, bf16[512,3072]{1,0:T(8,128)(2,1)S(1)}, u32[]{:S(2)}, u32[]{:S(2)}) collective-permute-start(bf16[512,3072]{1,0:T(8,128)(2,1)} %bitcast.26), channel_id=1, source_target_pairs={{0,1},{1,0},{2,3},{3,2},{4,5},{5,4},{6,7},{7,6},{8,9},{9,8},{10,11... | collective-permute-start | bytes 9437192 | tf_op jit(solution)/shard_map/ppermute | solution.py:666
  1.2 60.0 %collective-permute-start.2 = (bf16[512,3072]{1,0:T(8,128)(2,1)}, bf16[512,3072]{1,0:T(8,128)(2,1)}, u32[]{:S(2)}, u32[]{:S(2)}) collective-permute-start(bf16[512,3072]{1,0:T(8,128)(2,1)} %bitcast.27), channel_id=1, source_target_pairs={{2,4},{3,5},{4,2},{5,3},{0,1},{1,0},{6,7},{7,6},{10,12},{11,13},{1... | collective-permute-start | bytes 9437192 | tf_op jit(solution)/shard_map/ppermute | solution.py:666
  4.5 56.1 %collective-permute-start.3 = (bf16[384,3072]{1,0:T(8,128)(2,1)}, bf16[384,3072]{1,0:T(8,128)(2,1)}, u32[]{:S(2)}, u32[]{:S(2)}) collective-permute-start(bf16[384,3072]{1,0:T(8,128)(2,1)} %get-tuple-element.59), channel_id=1, source_target_pairs={{0,2},{1,3},{6,4},{7,5},{2,0},{3,1},{4,6},{5,7},{8,10},{9,11},{14,... | collective-permute-start | bytes 7077896 | tf_op jit(solution)/shard_map/ppermute | solution.py:666
  8.7 12.2 %copy-start.11 = (s32[1,384]{1,0:T(1,128)S(1)}, s32[1,384]{1,0:T(1,128)}, u32[]{:S(2)}) copy-start(s32[1,384]{1,0:T(1,128)} %param.7) | copy-start | bytes 4612
  17.8 70.3 %collective-permute-start.10 = (bf16[2,256,3072]{2,1,0:T(8,128)(2,1)}, bf16[2,256,3072]{2,1,0:T(8,128)(2,1)}, u32[]{:S(2)}, u32[]{:S(2)}) collective-permute-start(bf16[2,256,3072]{2,1,0:T(8,128)(2,1)} %get-tuple-element.75.piece), channel_id=1, source_target_pairs={{0,16},{8,24},{16,0},{24,8},{1,17},{9,25},{17,1},{25,9},{2,18},{10... | collective-permute-start | bytes 9437192 | tf_op jit(solution)/shard_map/ppermute | solution.py:689
  19.4 71.9 %collective-permute-start.9 = (bf16[2,256,3072]{2,1,0:T(8,128)(2,1)}, bf16[2,256,3072]{2,1,0:T(8,128)(2,1)}, u32[]{:S(2)}, u32[]{:S(2)}) collective-permute-start(bf16[2,256,3072]{2,1,0:T(8,128)(2,1)} %get-tuple-element.74.piece), channel_id=1, source_target_pairs={{0,8},{8,0},{16,24},{24,16},{1,9},{9,1},{17,25},{25,17},{2,10},{10... | collective-permute-start | bytes 9437192 | tf_op jit(solution)/shard_map/ppermute | solution.py:689
  20.9 1.7 copy-start
  20.9 4.9 %collective-permute-start.4 = (s32[384]{0:T(512)S(1)}, s32[384]{0:T(512)S(1)}, u32[]{:S(2)}, u32[]{:S(2)}) collective-permute-start(s32[384]{0:T(512)S(1)} %reduce), channel_id=1, source_target_pairs={{0,1},{1,0},{2,3},{3,2},{4,5},{5,4},{6,7},{7,6},{8,9},{9,8},{10,11... | collective-permute-start | bytes 4616 | tf_op jit(solution)/shard_map/ppermute | solution.py:666
  25.8 56.5 %collective-permute-start.5 = (bf16[2,512,512]{2,1,0:T(8,128)(2,1)}, bf16[2,512,512]{2,1,0:T(8,128)(2,1)S(1)}, u32[]{:S(2)}, u32[]{:S(2)}) collective-permute-start(bf16[2,512,512]{2,1,0:T(8,128)(2,1)} %get-tuple-element.67), channel_id=1, source_target_pairs={{0,2},{1,3},{6,4},{7,5},{8,10},{9,11},{14,12},{15,13},{16,18},{17,... | collective-permute-start | bytes 3145736 | tf_op jit(solution)/shard_map/ppermute | solution.py:666
  83.9 33.6 %collective-permute-start.6 = (bf16[512,3072]{1,0:T(8,128)(2,1)}, bf16[512,3072]{1,0:T(8,128)(2,1)S(1)}, u32[]{:S(2)}, u32[]{:S(2)}) collective-permute-start(bf16[512,3072]{1,0:T(8,128)(2,1)} %get-tuple-element.68.refs_6_), channel_id=1, source_target_pairs={{0,1},{1,0},{2,3},{3,2},{4,5},{5,4},{6,7},{7,6},{8,9},{9,8},{10,11... | collective-permute-start | bytes 9437192 | tf_op jit(solution)/shard_map/ppermute | solution.py:666
  83.9 33.0 %collective-permute-start.12 = (bf16[384,3072]{1,0:T(8,128)(2,1)}, bf16[384,3072]{1,0:T(8,128)(2,1)}, u32[]{:S(2)}, u32[]{:S(2)}) collective-permute-start(bf16[384,3072]{1,0:T(8,128)(2,1)} %get-tuple-element.79.refs_2_), channel_id=1, source_target_pairs={{0,1},{1,0},{2,3},{3,2},{4,5},{5,4},{6,7},{7,6},{8,9},{9,8},{10,11... | collective-permute-start | bytes 7077896 | tf_op jit(solution)/shard_map/ppermute | solution.py:666
  84.4 42.3 %collective-permute-start = (bf16[384,4096]{1,0:T(8,128)(2,1)}, bf16[384,4096]{1,0:T(8,128)(2,1)}, u32[]{:S(2)}, u32[]{:S(2)}) collective-permute-start(bf16[384,4096]{1,0:T(8,128)(2,1)} %bitcast.42), channel_id=1, source_target_pairs={{0,1},{1,0},{2,3},{3,2},{4,5},{5,4},{6,7},{7,6},{8,9},{9,8},{10,11... | collective-permute-start | bytes 9437192 | tf_op jit(solution)/shard_map/ppermute | solution.py:666
  88.1 25.2 %collective-permute-start.7 = (bf16[2,512,512]{2,1,0:T(8,128)(2,1)}, bf16[2,512,512]{2,1,0:T(8,128)(2,1)}, u32[]{:S(2)}, u32[]{:S(2)}) collective-permute-start(bf16[2,512,512]{2,1,0:T(8,128)(2,1)} %get-tuple-element.72), channel_id=1, source_target_pairs={{0,2},{1,3},{6,4},{7,5},{8,10},{9,11},{14,12},{15,13},{16,18},{17,... | collective-permute-start | bytes 3145736 | tf_op jit(solution)/shard_map/ppermute | solution.py:666
  91.3 23.5 %collective-permute-start.8 = (bf16[2,512,512]{2,1,0:T(8,128)(2,1)}, bf16[2,512,512]{2,1,0:T(8,128)(2,1)}, u32[]{:S(2)}, u32[]{:S(2)}) collective-permute-start(bf16[2,512,512]{2,1,0:T(8,128)(2,1)} %get-tuple-element.73.refs_9_), channel_id=1, source_target_pairs={{2,4},{3,5},{4,2},{5,3},{0,1},{1,0},{6,7},{7,6},{10,12},{11,13},{1... | collective-permute-start | bytes 3145736 | tf_op jit(solution)/shard_map/ppermute | solution.py:666
  113.3 85.3 %collective-permute-start.23 = (bf16[2,256,3072]{2,1,0:T(8,128)(2,1)}, bf16[2,256,3072]{2,1,0:T(8,128)(2,1)}, u32[]{:S(2)}, u32[]{:S(2)}) collective-permute-start(bf16[2,256,3072]{2,1,0:T(8,128)(2,1)} %get-tuple-element.111), channel_id=1, source_target_pairs={{0,16},{8,24},{16,0},{24,8},{1,17},{9,25},{17,1},{25,9},{2,18},{10... | collective-permute-start | bytes 9437192 | tf_op jit(solution)/shard_map/ppermute | solution.py:760
  114.8 83.8 %collective-permute-start.22 = (bf16[2,256,3072]{2,1,0:T(8,128)(2,1)}, bf16[2,256,3072]{2,1,0:T(8,128)(2,1)}, u32[]{:S(2)}, u32[]{:S(2)}) collective-permute-start(bf16[2,256,3072]{2,1,0:T(8,128)(2,1)} %get-tuple-element.110), channel_id=1, source_target_pairs={{0,8},{8,0},{16,24},{24,16},{1,9},{9,1},{17,25},{25,17},{2,10},{10... | collective-permute-start | bytes 9437192 | tf_op jit(solution)/shard_map/ppermute | solution.py:760
  116.9 18.1 %collective-permute-start.11 = (bf16[2,512,512]{2,1,0:T(8,128)(2,1)}, bf16[2,512,512]{2,1,0:T(8,128)(2,1)}, u32[]{:S(2)}, u32[]{:S(2)}) collective-permute-start(bf16[2,512,512]{2,1,0:T(8,128)(2,1)} %get-tuple-element.78.refs_9_), channel_id=1, source_target_pairs={{2,4},{3,5},{4,2},{5,3},{0,1},{1,0},{6,7},{7,6},{10,12},{11,13},{1... | collective-permute-start | bytes 3145736 | tf_op jit(solution)/shard_map/ppermute | solution.py:666
  117.5 6.4 %copy-start.1 = (bf16[512,3072]{1,0:T(8,128)(2,1)}, bf16[512,3072]{1,0:T(8,128)(2,1)S(1)}, u32[]{:S(2)}) copy-start(bf16[512,3072]{1,0:T(8,128)(2,1)S(1)} %collective-permute-done.6.refs_7_) | copy-start | bytes 9437188
  117.5 17.5 %collective-permute-start.13 = (bf16[2,512,256]{2,1,0:T(8,128)(2,1)}, bf16[2,512,256]{2,1,0:T(8,128)(2,1)}, u32[]{:S(2)}, u32[]{:S(2)}) collective-permute-start(bf16[2,512,256]{2,1,0:T(8,128)(2,1)} %get-tuple-element.82), channel_id=1, source_target_pairs={{0,2},{1,3},{6,4},{7,5},{8,10},{9,11},{14,12},{15,13},{16,18},{17,... | collective-permute-start | bytes 1572872 | tf_op jit(solution)/shard_map/ppermute | solution.py:666
  126.7 28.6 %collective-permute-start.14 = (bf16[768,512]{1,0:T(8,128)(2,1)}, bf16[768,512]{1,0:T(8,128)(2,1)S(1)}, u32[]{:S(2)}, u32[]{:S(2)}) collective-permute-start(bf16[768,512]{1,0:T(8,128)(2,1)} %get-tuple-element.90), channel_id=1, source_target_pairs={{0,2},{1,3},{6,4},{7,5},{2,0},{3,1},{4,6},{5,7},{8,10},{9,11},{14,... | collective-permute-start | bytes 2359304 | tf_op jit(solution)/shard_map/ppermute | solution.py:666
  135.6 19.7 %collective-permute-start.15 = (bf16[2,512,256]{2,1,0:T(8,128)(2,1)}, bf16[2,512,256]{2,1,0:T(8,128)(2,1)S(1)}, u32[]{:S(2)}, u32[]{:S(2)}) collective-permute-start(bf16[2,512,256]{2,1,0:T(8,128)(2,1)} %get-tuple-element.91.refs_10_), channel_id=1, source_target_pairs={{2,4},{3,5},{4,2},{5,3},{0,1},{1,0},{6,7},{7,6},{10,12},{11,13},{1... | collective-permute-start | bytes 1572872 | tf_op jit(solution)/shard_map/ppermute | solution.py:666
  137.4 34.7 %collective-permute-start.16 = (bf16[768,512]{1,0:T(8,128)(2,1)}, bf16[768,512]{1,0:T(8,128)(2,1)S(1)}, u32[]{:S(2)}, u32[]{:S(2)}) collective-permute-start(bf16[768,512]{1,0:T(8,128)(2,1)} %get-tuple-element.97), channel_id=1, source_target_pairs={{0,2},{1,3},{6,4},{7,5},{2,0},{3,1},{4,6},{5,7},{8,10},{9,11},{14,... | collective-permute-start | bytes 2359304 | tf_op jit(solution)/shard_map/ppermute | solution.py:666
  155.3 1.0 copy-start.4
  158.7 13.4 %collective-permute-start.17 = (bf16[2,512,256]{2,1,0:T(8,128)(2,1)}, bf16[2,512,256]{2,1,0:T(8,128)(2,1)S(1)}, u32[]{:S(2)}, u32[]{:S(2)}) collective-permute-start(bf16[2,512,256]{2,1,0:T(8,128)(2,1)} %get-tuple-element.98.refs_11_), channel_id=1, source_target_pairs={{2,4},{3,5},{4,2},{5,3},{0,1},{1,0},{6,7},{7,6},{10,12},{11,13},{1... | collective-permute-start | bytes 1572872 | tf_op jit(solution)/shard_map/ppermute | solution.py:666
  160.6 30.4 %collective-permute-start.18 = (bf16[768,256]{1,0:T(8,128)(2,1)}, bf16[768,256]{1,0:T(8,128)(2,1)S(1)}, u32[]{:S(2)}, u32[]{:S(2)}) collective-permute-start(bf16[768,256]{1,0:T(8,128)(2,1)} %get-tuple-element.104), channel_id=1, source_target_pairs={{0,2},{1,3},{6,4},{7,5},{2,0},{3,1},{4,6},{5,7},{8,10},{9,11},{14,... | collective-permute-start | bytes 1179656 | tf_op jit(solution)/shard_map/ppermute | solution.py:666
  172.1 1.0 copy-start.6
  174.7 16.3 %collective-permute-start.19 = (bf16[768,256]{1,0:T(8,128)(2,1)}, bf16[768,256]{1,0:T(8,128)(2,1)S(1)}, u32[]{:S(2)}, u32[]{:S(2)}) collective-permute-start(bf16[768,256]{1,0:T(8,128)(2,1)} %get-tuple-element.105), channel_id=1, source_target_pairs={{0,2},{1,3},{6,4},{7,5},{2,0},{3,1},{4,6},{5,7},{8,10},{9,11},{14,... | collective-permute-start | bytes 1179656 | tf_op jit(solution)/shard_map/ppermute | solution.py:666
  186.1 26.6 %collective-permute-start.20 = (bf16[384,512]{1,0:T(8,128)(2,1)}, bf16[384,512]{1,0:T(8,128)(2,1)S(1)}, u32[]{:S(2)}, u32[]{:S(2)}) collective-permute-start(bf16[384,512]{1,0:T(8,128)(2,1)} %get-tuple-element.108), channel_id=1, source_target_pairs={{0,1},{1,0},{2,3},{3,2},{4,5},{5,4},{6,7},{7,6},{8,9},{9,8},{10,11... | collective-permute-start | bytes 1179656 | tf_op jit(solution)/shard_map/ppermute | solution.py:666
  197.5 15.2 %collective-permute-start.21 = (bf16[384,512]{1,0:T(8,128)(2,1)}, bf16[384,512]{1,0:T(8,128)(2,1)S(1)}, u32[]{:S(2)}, u32[]{:S(2)}) collective-permute-start(bf16[384,512]{1,0:T(8,128)(2,1)} %get-tuple-element.109), channel_id=1, source_target_pairs={{0,1},{1,0},{2,3},{3,2},{4,5},{5,4},{6,7},{7,6},{8,9},{9,8},{10,11... | collective-permute-start | bytes 1179656 | tf_op jit(solution)/shard_map/ppermute | solution.py:666
  198.6 14.0 %copy-start.9 = (bf16[384,512]{1,0:T(8,128)(2,1)S(1)}, bf16[384,512]{1,0:T(8,128)(2,1)}, u32[]{:S(2)}) copy-start(bf16[384,512]{1,0:T(8,128)(2,1)} %get-tuple-element.101) | copy-start | bytes 1179652
  198.6 14.0 %copy-start.10 = (bf16[384,512]{1,0:T(8,128)(2,1)S(1)}, bf16[384,512]{1,0:T(8,128)(2,1)}, u32[]{:S(2)}) copy-start(bf16[384,512]{1,0:T(8,128)(2,1)} %get-tuple-element.107) | copy-start | bytes 1179652
  (5 other events, 4.3 us)

commit v5 on v4

--- a/solution.py
+++ b/solution.py
@@ -501,8 +501,8 @@
         )
 
     for place in places:
-        for copy in loads(*place):
-            copy.start()
+        for at, copy in enumerate(loads(*place)):
+            copy.start(priority=at % 2)
     for part, tile in places:
         for copy in loads(part, tile):
             copy.wait()
@@ -590,13 +590,13 @@
 
     def begin():
         for tile in range(tiles):
-            for copy in loads(tile):
-                copy.start()
+            for at, copy in enumerate(loads(tile)):
+                copy.start(priority=at % 2)
             for at, source in enumerate(came):
 
                 @pl.when(table[tile // per_part] == at)
                 def _():
-                    mate_copy(tile, source).start()
+                    mate_copy(tile, source).start(priority=1)
 
     def finish():
         for tile in range(tiles):
@@ -611,8 +611,8 @@
             made = MOMENTUM_RATE * mom_mean + grad_mean
             moved[here] = made
             start[here] = begun - OUTER_RATE * (grad_mean + MOMENTUM_RATE * made)
-            for copy in stores(tile):
-                copy.start()
+            for at, copy in enumerate(stores(tile)):
+                copy.start(priority=at % 2)
         for tile in range(tiles):
             for copy in stores(tile):
                 copy.wait()
@@ -716,15 +716,18 @@
     OURS, HANDED = 2, 2 + LINE
     ours = (rows, sibling_tokens)
 
-    handed, mark = touch(handed, mark, cosine, sine)
+    handed, mark = touch(handed, mark, cosine, sine, reach)
     theirs = (handed, over(handed, swap))
     near, far = [over(packed[0], inward)], []
 
-    def stage(j, *after):
-        near[j], mark = touch(near[j], *far[j - 1 :], *after)
-        far.append(over(near[j], across))
+    def stage(j, mark):
         if j + 2 < chunks:
-            near.append(over(touch(packed[j + 1], mark)[0], inward))
+            made, mark = touch(packed[j + 1], mark, near[j], *far[j - 1 :])
+            far.append(over(near[j], across))
+            near.append(over(made, inward))
+        else:
+            near[j], mark = touch(near[j], *far[j - 1 :], mark)
+            far.append(over(near[j], across))
         return mark
 
     other_rows, mark = touch(other_rows, mark, near[0])

time: 215 us -> 212 us (0.986)
  Pallas kernels: 89.4 us -> 86.8 us
  transfers between devices with their start and end apart: 24 -> 24, of which waited for: 5 -> 5; matrix products, arithmetic and copies ran while one was open for 3% -> 3% of each run, Pallas kernels for 42% -> 41%
where the time goes in v5:
time: 212 us
  Pallas kernels  86.8 us (41%)
  waiting for transfers between devices  60.2 us (28%)
  starting transfers between devices  51.6 us (24%)
  local copies, waits for them, and re-layouts  7.16 us (3%)
  other arithmetic  4.66 us (2%)
    ppermute x20, waiting for transfers between devices, over(): return lax.ppermute(value, 'fsdp', pairs)  57.8 us
    ppermute x20, starting transfers between devices, over(): return lax.ppermute(value, 'fsdp', pairs)  45.5 us
    pallas_call x7, Pallas kernels, project(): pl.pallas_call(lambda *refs: project_kernel(span, len(wide), len(chunks),...  22.2 us
    pallas_call x1, Pallas kernels, outer_update(): pl.pallas_call(kernel, in_specs=[SMEM] + [HBM] * (3 + len(came) + len(aft...  13.4 us
    pallas_call x4, Pallas kernels, pack(): pl.pallas_call(lambda *refs: pack_kernel(first, count, *refs), in_specs=[...  12.6 us
    pallas_call x2, Pallas kernels, attend_chunks(): pl.pallas_call(lambda *refs: attend_kernel(heads, group, len(came), *refs...  11.2 us
    pallas_call x1, Pallas kernels, sent_parts(): pl.pallas_call(sent_kernel, in_specs=[SMEM] + [HBM] * (3 + len(after)), o...  8.36 us
    pallas_call x2, Pallas kernels, relay(): pl.pallas_call(relay_kernel, in_specs=[SMEM] + [HBM] * (2 + len(after)),...  7.43 us
  transfers between devices with their start and end apart: 24, of which 5 were waited for; matrix products, arithmetic and copies ran while one was open for 3% of the time, Pallas kernels for 41%

profile of v5, /device:TPU:0, one launch (start us, length us, event | category | flops | bytes accessed | tf_op | source)
XLA Modules:
  0.0 211.6 jit_solution(6121256460963011261)
XLA Ops:
  1.2 3.2 %hand_tokens.1 = (bf16[384,3072]{1,0:T(8,128)(2,1)}, f32[8,128]{1,0:T(8,128)}) custom-call(s32[1]{0:T(128)} %bitcast.14.lead, bf16[384,4096]{1,0:T(8,128)(2,1)} %bitcast.41), custom_call_target="tpu_custom_call" | custom-call | flops 1 | bytes 1 | tf_op jit(solution)/shard_map/hand_tokens/pallas_call | solution.py:156
  4.4 4.2 %collective-permute-start.3 = (bf16[384,3072]{1,0:T(8,128)(2,1)}, bf16[384,3072]{1,0:T(8,128)(2,1)}, u32[]{:S(2)}, u32[]{:S(2)}) collective-permute-start(bf16[384,3072]{1,0:T(8,128)(2,1)} %get-tuple-element.57), channel_id=1, source_target_pairs={{0,2},{1,3},{6,4},{7,5},{2,0},{3,1},{4,6},{5,7},{8,10},{9,11},{14,... | collective-permute-start | bytes 7077896 | tf_op jit(solution)/shard_map/ppermute | solution.py:666
  8.7 8.4 %sent_parts.1 = (bf16[2,256,3072]{2,1,0:T(8,128)(2,1)}, bf16[2,256,3072]{2,1,0:T(8,128)(2,1)}, f32[8,128]{1,0:T(8,128)}) custom-call(s32[1]{0:T(128)S(6)} %convert_element_type.20.swapped, f32[512,3072]{1,0:T(8,128)} %bitcast.46, bf16[512,3072]{1,0:T(8,128)(2,1)} %bitcast.28, f32[512,3072]{1,0:T(8,128)} %bitcast.48, f32[8,128]{1,0:T(8,128)} %get-tuple-element.58.refs_0_), custom_call_target="tpu_custom_call" | custom-call | flops 1 | bytes 1 | tf_op jit(solution)/shard_map/sent_parts/pallas_call | solution.py:520
  21.8 3.2 %pack.4 = (bf16[2,512,512]{2,1,0:T(8,128)(2,1)}, f32[8,128]{1,0:T(8,128)}) custom-call(s32[6]{0:T(128)} %stack.70.refs_0_.refs_1_, bf16[512,3072]{1,0:T(8,128)(2,1)} %bitcast.29, bf16[512,3072]{1,0:T(8,128)(2,1)} %copy-done, f32[8,128]{1,0:T(8,128)} %get-tuple-element.59.refs_3_), custom_call_target="tpu_custom_call" | custom-call | flops 1 | bytes 1 | tf_op jit(solution)/shard_map/pack/pallas_call | solution.py:185
  25.1 2.0 collective-permute-start.5
  30.7 3.3 %pack.5 = (bf16[2,512,512]{2,1,0:T(8,128)(2,1)}, f32[8,128]{1,0:T(8,128)}) custom-call(s32[6]{0:T(128)} %stack.70.refs_0_.refs_1_, bf16[512,3072]{1,0:T(8,128)(2,1)} %bitcast.30, bf16[512,3072]{1,0:T(8,128)(2,1)} %copy-done, f32[8,128]{1,0:T(8,128)} %get-tuple-element.60.refs_3_), custom_call_target="tpu_custom_call" | custom-call | flops 1 | bytes 1 | tf_op jit(solution)/shard_map/pack/pallas_call | solution.py:185
  34.0 3.0 %pack.6 = (bf16[2,512,256]{2,1,0:T(8,128)(2,1)}, f32[8,128]{1,0:T(8,128)}) custom-call(s32[6]{0:T(128)} %stack.70.refs_0_.refs_1_, bf16[512,3072]{1,0:T(8,128)(2,1)} %bitcast.31, bf16[512,3072]{1,0:T(8,128)(2,1)} %copy-done, f32[8,128]{1,0:T(8,128)} %get-tuple-element.61.refs_3_), custom_call_target="tpu_custom_call" | custom-call | flops 1 | bytes 1 | tf_op jit(solution)/shard_map/pack/pallas_call | solution.py:185
  37.1 3.1 %pack.7 = (bf16[2,512,256]{2,1,0:T(8,128)(2,1)}, f32[8,128]{1,0:T(8,128)}) custom-call(s32[6]{0:T(128)} %stack.70.refs_0_.refs_1_, bf16[512,3072]{1,0:T(8,128)(2,1)} %bitcast.32, bf16[512,3072]{1,0:T(8,128)(2,1)} %copy-done, f32[8,128]{1,0:T(8,128)} %get-tuple-element.62.refs_3_), custom_call_target="tpu_custom_call" | custom-call | flops 1 | bytes 1 | tf_op jit(solution)/shard_map/pack/pallas_call | solution.py:185
  40.1 20.4 %collective-permute-done.3.refs_0_ = bf16[384,3072]{1,0:T(8,128)(2,1)} collective-permute-done((bf16[384,3072]{1,0:T(8,128)(2,1)}, bf16[384,3072]{1,0:T(8,128)(2,1)}, u32[]{:S(2)}, u32[]{:S(2)}) %collective-permute-start.3) | collective-permute-done | bytes 2359328 | tf_op jit(solution)/shard_map/ppermute | solution.py:666
  61.2 21.1 %collective-permute-done.5.refs_2_.refs_9_ = bf16[2,512,512]{2,1,0:T(8,128)(2,1)S(1)} collective-permute-done((bf16[2,512,512]{2,1,0:T(8,128)(2,1)}, bf16[2,512,512]{2,1,0:T(8,128)(2,1)S(1)}, u32[]{:S(2)}, u32[]{:S(2)}) %collective-permute-start.5) | collective-permute-done | bytes 1048608 | tf_op jit(solution)/shard_map/ppermute | solution.py:666
  85.0 2.4 %collective-permute-done.11.came.refs_4_ = bf16[2,256,3072]{2,1,0:T(8,128)(2,1)} collective-permute-done((bf16[2,256,3072]{2,1,0:T(8,128)(2,1)}, bf16[2,256,3072]{2,1,0:T(8,128)(2,1)}, u32[]{:S(2)}, u32[]{:S(2)}) %collective-permute-start.11) | collective-permute-done | bytes 3145760 | tf_op jit(solution)/shard_map/ppermute | solution.py:689
  87.3 3.2 %collective-permute-start.7 = (bf16[2,512,512]{2,1,0:T(8,128)(2,1)}, bf16[2,512,512]{2,1,0:T(8,128)(2,1)}, u32[]{:S(2)}, u32[]{:S(2)}) collective-permute-start(bf16[2,512,512]{2,1,0:T(8,128)(2,1)} %get-tuple-element.69), channel_id=1, source_target_pairs={{0,2},{1,3},{6,4},{7,5},{8,10},{9,11},{14,12},{15,13},{16,18},{17,... | collective-permute-start | bytes 3145736 | tf_op jit(solution)/shard_map/ppermute | solution.py:666
  90.6 3.7 %relay.2 = (bf16[2,256,3072]{2,1,0:T(8,128)(2,1)}, f32[8,128]{1,0:T(8,128)}) custom-call(s32[1]{0:T(128)S(6)} %convert_element_type.22.onward, bf16[2,256,3072]{2,1,0:T(8,128)(2,1)} %collective-permute-done.11.came.refs_4_, bf16[2,256,3072]{2,1,0:T(8,128)(2,1)} %get-tuple-element.73.piece, ...), custom_call_target="tpu_custom_call", output_to_operand_aliasing={{0}: (2, {})} | custom-call | flops 1 | bytes 1 | tf_op jit(solution)/shard_map/relay/pallas_call | solution.py:550
  94.3 3.7 %relay.3 = (bf16[2,256,3072]{2,1,0:T(8,128)(2,1)}, f32[8,128]{1,0:T(8,128)}) custom-call(s32[1]{0:T(128)S(6)} %convert_element_type.22.onward, bf16[2,256,3072]{2,1,0:T(8,128)(2,1)} %collective-permute-done.10.came.refs_3_, bf16[2,256,3072]{2,1,0:T(8,128)(2,1)} %get-tuple-element.72.piece, ...), custom_call_target="tpu_custom_call", output_to_operand_aliasing={{0}: (2, {})} | custom-call | flops 1 | bytes 1 | tf_op jit(solution)/shard_map/relay/pallas_call | solution.py:550
  98.0 14.6 %collective-permute-done.7.refs_2_.refs_9_ = bf16[2,512,512]{2,1,0:T(8,128)(2,1)} collective-permute-done((bf16[2,512,512]{2,1,0:T(8,128)(2,1)}, bf16[2,512,512]{2,1,0:T(8,128)(2,1)}, u32[]{:S(2)}, u32[]{:S(2)}) %collective-permute-start.7) | collective-permute-done | bytes 1048608 | tf_op jit(solution)/shard_map/ppermute | solution.py:666
  116.2 5.7 %collective-permute-start.13 = (bf16[2,512,256]{2,1,0:T(8,128)(2,1)}, bf16[2,512,256]{2,1,0:T(8,128)(2,1)}, u32[]{:S(2)}, u32[]{:S(2)}) collective-permute-start(bf16[2,512,256]{2,1,0:T(8,128)(2,1)} %get-tuple-element.77), channel_id=1, source_target_pairs={{0,2},{1,3},{6,4},{7,5},{8,10},{9,11},{14,12},{15,13},{16,18},{17,... | collective-permute-start | bytes 1572872 | tf_op jit(solution)/shard_map/ppermute | solution.py:666
  122.7 2.8 %project.7 = (bf16[768,512]{1,0:T(8,128)(2,1)}, f32[8,128]{1,0:T(8,128)}) custom-call(s32[10]{0:T(128)} %concatenate.46.refs_0_.table, s32[6]{0:T(128)} %stack.70.refs_0_.refs_1_, bf16[384,3072]{1,0:T(8,128)(2,1)} %get-tuple-element.70.refs_2_, bf16[384,3072]{1,0:T(8,128)(2,1)} %collective-permute-done.9.refs_3_, bf16[512,3072]{1,0:T(8,128)(2,1)} %bitcast.33, ...), custom_call_target="tpu_custom_call" | custom-call | flops 1 | bytes 1 | tf_op jit(solution)/shard_map/project/pallas_call | solution.py:315
  125.5 2.0 collective-permute-start.14
  127.5 4.7 %project.8 = (f32[768,512]{1,0:T(8,128)}, f32[8,128]{1,0:T(8,128)}) custom-call(s32[10]{0:T(128)} %concatenate.46.refs_0_.table, s32[6]{0:T(128)} %stack.70.refs_0_.refs_1_, bf16[384,4096]{1,0:T(8,128)(2,1)} %bitcast.43, bf16[384,4096]{1,0:T(8,128)(2,1)} %collective-permute-done.refs_3_, bf16[512,3072]{1,0:T(8,128)(2,1)} %bitcast.34, ...), custom_call_target="tpu_custom_call" | custom-call | flops 1 | bytes 1 | tf_op jit(solution)/shard_map/project/pallas_call | solution.py:315
  132.1 1.6 collective-permute-done.13.refs_0_
  134.3 1.8 project.9
  136.1 13.3 %collective-permute-start.16 = (bf16[768,512]{1,0:T(8,128)(2,1)}, bf16[768,512]{1,0:T(8,128)(2,1)S(1)}, u32[]{:S(2)}, u32[]{:S(2)}) collective-permute-start(bf16[768,512]{1,0:T(8,128)(2,1)} %get-tuple-element.93), channel_id=1, source_target_pairs={{0,2},{1,3},{6,4},{7,5},{2,0},{3,1},{4,6},{5,7},{8,10},{9,11},{14,... | collective-permute-start | bytes 2359304 | tf_op jit(solution)/shard_map/ppermute | solution.py:666
  149.4 4.9 %project.10 = (f32[768,512]{1,0:T(8,128)}, f32[8,128]{1,0:T(8,128)}) custom-call(s32[10]{0:T(128)} %concatenate.46.refs_0_.table, s32[6]{0:T(128)} %stack.70.refs_0_.refs_1_, bf16[384,4096]{1,0:T(8,128)(2,1)} %bitcast.44, bf16[384,4096]{1,0:T(8,128)(2,1)} %collective-permute-done.refs_3_, bf16[512,3072]{1,0:T(8,128)(2,1)} %bitcast.36, ...), custom_call_target="tpu_custom_call" | custom-call | flops 1 | bytes 1 | tf_op jit(solution)/shard_map/project/pallas_call | solution.py:315
  155.4 2.4 %unpack.1 = (bf16[2,512,256]{2,1,0:T(8,128)(2,1)}, f32[8,128]{1,0:T(8,128)}) custom-call(bf16[768,512]{1,0:T(8,128)(2,1)} %copy-done.4, f32[8,128]{1,0:T(8,128)} %get-tuple-element.88.refs_0_, bf16[2,512,256]{2,1,0:T(8,128)(2,1)} %copy-done.3), custom_call_target="tpu_custom_call" | custom-call | flops 1 | bytes 1 | tf_op jit(solution)/shard_map/unpack/pallas_call | solution.py:353
  157.8 1.6 project.11
  159.4 8.5 %collective-permute-start.18 = (bf16[768,256]{1,0:T(8,128)(2,1)}, bf16[768,256]{1,0:T(8,128)(2,1)S(1)}, u32[]{:S(2)}, u32[]{:S(2)}) collective-permute-start(bf16[768,256]{1,0:T(8,128)(2,1)} %get-tuple-element.100), channel_id=1, source_target_pairs={{0,2},{1,3},{6,4},{7,5},{2,0},{3,1},{4,6},{5,7},{8,10},{9,11},{14,... | collective-permute-start | bytes 1179656 | tf_op jit(solution)/shard_map/ppermute | solution.py:666
  167.9 3.1 %keep_keys.1 = (bf16[2,2,384,128]{3,2,1,0:T(8,128)(2,1)}, bf16[2,2,384,128]{3,2,1,0:T(8,128)(2,1)}, f32[8,128]{1,0:T(8,128)}) custom-call(s32[10]{0:T(128)} %concatenate.46.refs_0_.table, f32[768,512]{1,0:T(8,128)} %get-tuple-element.85.own, bf16[768,512]{1,0:T(8,128)(2,1)} %copy-done.4, f32[2,384,128]{2,1,0:T(8,128)} %get-tuple-element.116.refs_2_.cosine.refs_1_, ...), custom_call_target="tpu_custom_call" | custom-call | flops 1 | bytes 1 | tf_op jit(solution)/shard_map/keep_keys/pallas_call | solution.py:401
  173.6 4.9 %collective-permute-start.19 = (bf16[768,256]{1,0:T(8,128)(2,1)}, bf16[768,256]{1,0:T(8,128)(2,1)S(1)}, u32[]{:S(2)}, u32[]{:S(2)}) collective-permute-start(bf16[768,256]{1,0:T(8,128)(2,1)} %get-tuple-element.101), channel_id=1, source_target_pairs={{0,2},{1,3},{6,4},{7,5},{2,0},{3,1},{4,6},{5,7},{8,10},{9,11},{14,... | collective-permute-start | bytes 1179656 | tf_op jit(solution)/shard_map/ppermute | solution.py:666
  178.6 5.6 %attend_chunks.2 = (bf16[384,512]{1,0:T(8,128)(2,1)}, bf16[384,512]{1,0:T(8,128)(2,1)}, f32[8,128]{1,0:T(8,128)}) custom-call(f32[768,512]{1,0:T(8,128)} %get-tuple-element.84.refs_0_, f32[2,384,128]{2,1,0:T(8,128)} %get-tuple-element.116.refs_2_.cosine.refs_1_, f32[2,384,128]{2,1,0:T(8,128)} %get-tuple-element.117.refs_3_.sine.refs_2_, ...), custom_call_target="tpu_custom_call" | custom-call | flops 1 | bytes 1 | tf_op jit(solution)/shard_map/attend_chunks/pallas_call | solution.py:458
  184.2 4.9 %project.13 = (f32[768,512]{1,0:T(8,128)}, f32[8,128]{1,0:T(8,128)}) custom-call(s32[10]{0:T(128)} %concatenate.46.refs_0_.table, s32[6]{0:T(128)} %stack.70.refs_0_.refs_1_, bf16[384,4096]{1,0:T(8,128)(2,1)} %bitcast.45, bf16[384,4096]{1,0:T(8,128)(2,1)} %collective-permute-done.refs_3_, bf16[512,3072]{1,0:T(8,128)(2,1)} %bitcast.39, ...), custom_call_target="tpu_custom_call" | custom-call | flops 1 | bytes 1 | tf_op jit(solution)/shard_map/project/pallas_call | solution.py:315
  190.0 5.6 %attend_chunks.3 = (bf16[384,512]{1,0:T(8,128)(2,1)}, bf16[384,512]{1,0:T(8,128)(2,1)}, f32[8,128]{1,0:T(8,128)}) custom-call(f32[768,512]{1,0:T(8,128)} %get-tuple-element.99.refs_0_, f32[2,384,128]{2,1,0:T(8,128)} %get-tuple-element.116.refs_2_.cosine.refs_1_, f32[2,384,128]{2,1,0:T(8,128)} %get-tuple-element.117.refs_3_.sine.refs_2_, ...), custom_call_target="tpu_custom_call" | custom-call | flops 1 | bytes 1 | tf_op jit(solution)/shard_map/attend_chunks/pallas_call | solution.py:458
  196.7 13.4 %outer_update.1 = (f32[512,3072]{1,0:T(8,128)}, f32[512,3072]{1,0:T(8,128)}, f32[8,128]{1,0:T(8,128)}) custom-call(s32[2]{0:T(128)} %pad_add_fusion.1.choice, f32[512,3072]{1,0:T(8,128)} %bitcast.47, bf16[512,3072]{1,0:T(8,128)(2,1)} %bitcast.40, f32[512,3072]{1,0:T(8,128)} %bitcast.49, bf16[2,256,3072]{2,1,0:T(8,128)(2,1)} %collective-permute-done.10.came.refs_3_, ...), custom_call_target="tpu_custom_call" | custom-call | flops 1 | bytes 1 | tf_op jit(solution)/shard_map/outer_update/pallas_call | solution.py:637
  (79 shorter events, 24.2 us)
Async XLA Ops:
  0.6 8.0 %copy-start.12 = (s32[4]{0:T(128)S(1)}, s32[4]{0:T(128)}, u32[]{:S(2)}) copy-start(s32[4]{0:T(128)} %param.8) | copy-start | bytes 52
  0.6 19.5 %collective-permute-start.1 = (bf16[512,3072]{1,0:T(8,128)(2,1)}, bf16[512,3072]{1,0:T(8,128)(2,1)S(1)}, u32[]{:S(2)}, u32[]{:S(2)}) collective-permute-start(bf16[512,3072]{1,0:T(8,128)(2,1)} %bitcast.26), channel_id=1, source_target_pairs={{0,1},{1,0},{2,3},{3,2},{4,5},{5,4},{6,7},{7,6},{8,9},{9,8},{10,11... | collective-permute-start | bytes 9437192 | tf_op jit(solution)/shard_map/ppermute | solution.py:666
  1.2 60.0 %collective-permute-start.2 = (bf16[512,3072]{1,0:T(8,128)(2,1)}, bf16[512,3072]{1,0:T(8,128)(2,1)}, u32[]{:S(2)}, u32[]{:S(2)}) collective-permute-start(bf16[512,3072]{1,0:T(8,128)(2,1)} %bitcast.27), channel_id=1, source_target_pairs={{2,4},{3,5},{4,2},{5,3},{0,1},{1,0},{6,7},{7,6},{10,12},{11,13},{1... | collective-permute-start | bytes 9437192 | tf_op jit(solution)/shard_map/ppermute | solution.py:666
  4.4 56.1 %collective-permute-start.3 = (bf16[384,3072]{1,0:T(8,128)(2,1)}, bf16[384,3072]{1,0:T(8,128)(2,1)}, u32[]{:S(2)}, u32[]{:S(2)}) collective-permute-start(bf16[384,3072]{1,0:T(8,128)(2,1)} %get-tuple-element.57), channel_id=1, source_target_pairs={{0,2},{1,3},{6,4},{7,5},{2,0},{3,1},{4,6},{5,7},{8,10},{9,11},{14,... | collective-permute-start | bytes 7077896 | tf_op jit(solution)/shard_map/ppermute | solution.py:666
  8.7 11.5 %copy-start.11 = (s32[1,384]{1,0:T(1,128)S(1)}, s32[1,384]{1,0:T(1,128)}, u32[]{:S(2)}) copy-start(s32[1,384]{1,0:T(1,128)} %param.7) | copy-start | bytes 4612
  17.1 70.3 %collective-permute-start.11 = (bf16[2,256,3072]{2,1,0:T(8,128)(2,1)}, bf16[2,256,3072]{2,1,0:T(8,128)(2,1)}, u32[]{:S(2)}, u32[]{:S(2)}) collective-permute-start(bf16[2,256,3072]{2,1,0:T(8,128)(2,1)} %get-tuple-element.73.piece), channel_id=1, source_target_pairs={{0,16},{8,24},{16,0},{24,8},{1,17},{9,25},{17,1},{25,9},{2,18},{10... | collective-permute-start | bytes 9437192 | tf_op jit(solution)/shard_map/ppermute | solution.py:689
  18.7 71.9 %collective-permute-start.10 = (bf16[2,256,3072]{2,1,0:T(8,128)(2,1)}, bf16[2,256,3072]{2,1,0:T(8,128)(2,1)}, u32[]{:S(2)}, u32[]{:S(2)}) collective-permute-start(bf16[2,256,3072]{2,1,0:T(8,128)(2,1)} %get-tuple-element.72.piece), channel_id=1, source_target_pairs={{0,8},{8,0},{16,24},{24,16},{1,9},{9,1},{17,25},{25,17},{2,10},{10... | collective-permute-start | bytes 9437192 | tf_op jit(solution)/shard_map/ppermute | solution.py:689
  20.2 1.7 copy-start
  20.2 4.9 %collective-permute-start.4 = (s32[384]{0:T(512)S(1)}, s32[384]{0:T(512)S(1)}, u32[]{:S(2)}, u32[]{:S(2)}) collective-permute-start(s32[384]{0:T(512)S(1)} %reduce), channel_id=1, source_target_pairs={{0,1},{1,0},{2,3},{3,2},{4,5},{5,4},{6,7},{7,6},{8,9},{9,8},{10,11... | collective-permute-start | bytes 4616 | tf_op jit(solution)/shard_map/ppermute | solution.py:666
  25.1 57.2 %collective-permute-start.5 = (bf16[2,512,512]{2,1,0:T(8,128)(2,1)}, bf16[2,512,512]{2,1,0:T(8,128)(2,1)S(1)}, u32[]{:S(2)}, u32[]{:S(2)}) collective-permute-start(bf16[2,512,512]{2,1,0:T(8,128)(2,1)} %get-tuple-element.65), channel_id=1, source_target_pairs={{0,2},{1,3},{6,4},{7,5},{8,10},{9,11},{14,12},{15,13},{16,18},{17,... | collective-permute-start | bytes 3145736 | tf_op jit(solution)/shard_map/ppermute | solution.py:666
  83.8 32.4 %collective-permute-start.6 = (bf16[512,3072]{1,0:T(8,128)(2,1)}, bf16[512,3072]{1,0:T(8,128)(2,1)S(1)}, u32[]{:S(2)}, u32[]{:S(2)}) collective-permute-start(bf16[512,3072]{1,0:T(8,128)(2,1)} %get-tuple-element.66.refs_6_), channel_id=1, source_target_pairs={{0,1},{1,0},{2,3},{3,2},{4,5},{5,4},{6,7},{7,6},{8,9},{9,8},{10,11... | collective-permute-start | bytes 9437192 | tf_op jit(solution)/shard_map/ppermute | solution.py:666
  83.8 31.8 %collective-permute-start.9 = (bf16[384,3072]{1,0:T(8,128)(2,1)}, bf16[384,3072]{1,0:T(8,128)(2,1)}, u32[]{:S(2)}, u32[]{:S(2)}) collective-permute-start(bf16[384,3072]{1,0:T(8,128)(2,1)} %get-tuple-element.70.refs_2_), channel_id=1, source_target_pairs={{0,1},{1,0},{2,3},{3,2},{4,5},{5,4},{6,7},{7,6},{8,9},{9,8},{10,11... | collective-permute-start | bytes 7077896 | tf_op jit(solution)/shard_map/ppermute | solution.py:666
  84.4 41.1 %collective-permute-start = (bf16[384,4096]{1,0:T(8,128)(2,1)}, bf16[384,4096]{1,0:T(8,128)(2,1)}, u32[]{:S(2)}, u32[]{:S(2)}) collective-permute-start(bf16[384,4096]{1,0:T(8,128)(2,1)} %bitcast.42), channel_id=1, source_target_pairs={{0,1},{1,0},{2,3},{3,2},{4,5},{5,4},{6,7},{7,6},{8,9},{9,8},{10,11... | collective-permute-start | bytes 9437192 | tf_op jit(solution)/shard_map/ppermute | solution.py:666
  87.3 25.3 %collective-permute-start.7 = (bf16[2,512,512]{2,1,0:T(8,128)(2,1)}, bf16[2,512,512]{2,1,0:T(8,128)(2,1)}, u32[]{:S(2)}, u32[]{:S(2)}) collective-permute-start(bf16[2,512,512]{2,1,0:T(8,128)(2,1)} %get-tuple-element.69), channel_id=1, source_target_pairs={{0,2},{1,3},{6,4},{7,5},{8,10},{9,11},{14,12},{15,13},{16,18},{17,... | collective-permute-start | bytes 3145736 | tf_op jit(solution)/shard_map/ppermute | solution.py:666
  90.5 23.6 %collective-permute-start.12 = (bf16[2,512,512]{2,1,0:T(8,128)(2,1)}, bf16[2,512,512]{2,1,0:T(8,128)(2,1)}, u32[]{:S(2)}, u32[]{:S(2)}) collective-permute-start(bf16[2,512,512]{2,1,0:T(8,128)(2,1)} %copy-done.2), channel_id=1, source_target_pairs={{2,4},{3,5},{4,2},{5,3},{0,1},{1,0},{6,7},{7,6},{10,12},{11,13},{1... | collective-permute-start | bytes 3145736 | tf_op jit(solution)/shard_map/ppermute | solution.py:666
  112.6 84.1 %collective-permute-start.23 = (bf16[2,256,3072]{2,1,0:T(8,128)(2,1)}, bf16[2,256,3072]{2,1,0:T(8,128)(2,1)}, u32[]{:S(2)}, u32[]{:S(2)}) collective-permute-start(bf16[2,256,3072]{2,1,0:T(8,128)(2,1)} %get-tuple-element.107), channel_id=1, source_target_pairs={{0,16},{8,24},{16,0},{24,8},{1,17},{9,25},{17,1},{25,9},{2,18},{10... | collective-permute-start | bytes 9437192 | tf_op jit(solution)/shard_map/ppermute | solution.py:763
  114.1 82.6 %collective-permute-start.22 = (bf16[2,256,3072]{2,1,0:T(8,128)(2,1)}, bf16[2,256,3072]{2,1,0:T(8,128)(2,1)}, u32[]{:S(2)}, u32[]{:S(2)}) collective-permute-start(bf16[2,256,3072]{2,1,0:T(8,128)(2,1)} %get-tuple-element.106), channel_id=1, source_target_pairs={{0,8},{8,0},{16,24},{24,16},{1,9},{9,1},{17,25},{25,17},{2,10},{10... | collective-permute-start | bytes 9437192 | tf_op jit(solution)/shard_map/ppermute | solution.py:763
  115.6 18.1 %collective-permute-start.8 = (bf16[2,512,512]{2,1,0:T(8,128)(2,1)}, bf16[2,512,512]{2,1,0:T(8,128)(2,1)}, u32[]{:S(2)}, u32[]{:S(2)}) collective-permute-start(bf16[2,512,512]{2,1,0:T(8,128)(2,1)} %collective-permute-done.7.refs_2_.refs_9_), channel_id=1, source_target_pairs={{2,4},{3,5},{4,2},{5,3},{0,1},{1,0},{6,7},{7,6},{10,12},{11,13},{1... | collective-permute-start | bytes 3145736 | tf_op jit(solution)/shard_map/ppermute | solution.py:666
  116.2 6.4 %copy-start.1 = (bf16[512,3072]{1,0:T(8,128)(2,1)}, bf16[512,3072]{1,0:T(8,128)(2,1)S(1)}, u32[]{:S(2)}) copy-start(bf16[512,3072]{1,0:T(8,128)(2,1)S(1)} %collective-permute-done.6.refs_7_) | copy-start | bytes 9437188
  116.2 17.5 %collective-permute-start.13 = (bf16[2,512,256]{2,1,0:T(8,128)(2,1)}, bf16[2,512,256]{2,1,0:T(8,128)(2,1)}, u32[]{:S(2)}, u32[]{:S(2)}) collective-permute-start(bf16[2,512,256]{2,1,0:T(8,128)(2,1)} %get-tuple-element.77), channel_id=1, source_target_pairs={{0,2},{1,3},{6,4},{7,5},{8,10},{9,11},{14,12},{15,13},{16,18},{17,... | collective-permute-start | bytes 1572872 | tf_op jit(solution)/shard_map/ppermute | solution.py:666
  125.5 28.8 %collective-permute-start.14 = (bf16[768,512]{1,0:T(8,128)(2,1)}, bf16[768,512]{1,0:T(8,128)(2,1)S(1)}, u32[]{:S(2)}, u32[]{:S(2)}) collective-permute-start(bf16[768,512]{1,0:T(8,128)(2,1)} %get-tuple-element.86), channel_id=1, source_target_pairs={{0,2},{1,3},{6,4},{7,5},{2,0},{3,1},{4,6},{5,7},{8,10},{9,11},{14,... | collective-permute-start | bytes 2359304 | tf_op jit(solution)/shard_map/ppermute | solution.py:666
  134.3 19.9 %collective-permute-start.15 = (bf16[2,512,256]{2,1,0:T(8,128)(2,1)}, bf16[2,512,256]{2,1,0:T(8,128)(2,1)S(1)}, u32[]{:S(2)}, u32[]{:S(2)}) collective-permute-start(bf16[2,512,256]{2,1,0:T(8,128)(2,1)} %get-tuple-element.87.refs_10_), channel_id=1, source_target_pairs={{2,4},{3,5},{4,2},{5,3},{0,1},{1,0},{6,7},{7,6},{10,12},{11,13},{1... | collective-permute-start | bytes 1572872 | tf_op jit(solution)/shard_map/ppermute | solution.py:666
  136.1 34.9 %collective-permute-start.16 = (bf16[768,512]{1,0:T(8,128)(2,1)}, bf16[768,512]{1,0:T(8,128)(2,1)S(1)}, u32[]{:S(2)}, u32[]{:S(2)}) collective-permute-start(bf16[768,512]{1,0:T(8,128)(2,1)} %get-tuple-element.93), channel_id=1, source_target_pairs={{0,2},{1,3},{6,4},{7,5},{2,0},{3,1},{4,6},{5,7},{8,10},{9,11},{14,... | collective-permute-start | bytes 2359304 | tf_op jit(solution)/shard_map/ppermute | solution.py:666
  154.3 1.1 copy-start.4
  157.7 13.3 %collective-permute-start.17 = (bf16[2,512,256]{2,1,0:T(8,128)(2,1)}, bf16[2,512,256]{2,1,0:T(8,128)(2,1)S(1)}, u32[]{:S(2)}, u32[]{:S(2)}) collective-permute-start(bf16[2,512,256]{2,1,0:T(8,128)(2,1)} %get-tuple-element.94.refs_11_), channel_id=1, source_target_pairs={{2,4},{3,5},{4,2},{5,3},{0,1},{1,0},{6,7},{7,6},{10,12},{11,13},{1... | collective-permute-start | bytes 1572872 | tf_op jit(solution)/shard_map/ppermute | solution.py:666
  159.4 29.7 %collective-permute-start.18 = (bf16[768,256]{1,0:T(8,128)(2,1)}, bf16[768,256]{1,0:T(8,128)(2,1)S(1)}, u32[]{:S(2)}, u32[]{:S(2)}) collective-permute-start(bf16[768,256]{1,0:T(8,128)(2,1)} %get-tuple-element.100), channel_id=1, source_target_pairs={{0,2},{1,3},{6,4},{7,5},{2,0},{3,1},{4,6},{5,7},{8,10},{9,11},{14,... | collective-permute-start | bytes 1179656 | tf_op jit(solution)/shard_map/ppermute | solution.py:666
  171.0 1.1 copy-start.6
  173.6 15.5 %collective-permute-start.19 = (bf16[768,256]{1,0:T(8,128)(2,1)}, bf16[768,256]{1,0:T(8,128)(2,1)S(1)}, u32[]{:S(2)}, u32[]{:S(2)}) collective-permute-start(bf16[768,256]{1,0:T(8,128)(2,1)} %get-tuple-element.101), channel_id=1, source_target_pairs={{0,2},{1,3},{6,4},{7,5},{2,0},{3,1},{4,6},{5,7},{8,10},{9,11},{14,... | collective-permute-start | bytes 1179656 | tf_op jit(solution)/shard_map/ppermute | solution.py:666
  184.2 26.0 %collective-permute-start.20 = (bf16[384,512]{1,0:T(8,128)(2,1)}, bf16[384,512]{1,0:T(8,128)(2,1)S(1)}, u32[]{:S(2)}, u32[]{:S(2)}) collective-permute-start(bf16[384,512]{1,0:T(8,128)(2,1)} %get-tuple-element.104), channel_id=1, source_target_pairs={{0,1},{1,0},{2,3},{3,2},{4,5},{5,4},{6,7},{7,6},{8,9},{9,8},{10,11... | collective-permute-start | bytes 1179656 | tf_op jit(solution)/shard_map/ppermute | solution.py:666
  195.6 14.6 %collective-permute-start.21 = (bf16[384,512]{1,0:T(8,128)(2,1)}, bf16[384,512]{1,0:T(8,128)(2,1)S(1)}, u32[]{:S(2)}, u32[]{:S(2)}) collective-permute-start(bf16[384,512]{1,0:T(8,128)(2,1)} %get-tuple-element.105), channel_id=1, source_target_pairs={{0,1},{1,0},{2,3},{3,2},{4,5},{5,4},{6,7},{7,6},{8,9},{9,8},{10,11... | collective-permute-start | bytes 1179656 | tf_op jit(solution)/shard_map/ppermute | solution.py:666
  196.7 13.5 %copy-start.9 = (bf16[384,512]{1,0:T(8,128)(2,1)S(1)}, bf16[384,512]{1,0:T(8,128)(2,1)}, u32[]{:S(2)}) copy-start(bf16[384,512]{1,0:T(8,128)(2,1)} %get-tuple-element.97) | copy-start | bytes 1179652
  196.7 13.5 %copy-start.10 = (bf16[384,512]{1,0:T(8,128)(2,1)S(1)}, bf16[384,512]{1,0:T(8,128)(2,1)}, u32[]{:S(2)}) copy-start(bf16[384,512]{1,0:T(8,128)(2,1)} %get-tuple-element.103) | copy-start | bytes 1179652
  (5 other events, 4.3 us)

commit v6 on v5

--- a/solution.py
+++ b/solution.py
@@ -213,7 +213,7 @@
     )(value, *after)
 
 
-def project_kernel(span, wide, parts, groups, slot, handed, riding, table, pairs, *refs):
+def project_kernel(span, wide, parts, groups, slot, handed, riding, table, pairs, *refs, meanwhile=None):
     first_unit, width = span
     tokens, refs = refs[:CORES], refs[CORES:]
     sources = refs[: wide * CORES + (groups - wide) * parts]
@@ -299,6 +299,8 @@
                     out[:depth, left : left + rider.shape[2]] = held[0, k, :, : rider.shape[2]]
 
     every_group(start)
+    if meanwhile is not None:
+        meanwhile()
     every_group(multiply)
 
 
@@ -469,6 +471,54 @@
     )(own, cosine, sine, places, *held, *came, *after)
 
 
+def attend_and_project(attending, projecting, after=()):
+    chunks, own, came, cosine, sine, places, held = attending
+    spans, table, pairs, tokens, slot, wide, packed = projecting
+    count = cosine.shape[1]
+    heads, group = sum(len(CHUNKS[j]) for j in chunks), int(CHUNKS[chunks[0]][0][1])
+    width = sum(len(CHUNKS[j]) for j in spans)
+    rows, depth = tokens[0].shape[0], packed[0][0].shape[1]
+    groups = len(wide) + len(packed)
+    sources = [half for both in wide for half in both]
+    sources += [part for parts in packed for part in parts]
+    attended = (own, cosine, sine, places, *held, *came)
+    projected = (table, pairs, *tokens, *sources)
+    out = jax.ShapeDtypeStruct((count, heads * UNIT), jnp.bfloat16)
+    product = jax.ShapeDtypeStruct((CORES * rows, width * UNIT), jnp.float32)
+
+    def kernel(*refs):
+        inputs, refs = refs[: len(attended)], refs[len(attended) :]
+        terms, refs = refs[: len(projected)], refs[len(projected) + len(after) :]
+        left, right, made, mark, hidden, *scratch = refs
+        project_kernel(
+            (FIRST_UNIT[spans[0]], width), len(wide), len(spans), groups, slot, False, False,
+            *terms, made, mark, *scratch,
+            meanwhile=lambda: attend_kernel(
+                heads, group, len(came), *inputs, left, right, mark, hidden
+            ),
+        )
+
+    return pl.pallas_call(
+        kernel,
+        grid=(1,),
+        in_specs=[whole_spec(a) for a in attended]
+        + [SMEM] * 2
+        + [HBM] * (len(projected) - 2 + len(after)),
+        out_specs=[whole_spec(a) for a in (out, out, product, MARK)],
+        out_shape=(out, out, product, MARK),
+        scratch_shapes=[
+            pltpu.VMEM((count, count), jnp.float32),
+            pltpu.VMEM((groups, CORES * rows, CORES * depth), tokens[0].dtype),
+            pltpu.VMEM((groups, CORES, depth, width * UNIT), tokens[0].dtype),
+            pltpu.VMEM((8, 128), jnp.float32),
+            pltpu.SemaphoreType.DMA((groups, CORES * (1 + width // 2))),
+        ],
+        compiler_params=pltpu.CompilerParams(vmem_limit_bytes=60 * MIB),
+        cost_estimate=SMALL,
+        name="attend_and_project",
+    )(*attended, *projected, *after)
+
+
 PARTS = 2
 TILE = 64
 
@@ -773,8 +823,14 @@
     mark = product(2, mark)
     *held, mark = keep_keys(spots, owns[0], backs[0], cosine, sine, (mark,))
     mark = product(3, mark, backs[1])
-    mark = attention(1, (1,), mark)
-    mark = own((2, 3), mark)
+    parts = tuple(tuple(rows_of[j] for j in (2, 3)) for rows_of in (far, near))
+    left, right, made, mark = attend_and_project(
+        ((1,), owns[1], [backs[1]], cosine, sine, reach, held),
+        ((2, 3), spots, pairs, ours, OURS, wide, parts),
+        (mark,),
+    )
+    contexts.append((left, over(right, swap)))
+    owns.append(made)
     mark = attention(2, (2, 3), mark)
     new_params, new_momentum, mark = outer_update(table, values, came, (mark,))
 

time: 212 us -> 211 us (level)
    pallas_call x0 -> x1, Pallas kernels: none -> 8.55 us  [attend_and_project(): pl.pallas_call(kernel, grid=(1,), in_specs=[whole_spec(a) for a in attend...]
    pallas_call x2 -> x1, Pallas kernels: 11.2 us -> 5.56 us  [attend_chunks(): pl.pallas_call(lambda *refs: attend_kernel(heads, group, len(came), *refs...]
    pallas_call x7 -> x6, Pallas kernels: 22.2 us -> 17.3 us  [project(): pl.pallas_call(lambda *refs: project_kernel(span, len(wide), len(chunks),...]
  transfers between devices with their start and end apart: 24 -> 24, of which waited for: 5 -> 5; matrix products, arithmetic and copies ran while one was open for 3% -> 3% of each run, Pallas kernels for 41% -> 40%
where the time goes in v6:
time: 211 us; the launch traced here: 210 us
  Pallas kernels  84.8 us (40%)
  waiting for transfers between devices  60.3 us (29%)
  starting transfers between devices  51.7 us (25%)
  local copies, waits for them, and re-layouts  7.15 us (3%)
  other arithmetic  4.77 us (2%)
    ppermute x20, waiting for transfers between devices, over(): return lax.ppermute(value, 'fsdp', pairs)  57.9 us
    ppermute x20, starting transfers between devices, over(): return lax.ppermute(value, 'fsdp', pairs)  45.6 us
    pallas_call x6, Pallas kernels, project(): pl.pallas_call(lambda *refs: project_kernel(span, len(wide), len(chunks),...  17.3 us
    pallas_call x1, Pallas kernels, outer_update(): pl.pallas_call(kernel, in_specs=[SMEM] + [HBM] * (3 + len(came) + len(aft...  13.4 us
    pallas_call x4, Pallas kernels, pack(): pl.pallas_call(lambda *refs: pack_kernel(first, count, *refs), in_specs=[...  12.6 us
    pallas_call x1, Pallas kernels, attend_and_project(): pl.pallas_call(kernel, grid=(1,), in_specs=[whole_spec(a) for a in attend...  8.55 us
    pallas_call x1, Pallas kernels, sent_parts(): pl.pallas_call(sent_kernel, in_specs=[SMEM] + [HBM] * (3 + len(after)), o...  8.33 us
    pallas_call x2, Pallas kernels, relay(): pl.pallas_call(relay_kernel, in_specs=[SMEM] + [HBM] * (2 + len(after)),...  7.43 us
  transfers between devices with their start and end apart: 24, of which 5 were waited for; matrix products, arithmetic and copies ran while one was open for 3% of the time, Pallas kernels for 40%

profile of v6, /device:TPU:0, one launch (start us, length us, event | category | flops | bytes accessed | tf_op | source)
XLA Modules:
  0.0 209.8 jit_solution(5875030021046512623)
XLA Ops:
  1.2 3.2 %hand_tokens.1 = (bf16[384,3072]{1,0:T(8,128)(2,1)}, f32[8,128]{1,0:T(8,128)}) custom-call(s32[1]{0:T(128)} %bitcast.14.lead, bf16[384,4096]{1,0:T(8,128)(2,1)} %bitcast.41), custom_call_target="tpu_custom_call" | custom-call | flops 1 | bytes 1 | tf_op jit(solution)/shard_map/hand_tokens/pallas_call | solution.py:156
  4.5 4.2 %collective-permute-start.3 = (bf16[384,3072]{1,0:T(8,128)(2,1)}, bf16[384,3072]{1,0:T(8,128)(2,1)}, u32[]{:S(2)}, u32[]{:S(2)}) collective-permute-start(bf16[384,3072]{1,0:T(8,128)(2,1)} %get-tuple-element.56), channel_id=1, source_target_pairs={{0,2},{1,3},{6,4},{7,5},{2,0},{3,1},{4,6},{5,7},{8,10},{9,11},{14,... | collective-permute-start | bytes 7077896 | tf_op jit(solution)/shard_map/ppermute | solution.py:716
  8.7 8.3 %sent_parts.1 = (bf16[2,256,3072]{2,1,0:T(8,128)(2,1)}, bf16[2,256,3072]{2,1,0:T(8,128)(2,1)}, f32[8,128]{1,0:T(8,128)}) custom-call(s32[1]{0:T(128)S(6)} %convert_element_type.20.swapped, f32[512,3072]{1,0:T(8,128)} %bitcast.46, bf16[512,3072]{1,0:T(8,128)(2,1)} %bitcast.28, f32[512,3072]{1,0:T(8,128)} %bitcast.48, f32[8,128]{1,0:T(8,128)} %get-tuple-element.57.refs_0_), custom_call_target="tpu_custom_call" | custom-call | flops 1 | bytes 1 | tf_op jit(solution)/shard_map/sent_parts/pallas_call | solution.py:570
  21.8 3.2 %pack.4 = (bf16[2,512,512]{2,1,0:T(8,128)(2,1)}, f32[8,128]{1,0:T(8,128)}) custom-call(s32[6]{0:T(128)} %stack.70.refs_0_.refs_1_.refs_8_, bf16[512,3072]{1,0:T(8,128)(2,1)} %bitcast.29, bf16[512,3072]{1,0:T(8,128)(2,1)} %copy-done, f32[8,128]{1,0:T(8,128)} %get-tuple-element.58.refs_3_), custom_call_target="tpu_custom_call" | custom-call | flops 1 | bytes 1 | tf_op jit(solution)/shard_map/pack/pallas_call | solution.py:185
  25.1 2.0 collective-permute-start.5
  30.7 3.3 %pack.5 = (bf16[2,512,512]{2,1,0:T(8,128)(2,1)}, f32[8,128]{1,0:T(8,128)}) custom-call(s32[6]{0:T(128)} %stack.70.refs_0_.refs_1_.refs_8_, bf16[512,3072]{1,0:T(8,128)(2,1)} %bitcast.30, bf16[512,3072]{1,0:T(8,128)(2,1)} %copy-done, f32[8,128]{1,0:T(8,128)} %get-tuple-element.59.refs_3_), custom_call_target="tpu_custom_call" | custom-call | flops 1 | bytes 1 | tf_op jit(solution)/shard_map/pack/pallas_call | solution.py:185
  34.0 3.0 %pack.6 = (bf16[2,512,256]{2,1,0:T(8,128)(2,1)}, f32[8,128]{1,0:T(8,128)}) custom-call(s32[6]{0:T(128)} %stack.70.refs_0_.refs_1_.refs_8_, bf16[512,3072]{1,0:T(8,128)(2,1)} %bitcast.31, bf16[512,3072]{1,0:T(8,128)(2,1)} %copy-done, f32[8,128]{1,0:T(8,128)} %get-tuple-element.60.refs_3_), custom_call_target="tpu_custom_call" | custom-call | flops 1 | bytes 1 | tf_op jit(solution)/shard_map/pack/pallas_call | solution.py:185
  37.0 3.0 %pack.7 = (bf16[2,512,256]{2,1,0:T(8,128)(2,1)}, f32[8,128]{1,0:T(8,128)}) custom-call(s32[6]{0:T(128)} %stack.70.refs_0_.refs_1_.refs_8_, bf16[512,3072]{1,0:T(8,128)(2,1)} %bitcast.32, bf16[512,3072]{1,0:T(8,128)(2,1)} %copy-done, f32[8,128]{1,0:T(8,128)} %get-tuple-element.61.refs_3_), custom_call_target="tpu_custom_call" | custom-call | flops 1 | bytes 1 | tf_op jit(solution)/shard_map/pack/pallas_call | solution.py:185
  40.0 20.5 %collective-permute-done.3.refs_0_ = bf16[384,3072]{1,0:T(8,128)(2,1)} collective-permute-done((bf16[384,3072]{1,0:T(8,128)(2,1)}, bf16[384,3072]{1,0:T(8,128)(2,1)}, u32[]{:S(2)}, u32[]{:S(2)}) %collective-permute-start.3) | collective-permute-done | bytes 2359328 | tf_op jit(solution)/shard_map/ppermute | solution.py:716
  61.2 21.1 %collective-permute-done.5.refs_2_.refs_9_ = bf16[2,512,512]{2,1,0:T(8,128)(2,1)S(1)} collective-permute-done((bf16[2,512,512]{2,1,0:T(8,128)(2,1)}, bf16[2,512,512]{2,1,0:T(8,128)(2,1)S(1)}, u32[]{:S(2)}, u32[]{:S(2)}) %collective-permute-start.5) | collective-permute-done | bytes 1048608 | tf_op jit(solution)/shard_map/ppermute | solution.py:716
  84.9 2.4 %collective-permute-done.10.came.refs_3_ = bf16[2,256,3072]{2,1,0:T(8,128)(2,1)} collective-permute-done((bf16[2,256,3072]{2,1,0:T(8,128)(2,1)}, bf16[2,256,3072]{2,1,0:T(8,128)(2,1)}, u32[]{:S(2)}, u32[]{:S(2)}) %collective-permute-start.10) | collective-permute-done | bytes 3145760 | tf_op jit(solution)/shard_map/ppermute | solution.py:739
  87.3 3.2 %collective-permute-start.7 = (bf16[2,512,512]{2,1,0:T(8,128)(2,1)}, bf16[2,512,512]{2,1,0:T(8,128)(2,1)}, u32[]{:S(2)}, u32[]{:S(2)}) collective-permute-start(bf16[2,512,512]{2,1,0:T(8,128)(2,1)} %get-tuple-element.68), channel_id=1, source_target_pairs={{0,2},{1,3},{6,4},{7,5},{8,10},{9,11},{14,12},{15,13},{16,18},{17,... | collective-permute-start | bytes 3145736 | tf_op jit(solution)/shard_map/ppermute | solution.py:716
  90.6 3.7 %relay.2 = (bf16[2,256,3072]{2,1,0:T(8,128)(2,1)}, f32[8,128]{1,0:T(8,128)}) custom-call(s32[1]{0:T(128)S(6)} %convert_element_type.22.onward, bf16[2,256,3072]{2,1,0:T(8,128)(2,1)} %collective-permute-done.11.came.refs_4_, bf16[2,256,3072]{2,1,0:T(8,128)(2,1)} %get-tuple-element.72.piece, ...), custom_call_target="tpu_custom_call", output_to_operand_aliasing={{0}: (2, {})} | custom-call | flops 1 | bytes 1 | tf_op jit(solution)/shard_map/relay/pallas_call | solution.py:600
  94.3 3.7 %relay.3 = (bf16[2,256,3072]{2,1,0:T(8,128)(2,1)}, f32[8,128]{1,0:T(8,128)}) custom-call(s32[1]{0:T(128)S(6)} %convert_element_type.22.onward, bf16[2,256,3072]{2,1,0:T(8,128)(2,1)} %collective-permute-done.10.came.refs_3_, bf16[2,256,3072]{2,1,0:T(8,128)(2,1)} %get-tuple-element.71.piece, ...), custom_call_target="tpu_custom_call", output_to_operand_aliasing={{0}: (2, {})} | custom-call | flops 1 | bytes 1 | tf_op jit(solution)/shard_map/relay/pallas_call | solution.py:600
  98.0 14.6 %collective-permute-done.7.refs_2_.refs_9_ = bf16[2,512,512]{2,1,0:T(8,128)(2,1)} collective-permute-done((bf16[2,512,512]{2,1,0:T(8,128)(2,1)}, bf16[2,512,512]{2,1,0:T(8,128)(2,1)}, u32[]{:S(2)}, u32[]{:S(2)}) %collective-permute-start.7) | collective-permute-done | bytes 1048608 | tf_op jit(solution)/shard_map/ppermute | solution.py:716
  116.2 5.7 %collective-permute-start.13 = (bf16[2,512,256]{2,1,0:T(8,128)(2,1)}, bf16[2,512,256]{2,1,0:T(8,128)(2,1)}, u32[]{:S(2)}, u32[]{:S(2)}) collective-permute-start(bf16[2,512,256]{2,1,0:T(8,128)(2,1)} %get-tuple-element.76), channel_id=1, source_target_pairs={{0,2},{1,3},{6,4},{7,5},{8,10},{9,11},{14,12},{15,13},{16,18},{17,... | collective-permute-start | bytes 1572872 | tf_op jit(solution)/shard_map/ppermute | solution.py:716
  122.6 2.8 %project.6 = (bf16[768,512]{1,0:T(8,128)(2,1)}, f32[8,128]{1,0:T(8,128)}) custom-call(s32[10]{0:T(128)} %concatenate.46.refs_0_.table.refs_7_, s32[6]{0:T(128)} %stack.70.refs_0_.refs_1_.refs_8_, bf16[384,3072]{1,0:T(8,128)(2,1)} %get-tuple-element.69.refs_2_, bf16[384,3072]{1,0:T(8,128)(2,1)} %collective-permute-done.9.refs_3_, bf16[512,3072]{1,0:T(8,128)(2,1)} %bitcast.33, ...), custom_call_target="tpu_custom_call" | custom-call | flops 1 | bytes 1 | tf_op jit(solution)/shard_map/project/pallas_call | solution.py:317
  125.5 2.0 collective-permute-start.14
  127.4 4.7 %project.7 = (f32[768,512]{1,0:T(8,128)}, f32[8,128]{1,0:T(8,128)}) custom-call(s32[10]{0:T(128)} %concatenate.46.refs_0_.table.refs_7_, s32[6]{0:T(128)} %stack.70.refs_0_.refs_1_.refs_8_, bf16[384,4096]{1,0:T(8,128)(2,1)} %bitcast.43, bf16[384,4096]{1,0:T(8,128)(2,1)} %collective-permute-done.refs_3_.refs_10_, bf16[512,3072]{1,0:T(8,128)(2,1)} %bitcast.34, ...), custom_call_target="tpu_custom_call" | custom-call | flops 1 | bytes 1 | tf_op jit(solution)/shard_map/project/pallas_call | solution.py:317
  132.1 1.6 collective-permute-done.13.refs_0_
  134.4 1.8 project.8
  136.2 13.3 %collective-permute-start.16 = (bf16[768,512]{1,0:T(8,128)(2,1)}, bf16[768,512]{1,0:T(8,128)(2,1)S(1)}, u32[]{:S(2)}, u32[]{:S(2)}) collective-permute-start(bf16[768,512]{1,0:T(8,128)(2,1)} %get-tuple-element.92), channel_id=1, source_target_pairs={{0,2},{1,3},{6,4},{7,5},{2,0},{3,1},{4,6},{5,7},{8,10},{9,11},{14,... | collective-permute-start | bytes 2359304 | tf_op jit(solution)/shard_map/ppermute | solution.py:716
  149.4 4.8 %project.9 = (f32[768,512]{1,0:T(8,128)}, f32[8,128]{1,0:T(8,128)}) custom-call(s32[10]{0:T(128)} %concatenate.46.refs_0_.table.refs_7_, s32[6]{0:T(128)} %stack.70.refs_0_.refs_1_.refs_8_, bf16[384,4096]{1,0:T(8,128)(2,1)} %bitcast.44, bf16[384,4096]{1,0:T(8,128)(2,1)} %collective-permute-done.refs_3_.refs_10_, bf16[512,3072]{1,0:T(8,128)(2,1)} %bitcast.36, ...), custom_call_target="tpu_custom_call" | custom-call | flops 1 | bytes 1 | tf_op jit(solution)/shard_map/project/pallas_call | solution.py:317
  155.4 2.4 %unpack.1 = (bf16[2,512,256]{2,1,0:T(8,128)(2,1)}, f32[8,128]{1,0:T(8,128)}) custom-call(bf16[768,512]{1,0:T(8,128)(2,1)} %copy-done.5, f32[8,128]{1,0:T(8,128)} %get-tuple-element.87.refs_0_, bf16[2,512,256]{2,1,0:T(8,128)(2,1)} %copy-done.3), custom_call_target="tpu_custom_call" | custom-call | flops 1 | bytes 1 | tf_op jit(solution)/shard_map/unpack/pallas_call | solution.py:355
  157.8 1.6 project.10
  159.4 8.5 %collective-permute-start.18 = (bf16[768,256]{1,0:T(8,128)(2,1)}, bf16[768,256]{1,0:T(8,128)(2,1)S(1)}, u32[]{:S(2)}, u32[]{:S(2)}) collective-permute-start(bf16[768,256]{1,0:T(8,128)(2,1)} %get-tuple-element.98), channel_id=1, source_target_pairs={{0,2},{1,3},{6,4},{7,5},{2,0},{3,1},{4,6},{5,7},{8,10},{9,11},{14,... | collective-permute-start | bytes 1179656 | tf_op jit(solution)/shard_map/ppermute | solution.py:716
  167.9 3.1 %keep_keys.1 = (bf16[2,2,384,128]{3,2,1,0:T(8,128)(2,1)}, bf16[2,2,384,128]{3,2,1,0:T(8,128)(2,1)}, f32[8,128]{1,0:T(8,128)}) custom-call(s32[10]{0:T(128)} %concatenate.46.refs_0_.table.refs_7_, f32[768,512]{1,0:T(8,128)} %get-tuple-element.84.own, bf16[768,512]{1,0:T(8,128)(2,1)} %copy-done.5, f32[2,384,128]{2,1,0:T(8,128)} %get-tuple-element.114.refs_2_.cosine.refs_1_, ...), custom_call_target="tpu_custom_call" | custom-call | flops 1 | bytes 1 | tf_op jit(solution)/shard_map/keep_keys/pallas_call | solution.py:403
  172.1 1.6 project.11
  173.7 5.0 %collective-permute-start.19 = (bf16[768,256]{1,0:T(8,128)(2,1)}, bf16[768,256]{1,0:T(8,128)(2,1)S(1)}, u32[]{:S(2)}, u32[]{:S(2)}) collective-permute-start(bf16[768,256]{1,0:T(8,128)(2,1)} %get-tuple-element.99), channel_id=1, source_target_pairs={{0,2},{1,3},{6,4},{7,5},{2,0},{3,1},{4,6},{5,7},{8,10},{9,11},{14,... | collective-permute-start | bytes 1179656 | tf_op jit(solution)/shard_map/ppermute | solution.py:716
  178.6 8.5 %attend_and_project.1 = (bf16[384,512]{1,0:T(8,128)(2,1)}, bf16[384,512]{1,0:T(8,128)(2,1)}, f32[768,512]{1,0:T(8,128)}, f32[8,128]{1,0:T(8,128)}) custom-call(f32[768,512]{1,0:T(8,128)} %get-tuple-element.83.refs_0_, f32[2,384,128]{2,1,0:T(8,128)} %get-tuple-element.114.refs_2_.cosine.refs_1_, f32[2,384,128]{2,1,0:T(8,128)} %get-tuple-element.115.refs_3_.sine.refs_2_, ...), custom_call_target="tpu_custom_call" | custom-call | flops 1 | bytes 1 | tf_op jit(solution)/shard_map/attend_and_project/pallas_call | solution.py:501
  188.2 5.6 %attend_chunks.1 = (bf16[384,512]{1,0:T(8,128)(2,1)}, bf16[384,512]{1,0:T(8,128)(2,1)}, f32[8,128]{1,0:T(8,128)}) custom-call(f32[768,512]{1,0:T(8,128)} %get-tuple-element.97.refs_0_, f32[2,384,128]{2,1,0:T(8,128)} %get-tuple-element.114.refs_2_.cosine.refs_1_, f32[2,384,128]{2,1,0:T(8,128)} %get-tuple-element.115.refs_3_.sine.refs_2_, ...), custom_call_target="tpu_custom_call" | custom-call | flops 1 | bytes 1 | tf_op jit(solution)/shard_map/attend_chunks/pallas_call | solution.py:460
  194.9 13.4 %outer_update.1 = (f32[512,3072]{1,0:T(8,128)}, f32[512,3072]{1,0:T(8,128)}, f32[8,128]{1,0:T(8,128)}) custom-call(s32[2]{0:T(128)} %pad_add_fusion.1.choice, f32[512,3072]{1,0:T(8,128)} %bitcast.47, bf16[512,3072]{1,0:T(8,128)(2,1)} %bitcast.40, f32[512,3072]{1,0:T(8,128)} %bitcast.49, bf16[2,256,3072]{2,1,0:T(8,128)(2,1)} %collective-permute-done.10.came.refs_3_, ...), custom_call_target="tpu_custom_call" | custom-call | flops 1 | bytes 1 | tf_op jit(solution)/shard_map/outer_update/pallas_call | solution.py:687
  (78 shorter events, 22.8 us)
Async XLA Ops:
  0.6 8.0 %copy-start.12 = (s32[4]{0:T(128)S(1)}, s32[4]{0:T(128)}, u32[]{:S(2)}) copy-start(s32[4]{0:T(128)} %param.8) | copy-start | bytes 52
  0.6 19.5 %collective-permute-start.1 = (bf16[512,3072]{1,0:T(8,128)(2,1)}, bf16[512,3072]{1,0:T(8,128)(2,1)S(1)}, u32[]{:S(2)}, u32[]{:S(2)}) collective-permute-start(bf16[512,3072]{1,0:T(8,128)(2,1)} %bitcast.26), channel_id=1, source_target_pairs={{0,1},{1,0},{2,3},{3,2},{4,5},{5,4},{6,7},{7,6},{8,9},{9,8},{10,11... | collective-permute-start | bytes 9437192 | tf_op jit(solution)/shard_map/ppermute | solution.py:716
  1.2 60.0 %collective-permute-start.2 = (bf16[512,3072]{1,0:T(8,128)(2,1)}, bf16[512,3072]{1,0:T(8,128)(2,1)}, u32[]{:S(2)}, u32[]{:S(2)}) collective-permute-start(bf16[512,3072]{1,0:T(8,128)(2,1)} %bitcast.27), channel_id=1, source_target_pairs={{2,4},{3,5},{4,2},{5,3},{0,1},{1,0},{6,7},{7,6},{10,12},{11,13},{1... | collective-permute-start | bytes 9437192 | tf_op jit(solution)/shard_map/ppermute | solution.py:716
  4.5 56.1 %collective-permute-start.3 = (bf16[384,3072]{1,0:T(8,128)(2,1)}, bf16[384,3072]{1,0:T(8,128)(2,1)}, u32[]{:S(2)}, u32[]{:S(2)}) collective-permute-start(bf16[384,3072]{1,0:T(8,128)(2,1)} %get-tuple-element.56), channel_id=1, source_target_pairs={{0,2},{1,3},{6,4},{7,5},{2,0},{3,1},{4,6},{5,7},{8,10},{9,11},{14,... | collective-permute-start | bytes 7077896 | tf_op jit(solution)/shard_map/ppermute | solution.py:716
  8.7 11.4 %copy-start.11 = (s32[1,384]{1,0:T(1,128)S(1)}, s32[1,384]{1,0:T(1,128)}, u32[]{:S(2)}) copy-start(s32[1,384]{1,0:T(1,128)} %param.7) | copy-start | bytes 4612
  17.1 70.3 %collective-permute-start.10 = (bf16[2,256,3072]{2,1,0:T(8,128)(2,1)}, bf16[2,256,3072]{2,1,0:T(8,128)(2,1)}, u32[]{:S(2)}, u32[]{:S(2)}) collective-permute-start(bf16[2,256,3072]{2,1,0:T(8,128)(2,1)} %get-tuple-element.71.piece), channel_id=1, source_target_pairs={{0,8},{8,0},{16,24},{24,16},{1,9},{9,1},{17,25},{25,17},{2,10},{10... | collective-permute-start | bytes 9437192 | tf_op jit(solution)/shard_map/ppermute | solution.py:739
  18.6 71.9 %collective-permute-start.11 = (bf16[2,256,3072]{2,1,0:T(8,128)(2,1)}, bf16[2,256,3072]{2,1,0:T(8,128)(2,1)}, u32[]{:S(2)}, u32[]{:S(2)}) collective-permute-start(bf16[2,256,3072]{2,1,0:T(8,128)(2,1)} %get-tuple-element.72.piece), channel_id=1, source_target_pairs={{0,16},{8,24},{16,0},{24,8},{1,17},{9,25},{17,1},{25,9},{2,18},{10... | collective-permute-start | bytes 9437192 | tf_op jit(solution)/shard_map/ppermute | solution.py:739
  20.2 1.7 copy-start
  20.2 4.9 %collective-permute-start.4 = (s32[384]{0:T(512)S(1)}, s32[384]{0:T(512)S(1)}, u32[]{:S(2)}, u32[]{:S(2)}) collective-permute-start(s32[384]{0:T(512)S(1)} %reduce), channel_id=1, source_target_pairs={{0,1},{1,0},{2,3},{3,2},{4,5},{5,4},{6,7},{7,6},{8,9},{9,8},{10,11... | collective-permute-start | bytes 4616 | tf_op jit(solution)/shard_map/ppermute | solution.py:716
  25.1 57.2 %collective-permute-start.5 = (bf16[2,512,512]{2,1,0:T(8,128)(2,1)}, bf16[2,512,512]{2,1,0:T(8,128)(2,1)S(1)}, u32[]{:S(2)}, u32[]{:S(2)}) collective-permute-start(bf16[2,512,512]{2,1,0:T(8,128)(2,1)} %get-tuple-element.64), channel_id=1, source_target_pairs={{0,2},{1,3},{6,4},{7,5},{8,10},{9,11},{14,12},{15,13},{16,18},{17,... | collective-permute-start | bytes 3145736 | tf_op jit(solution)/shard_map/ppermute | solution.py:716
  83.8 32.4 %collective-permute-start.6 = (bf16[512,3072]{1,0:T(8,128)(2,1)}, bf16[512,3072]{1,0:T(8,128)(2,1)S(1)}, u32[]{:S(2)}, u32[]{:S(2)}) collective-permute-start(bf16[512,3072]{1,0:T(8,128)(2,1)} %get-tuple-element.65.refs_6_.refs_13_), channel_id=1, source_target_pairs={{0,1},{1,0},{2,3},{3,2},{4,5},{5,4},{6,7},{7,6},{8,9},{9,8},{10,11... | collective-permute-start | bytes 9437192 | tf_op jit(solution)/shard_map/ppermute | solution.py:716
  83.8 31.8 %collective-permute-start.9 = (bf16[384,3072]{1,0:T(8,128)(2,1)}, bf16[384,3072]{1,0:T(8,128)(2,1)}, u32[]{:S(2)}, u32[]{:S(2)}) collective-permute-start(bf16[384,3072]{1,0:T(8,128)(2,1)} %get-tuple-element.69.refs_2_), channel_id=1, source_target_pairs={{0,1},{1,0},{2,3},{3,2},{4,5},{5,4},{6,7},{7,6},{8,9},{9,8},{10,11... | collective-permute-start | bytes 7077896 | tf_op jit(solution)/shard_map/ppermute | solution.py:716
  84.4 41.1 %collective-permute-start = (bf16[384,4096]{1,0:T(8,128)(2,1)}, bf16[384,4096]{1,0:T(8,128)(2,1)}, u32[]{:S(2)}, u32[]{:S(2)}) collective-permute-start(bf16[384,4096]{1,0:T(8,128)(2,1)} %bitcast.42), channel_id=1, source_target_pairs={{0,1},{1,0},{2,3},{3,2},{4,5},{5,4},{6,7},{7,6},{8,9},{9,8},{10,11... | collective-permute-start | bytes 9437192 | tf_op jit(solution)/shard_map/ppermute | solution.py:716
  87.3 25.3 %collective-permute-start.7 = (bf16[2,512,512]{2,1,0:T(8,128)(2,1)}, bf16[2,512,512]{2,1,0:T(8,128)(2,1)}, u32[]{:S(2)}, u32[]{:S(2)}) collective-permute-start(bf16[2,512,512]{2,1,0:T(8,128)(2,1)} %get-tuple-element.68), channel_id=1, source_target_pairs={{0,2},{1,3},{6,4},{7,5},{8,10},{9,11},{14,12},{15,13},{16,18},{17,... | collective-permute-start | bytes 3145736 | tf_op jit(solution)/shard_map/ppermute | solution.py:716
  90.5 23.6 %collective-permute-start.12 = (bf16[2,512,512]{2,1,0:T(8,128)(2,1)}, bf16[2,512,512]{2,1,0:T(8,128)(2,1)}, u32[]{:S(2)}, u32[]{:S(2)}) collective-permute-start(bf16[2,512,512]{2,1,0:T(8,128)(2,1)} %copy-done.2), channel_id=1, source_target_pairs={{2,4},{3,5},{4,2},{5,3},{0,1},{1,0},{6,7},{7,6},{10,12},{11,13},{1... | collective-permute-start | bytes 3145736 | tf_op jit(solution)/shard_map/ppermute | solution.py:716
  112.6 82.3 %collective-permute-start.22 = (bf16[2,256,3072]{2,1,0:T(8,128)(2,1)}, bf16[2,256,3072]{2,1,0:T(8,128)(2,1)}, u32[]{:S(2)}, u32[]{:S(2)}) collective-permute-start(bf16[2,256,3072]{2,1,0:T(8,128)(2,1)} %get-tuple-element.104), channel_id=1, source_target_pairs={{0,8},{8,0},{16,24},{24,16},{1,9},{9,1},{17,25},{25,17},{2,10},{10... | collective-permute-start | bytes 9437192 | tf_op jit(solution)/shard_map/ppermute | solution.py:813
  114.1 80.8 %collective-permute-start.23 = (bf16[2,256,3072]{2,1,0:T(8,128)(2,1)}, bf16[2,256,3072]{2,1,0:T(8,128)(2,1)}, u32[]{:S(2)}, u32[]{:S(2)}) collective-permute-start(bf16[2,256,3072]{2,1,0:T(8,128)(2,1)} %get-tuple-element.105), channel_id=1, source_target_pairs={{0,16},{8,24},{16,0},{24,8},{1,17},{9,25},{17,1},{25,9},{2,18},{10... | collective-permute-start | bytes 9437192 | tf_op jit(solution)/shard_map/ppermute | solution.py:813
  115.6 18.1 %collective-permute-start.8 = (bf16[2,512,512]{2,1,0:T(8,128)(2,1)}, bf16[2,512,512]{2,1,0:T(8,128)(2,1)}, u32[]{:S(2)}, u32[]{:S(2)}) collective-permute-start(bf16[2,512,512]{2,1,0:T(8,128)(2,1)} %collective-permute-done.7.refs_2_.refs_9_), channel_id=1, source_target_pairs={{2,4},{3,5},{4,2},{5,3},{0,1},{1,0},{6,7},{7,6},{10,12},{11,13},{1... | collective-permute-start | bytes 3145736 | tf_op jit(solution)/shard_map/ppermute | solution.py:716
  116.2 6.4 %copy-start.1 = (bf16[512,3072]{1,0:T(8,128)(2,1)}, bf16[512,3072]{1,0:T(8,128)(2,1)S(1)}, u32[]{:S(2)}) copy-start(bf16[512,3072]{1,0:T(8,128)(2,1)S(1)} %collective-permute-done.6.refs_7_.refs_14_) | copy-start | bytes 9437188
  116.2 17.5 %collective-permute-start.13 = (bf16[2,512,256]{2,1,0:T(8,128)(2,1)}, bf16[2,512,256]{2,1,0:T(8,128)(2,1)}, u32[]{:S(2)}, u32[]{:S(2)}) collective-permute-start(bf16[2,512,256]{2,1,0:T(8,128)(2,1)} %get-tuple-element.76), channel_id=1, source_target_pairs={{0,2},{1,3},{6,4},{7,5},{8,10},{9,11},{14,12},{15,13},{16,18},{17,... | collective-permute-start | bytes 1572872 | tf_op jit(solution)/shard_map/ppermute | solution.py:716
  125.5 28.8 %collective-permute-start.14 = (bf16[768,512]{1,0:T(8,128)(2,1)}, bf16[768,512]{1,0:T(8,128)(2,1)S(1)}, u32[]{:S(2)}, u32[]{:S(2)}) collective-permute-start(bf16[768,512]{1,0:T(8,128)(2,1)} %get-tuple-element.85), channel_id=1, source_target_pairs={{0,2},{1,3},{6,4},{7,5},{2,0},{3,1},{4,6},{5,7},{8,10},{9,11},{14,... | collective-permute-start | bytes 2359304 | tf_op jit(solution)/shard_map/ppermute | solution.py:716
  134.3 19.9 %collective-permute-start.15 = (bf16[2,512,256]{2,1,0:T(8,128)(2,1)}, bf16[2,512,256]{2,1,0:T(8,128)(2,1)S(1)}, u32[]{:S(2)}, u32[]{:S(2)}) collective-permute-start(bf16[2,512,256]{2,1,0:T(8,128)(2,1)} %get-tuple-element.86.refs_17_), channel_id=1, source_target_pairs={{2,4},{3,5},{4,2},{5,3},{0,1},{1,0},{6,7},{7,6},{10,12},{11,13},{1... | collective-permute-start | bytes 1572872 | tf_op jit(solution)/shard_map/ppermute | solution.py:716
  136.2 34.8 %collective-permute-start.16 = (bf16[768,512]{1,0:T(8,128)(2,1)}, bf16[768,512]{1,0:T(8,128)(2,1)S(1)}, u32[]{:S(2)}, u32[]{:S(2)}) collective-permute-start(bf16[768,512]{1,0:T(8,128)(2,1)} %get-tuple-element.92), channel_id=1, source_target_pairs={{0,2},{1,3},{6,4},{7,5},{2,0},{3,1},{4,6},{5,7},{8,10},{9,11},{14,... | collective-permute-start | bytes 2359304 | tf_op jit(solution)/shard_map/ppermute | solution.py:716
  154.3 1.1 copy-start.5
  157.7 13.2 %collective-permute-start.17 = (bf16[2,512,256]{2,1,0:T(8,128)(2,1)}, bf16[2,512,256]{2,1,0:T(8,128)(2,1)S(1)}, u32[]{:S(2)}, u32[]{:S(2)}) collective-permute-start(bf16[2,512,256]{2,1,0:T(8,128)(2,1)} %get-tuple-element.93.refs_18_), channel_id=1, source_target_pairs={{2,4},{3,5},{4,2},{5,3},{0,1},{1,0},{6,7},{7,6},{10,12},{11,13},{1... | collective-permute-start | bytes 1572872 | tf_op jit(solution)/shard_map/ppermute | solution.py:716
  159.4 27.9 %collective-permute-start.18 = (bf16[768,256]{1,0:T(8,128)(2,1)}, bf16[768,256]{1,0:T(8,128)(2,1)S(1)}, u32[]{:S(2)}, u32[]{:S(2)}) collective-permute-start(bf16[768,256]{1,0:T(8,128)(2,1)} %get-tuple-element.98), channel_id=1, source_target_pairs={{0,2},{1,3},{6,4},{7,5},{2,0},{3,1},{4,6},{5,7},{8,10},{9,11},{14,... | collective-permute-start | bytes 1179656 | tf_op jit(solution)/shard_map/ppermute | solution.py:716
  171.0 1.1 copy-start.6
  173.7 13.6 %collective-permute-start.19 = (bf16[768,256]{1,0:T(8,128)(2,1)}, bf16[768,256]{1,0:T(8,128)(2,1)S(1)}, u32[]{:S(2)}, u32[]{:S(2)}) collective-permute-start(bf16[768,256]{1,0:T(8,128)(2,1)} %get-tuple-element.99), channel_id=1, source_target_pairs={{0,2},{1,3},{6,4},{7,5},{2,0},{3,1},{4,6},{5,7},{8,10},{9,11},{14,... | collective-permute-start | bytes 1179656 | tf_op jit(solution)/shard_map/ppermute | solution.py:716
  187.2 21.2 %collective-permute-start.20 = (bf16[384,512]{1,0:T(8,128)(2,1)}, bf16[384,512]{1,0:T(8,128)(2,1)S(1)}, u32[]{:S(2)}, u32[]{:S(2)}) collective-permute-start(bf16[384,512]{1,0:T(8,128)(2,1)} %get-tuple-element.102), channel_id=1, source_target_pairs={{0,1},{1,0},{2,3},{3,2},{4,5},{5,4},{6,7},{7,6},{8,9},{9,8},{10,11... | collective-permute-start | bytes 1179656 | tf_op jit(solution)/shard_map/ppermute | solution.py:716
  193.7 14.7 %collective-permute-start.21 = (bf16[384,512]{1,0:T(8,128)(2,1)}, bf16[384,512]{1,0:T(8,128)(2,1)S(1)}, u32[]{:S(2)}, u32[]{:S(2)}) collective-permute-start(bf16[384,512]{1,0:T(8,128)(2,1)} %get-tuple-element.103), channel_id=1, source_target_pairs={{0,1},{1,0},{2,3},{3,2},{4,5},{5,4},{6,7},{7,6},{8,9},{9,8},{10,11... | collective-permute-start | bytes 1179656 | tf_op jit(solution)/shard_map/ppermute | solution.py:716
  194.9 13.5 %copy-start.9 = (bf16[384,512]{1,0:T(8,128)(2,1)S(1)}, bf16[384,512]{1,0:T(8,128)(2,1)}, u32[]{:S(2)}) copy-start(bf16[384,512]{1,0:T(8,128)(2,1)} %get-tuple-element.96) | copy-start | bytes 1179652
  194.9 13.5 %copy-start.10 = (bf16[384,512]{1,0:T(8,128)(2,1)S(1)}, bf16[384,512]{1,0:T(8,128)(2,1)}, u32[]{:S(2)}) copy-start(bf16[384,512]{1,0:T(8,128)(2,1)} %get-tuple-element.101) | copy-start | bytes 1179652
  (5 other events, 4.3 us)
